TPU v7x, 32 devices: a whole 2x2x4 slice. The times are simulated.
32 devices in a mesh: grp: 2 (over x), req: 16 (over z, y, core).
Axes of the slice: x: 2, y: 2, z: 4, core: 2. Of those that a mesh axis runs over, the one named last changes fastest.
Arguments:
- queries: bfloat16 [2, 2048, 1024], P('grp', 'req')
- suffix_kv: bfloat16 [2, 2, 2048, 1024], P('grp', None, 'req')
- prefix_kv: bfloat16 [2, 2, 1024, 1024], P('grp', None, 'req'), may hold values from -6 to 6
- lengths: int32 [2, 12], P('grp'), may hold values from 1 to 512, 2048 in all within a row
Outputs:
- attended: bfloat16 [2, 2048, 1024], P('grp', 'req')
Inputs may be any that keep to these rules, and one draw needn't show every extreme that they name: Each group's 12 lengths sum to 2048, the longest exactly 512.
All inputs are finite; a program needn't handle non-finite values.
Results may differ from a plain program's by a relative error of at most 0.0075.
Values may be sent and summed in bfloat16 or wider, within the bound.
No kernel may reach another device: no remote copies, remote signals or barrier semaphores. Data moves between devices by JAX's collectives and lax.ppermute only.
A program may use at most 64 MiB of HBM per device.

v0:
```python
import jax
import jax.numpy as jnp
from jax import lax
from jax.sharding import PartitionSpec as P

HEADS = 16
HEAD = 64
WIN = 1024


def from_behind(block, axis, distance):
    devices = range(lax.axis_size(axis))
    route = [(i - distance, i) for i in devices if i - distance in devices]
    return lax.ppermute(block, axis, route)


def locate(positions, starts, ends):
    inside = (positions[:, None] >= starts[None, :]) & (positions[:, None] < ends[None, :])
    numbers = jnp.arange(1, starts.shape[0] + 1, dtype=jnp.int32)
    request = jnp.sum(jnp.where(inside, numbers[None, :], 0), axis=1) - 1
    offset = positions - jnp.sum(jnp.where(inside, starts[None, :], 0), axis=1)
    return (request, offset)


def absorb(carry, query, keys, vals, mask):
    running_max, running_total, running_acc = carry
    score = jnp.einsum("qhd,khd->hqk", query, keys, preferred_element_type=jnp.float32) * 0.125
    score = jnp.where(mask[None], score, -1e30)
    new_max = jnp.maximum(running_max, jnp.max(score, axis=-1))
    factor = jnp.exp(running_max - new_max)
    weight = jnp.where(mask[None], jnp.exp(score - new_max[..., None]), 0.0)
    new_total = running_total * factor + jnp.sum(weight, axis=-1)
    rounded = weight.astype(jnp.bfloat16)
    added = jnp.einsum("hqk,khd->hqd", rounded, vals, preferred_element_type=jnp.float32)
    return (new_max, new_total, running_acc * factor[..., None] + added)


def on_device(queries, suffix_kv, prefix_kv, lengths):
    tok_rows = queries.shape[1]
    width = queries.shape[2]
    req_count = lax.axis_size("req")
    position = lax.axis_index("req")
    lens = lengths[0]
    ends = jnp.cumsum(lens)
    starts = ends - lens
    query_index = position * tok_rows + jnp.arange(tok_rows, dtype=jnp.int32)
    query_req, query_off = locate(query_index, starts, ends)
    query = queries[0].reshape(tok_rows, HEADS, HEAD)

    def near_block(carry, block, distance):
        key_index = (position - distance) * tok_rows + jnp.arange(tok_rows, dtype=jnp.int32)
        key_req, key_off = locate(key_index, starts, ends)
        mask = (key_req[None, :] == query_req[:, None]) & (key_off[None, :] <= query_off[:, None])
        mask = mask & (query_off[:, None] - key_off[None, :] < WIN) & (key_index[None, :] >= 0)
        keys = block[0, 0].reshape(tok_rows, HEADS, HEAD)
        vals = block[0, 1].reshape(tok_rows, HEADS, HEAD)
        return absorb(carry, query, keys, vals, mask)

    carry = (
        jnp.full((HEADS, tok_rows), -1e30, jnp.float32),
        jnp.zeros((HEADS, tok_rows), jnp.float32),
        jnp.zeros((HEADS, tok_rows, HEAD), jnp.float32),
    )
    carry = near_block(carry, suffix_kv, 0)
    reach = min((WIN + tok_rows - 1) // tok_rows, req_count - 1)
    current = suffix_kv
    for distance in range(1, reach + 1):
        current = from_behind(current, "req", 1)
        carry = near_block(carry, current, distance)
    piece = lax.all_gather(prefix_kv, "req", axis=2, tiled=True)
    count = piece.shape[2]
    cached = jnp.arange(count, dtype=jnp.int32)
    mask = cached[None, :] > query_off[:, None]
    keys = piece[0, 0].reshape(count, HEADS, HEAD)
    vals = piece[0, 1].reshape(count, HEADS, HEAD)
    carry = absorb(carry, query, keys, vals, mask)
    final_max, final_total, final_acc = carry
    attended = final_acc / final_total[..., None]
    attended = jnp.transpose(attended, (1, 0, 2)).reshape(tok_rows, width).astype(jnp.bfloat16)
    return attended[None]


def solution(mesh):
    in_specs = (
        P("grp", "req", None),
        P("grp", None, "req", None),
        P("grp", None, "req", None),
        P("grp", None),
    )
    out_specs = P("grp", "req", None)
    return jax.shard_map(
        on_device, mesh=mesh, in_specs=in_specs, out_specs=out_specs, check_vma=False
    )
```

profile of v0, /device:TPU:0, one launch (start us, length us, event | category | flops | bytes accessed | tf_op | source)
XLA Modules:
  0.0 171.1 jit_solution(419747205586902801)
XLA Ops:
  6.5 0.7 all-gather.2.cloned.1.call-update
  7.3 2.4 %collective-permute-start = (bf16[1,2,128,1024]{3,2,1,0:T(8,128)(2,1)}, bf16[1,2,128,1024]{3,2,1,0:T(8,128)(2,1)S(1)}, u32[]{:S(2)}, u32[]{:S(2)}) collective-permute-start(bf16[1,2,128,1024]{3,2,1,0:T(8,128)(2,1)} %param.5), channel_id=1, source_target_pairs={{0,1},{1,2},{2,3},{3,4},{4,5},{5,6},{6,7},{7,8},{8,9},{9,10},{10,1... | collective-permute-start | bytes 1572872 | tf_op jit(solution)/shard_map/ppermute | solution.py:14
  9.8 0.8 reduce-window.4
  10.6 0.7 fusion.124
  11.6 9.0 %collective-permute-start.1 = (bf16[1,2,128,1024]{3,2,1,0:T(8,128)(2,1)S(1)}, bf16[1,2,128,1024]{3,2,1,0:T(8,128)(2,1)S(1)}, u32[]{:S(2)}, u32[]{:S(2)}) collective-permute-start(bf16[1,2,128,1024]{3,2,1,0:T(8,128)(2,1)S(1)} %collective-permute-done), channel_id=1, source_target_pairs={{0,1},{1,2},{2,3},{3,4},{4,5},{5,6},{6,7},{7,8},{8,9},{9,10},{10,1... | collective-permute-start | bytes 1572872 | tf_op jit(solution)/shard_map/ppermute | solution.py:14
  20.6 1.1 fusion.94
  21.8 1.1 fusion.159
  22.9 9.2 %collective-permute-start.2 = (bf16[1,2,128,1024]{3,2,1,0:T(8,128)(2,1)S(1)}, bf16[1,2,128,1024]{3,2,1,0:T(8,128)(2,1)}, u32[]{:S(2)}, u32[]{:S(2)}) collective-permute-start(bf16[1,2,128,1024]{3,2,1,0:T(8,128)(2,1)S(1)} %collective-permute-done.1), channel_id=1, source_target_pairs={{0,1},{1,2},{2,3},{3,4},{4,5},{5,6},{6,7},{7,8},{8,9},{9,10},{10,1... | collective-permute-start | bytes 1572872 | tf_op jit(solution)/shard_map/ppermute | solution.py:14
  32.0 0.8 fusion.100
  32.9 1.1 copy.76
  34.2 0.9 copy.78
  35.2 1.0 fusion.168
  36.1 6.4 %collective-permute-start.3 = (bf16[1,2,128,1024]{3,2,1,0:T(8,128)(2,1)}, bf16[1,2,128,1024]{3,2,1,0:T(8,128)(2,1)}, u32[]{:S(2)}, u32[]{:S(2)}) collective-permute-start(bf16[1,2,128,1024]{3,2,1,0:T(8,128)(2,1)} %collective-permute-done.2), channel_id=1, source_target_pairs={{0,1},{1,2},{2,3},{3,4},{4,5},{5,6},{6,7},{7,8},{8,9},{9,10},{10,1... | collective-permute-start | bytes 1572872 | tf_op jit(solution)/shard_map/ppermute | solution.py:14
  42.7 0.9 copy.81
  43.6 1.0 fusion.167
  44.5 1.8 %fusion.157 = (bf16[1,1,128,1024]{3,2,1,0:T(8,128)(2,1)}, bf16[1,1,128,1024]{3,2,1,0:T(8,128)(2,1)S(1)}) fusion(bf16[1,2,128,1024]{3,2,1,0:T(8,128)(2,1)} %copy-done.15), kind=kLoop, calls=%fused_computation.267 | loop fusion | bytes 1048576 | tf_op jit(solution)/shard_map/slice | solution.py:56
  46.3 0.8 copy.83
  47.2 12.8 %collective-permute-start.4 = (bf16[1,2,128,1024]{3,2,1,0:T(8,128)(2,1)}, bf16[1,2,128,1024]{3,2,1,0:T(8,128)(2,1)}, u32[]{:S(2)}, u32[]{:S(2)}) collective-permute-start(bf16[1,2,128,1024]{3,2,1,0:T(8,128)(2,1)} %collective-permute-done.3), channel_id=1, source_target_pairs={{0,1},{1,2},{2,3},{3,4},{4,5},{5,6},{6,7},{7,8},{8,9},{9,10},{10,1... | collective-permute-start | bytes 1572872 | tf_op jit(solution)/shard_map/ppermute | solution.py:14
  59.9 1.9 %fusion.166 = (f32[16,128]{1,0:T(8,128)}, f32[16,128,128]{1,2,0:T(8,128)S(1)}) fusion(bf16[128,16,64]{0,2,1:T(8,128)(2,1)S(1)} %bitcast.265, bf16[128,16,64]{0,2,1:T(8,128)(2,1)} %bitcast.284, pred[128,128]{0,1:T(8,128)(4,1)} %get-tuple-element.71), kind=kOutput, calls=%fused_computation.276 | convolution fusion | flops 34338816 | bytes 1597440 | tf_op jit(solution)/shard_map/qhd,khd->hqk/dot_general | solution.py:27
  61.9 1.8 %copy.84 = bf16[1,1,128,1024]{2,3,1,0:T(8,128)(2,1)} copy(bf16[1,1,128,1024]{3,2,1,0:T(8,128)(2,1)} %get-tuple-element.58) | data formatting | bytes 524288 | tf_op jit(solution)/shard_map/slice | solution.py:56
  63.7 1.9 %fusion.156 = (bf16[1,1,128,1024]{3,2,1,0:T(8,128)(2,1)}, bf16[1,1,128,1024]{3,2,1,0:T(8,128)(2,1)}) fusion(bf16[1,2,128,1024]{3,2,1,0:T(8,128)(2,1)} %collective-permute-done.2), kind=kLoop, calls=%fused_computation.266 | loop fusion | bytes 1048576 | tf_op jit(solution)/shard_map/slice | solution.py:56
  65.5 1.8 %copy.86 = bf16[1,1,128,1024]{2,3,1,0:T(8,128)(2,1)} copy(bf16[1,1,128,1024]{3,2,1,0:T(8,128)(2,1)} %get-tuple-element.57) | data formatting | bytes 524288 | tf_op jit(solution)/shard_map/slice | solution.py:55
  67.3 1.8 %copy.87 = bf16[1,1,128,1024]{2,3,1,0:T(8,128)(2,1)} copy(bf16[1,1,128,1024]{3,2,1,0:T(8,128)(2,1)} %get-tuple-element.56) | data formatting | bytes 524288 | tf_op jit(solution)/shard_map/slice | solution.py:56
  69.1 3.0 %fusion.165 = (f32[16,128]{1,0:T(8,128)}, f32[16,128,128]{1,2,0:T(8,128)}) fusion(bf16[128,16,64]{0,2,1:T(8,128)(2,1)S(1)} %bitcast.266, bf16[128,16,64]{0,2,1:T(8,128)(2,1)} %bitcast.288, pred[128,128]{0,1:T(8,128)(4,1)} %get-tuple-element.73), kind=kOutput, calls=%fused_computation.275 | convolution fusion | flops 34338816 | bytes 1597440 | tf_op jit(solution)/shard_map/qhd,khd->hqk/dot_general | solution.py:27
  72.1 10.6 %collective-permute-start.5 = (bf16[1,2,128,1024]{3,2,1,0:T(8,128)(2,1)}, bf16[1,2,128,1024]{3,2,1,0:T(8,128)(2,1)}, u32[]{:S(2)}, u32[]{:S(2)}) collective-permute-start(bf16[1,2,128,1024]{3,2,1,0:T(8,128)(2,1)} %collective-permute-done.4), channel_id=1, source_target_pairs={{0,1},{1,2},{2,3},{3,4},{4,5},{5,6},{6,7},{7,8},{8,9},{9,10},{10,1... | collective-permute-start | bytes 1572872 | tf_op jit(solution)/shard_map/ppermute | solution.py:14
  82.6 1.9 %fusion.155 = (bf16[1,1,128,1024]{3,2,1,0:T(8,128)(2,1)}, bf16[1,1,128,1024]{3,2,1,0:T(8,128)(2,1)}) fusion(bf16[1,2,128,1024]{3,2,1,0:T(8,128)(2,1)} %collective-permute-done.3), kind=kLoop, calls=%fused_computation.265 | loop fusion | bytes 1048576 | tf_op jit(solution)/shard_map/slice | solution.py:56
  84.5 1.8 %copy.89 = bf16[1,1,128,1024]{2,3,1,0:T(8,128)(2,1)} copy(bf16[1,1,128,1024]{3,2,1,0:T(8,128)(2,1)} %get-tuple-element.55) | data formatting | bytes 524288 | tf_op jit(solution)/shard_map/slice | solution.py:55
  86.3 1.8 %copy.90 = bf16[1,1,128,1024]{2,3,1,0:T(8,128)(2,1)} copy(bf16[1,1,128,1024]{3,2,1,0:T(8,128)(2,1)} %get-tuple-element.54) | data formatting | bytes 524288 | tf_op jit(solution)/shard_map/slice | solution.py:56
  88.1 2.9 %fusion.164 = (f32[16,128]{1,0:T(8,128)}, f32[16,128,128]{1,2,0:T(8,128)}) fusion(bf16[128,16,64]{0,2,1:T(8,128)(2,1)S(1)} %bitcast.267, bf16[128,16,64]{0,2,1:T(8,128)(2,1)} %bitcast.289, pred[128,128]{0,1:T(8,128)(4,1)} %get-tuple-element.75), kind=kOutput, calls=%fused_computation.274 | convolution fusion | flops 34338816 | bytes 1597440 | tf_op jit(solution)/shard_map/qhd,khd->hqk/dot_general | solution.py:27
  91.0 1.9 %fusion.154 = (bf16[1,1,128,1024]{3,2,1,0:T(8,128)(2,1)}, bf16[1,1,128,1024]{3,2,1,0:T(8,128)(2,1)}) fusion(bf16[1,2,128,1024]{3,2,1,0:T(8,128)(2,1)} %collective-permute-done.4), kind=kLoop, calls=%fused_computation.264 | loop fusion | bytes 1048576 | tf_op jit(solution)/shard_map/slice | solution.py:56
  92.8 1.8 %copy.92 = bf16[1,1,128,1024]{2,3,1,0:T(8,128)(2,1)} copy(bf16[1,1,128,1024]{3,2,1,0:T(8,128)(2,1)} %get-tuple-element.53) | data formatting | bytes 524288 | tf_op jit(solution)/shard_map/slice | solution.py:55
  94.6 7.1 %collective-permute-start.6 = (bf16[1,2,128,1024]{3,2,1,0:T(8,128)(2,1)}, bf16[1,2,128,1024]{3,2,1,0:T(8,128)(2,1)}, u32[]{:S(2)}, u32[]{:S(2)}) collective-permute-start(bf16[1,2,128,1024]{3,2,1,0:T(8,128)(2,1)} %collective-permute-done.5), channel_id=1, source_target_pairs={{0,1},{1,2},{2,3},{3,4},{4,5},{5,6},{6,7},{7,8},{8,9},{9,10},{10,1... | collective-permute-start | bytes 1572872 | tf_op jit(solution)/shard_map/ppermute | solution.py:14
  101.8 2.9 %fusion.163 = (f32[16,128]{1,0:T(8,128)}, f32[16,128,128]{1,2,0:T(8,128)}) fusion(bf16[128,16,64]{0,2,1:T(8,128)(2,1)S(1)} %bitcast.268, bf16[128,16,64]{0,2,1:T(8,128)(2,1)} %bitcast.283, pred[128,128]{0,1:T(8,128)(4,1)} %get-tuple-element.70), kind=kOutput, calls=%fused_computation.273 | convolution fusion | flops 34338816 | bytes 1597440 | tf_op jit(solution)/shard_map/qhd,khd->hqk/dot_general | solution.py:27
  104.7 1.8 %copy.93 = bf16[1,1,128,1024]{2,3,1,0:T(8,128)(2,1)} copy(bf16[1,1,128,1024]{3,2,1,0:T(8,128)(2,1)} %get-tuple-element.52) | data formatting | bytes 524288 | tf_op jit(solution)/shard_map/slice | solution.py:56
  106.4 1.9 %fusion.153 = (bf16[1,1,128,1024]{3,2,1,0:T(8,128)(2,1)}, bf16[1,1,128,1024]{3,2,1,0:T(8,128)(2,1)}) fusion(bf16[1,2,128,1024]{3,2,1,0:T(8,128)(2,1)} %collective-permute-done.5), kind=kLoop, calls=%fused_computation.263 | loop fusion | bytes 1048576 | tf_op jit(solution)/shard_map/slice | solution.py:56
  108.3 1.8 %copy.95 = bf16[1,1,128,1024]{2,3,1,0:T(8,128)(2,1)} copy(bf16[1,1,128,1024]{3,2,1,0:T(8,128)(2,1)} %get-tuple-element.51) | data formatting | bytes 524288 | tf_op jit(solution)/shard_map/slice | solution.py:55
  110.1 2.3 %fusion.162 = (f32[16,128]{1,0:T(8,128)S(1)}, f32[16,128,128]{1,2,0:T(8,128)}) fusion(bf16[128,16,64]{0,2,1:T(8,128)(2,1)S(1)} %bitcast.269, bf16[128,16,64]{0,2,1:T(8,128)(2,1)} %bitcast.291, pred[128,128]{0,1:T(8,128)(4,1)S(1)} %get-tuple-element.74), kind=kOutput, calls=%fused_computation.272 | convolution fusion | flops 34338816 | bytes 1597440 | tf_op jit(solution)/shard_map/qhd,khd->hqk/dot_general | solution.py:27
  112.4 5.3 %collective-permute-start.7 = (bf16[1,2,128,1024]{3,2,1,0:T(8,128)(2,1)}, bf16[1,2,128,1024]{3,2,1,0:T(8,128)(2,1)}, u32[]{:S(2)}, u32[]{:S(2)}) collective-permute-start(bf16[1,2,128,1024]{3,2,1,0:T(8,128)(2,1)} %collective-permute-done.6), channel_id=1, source_target_pairs={{0,1},{1,2},{2,3},{3,4},{4,5},{5,6},{6,7},{7,8},{8,9},{9,10},{10,1... | collective-permute-start | bytes 1572872 | tf_op jit(solution)/shard_map/ppermute | solution.py:14
  117.7 1.4 bitcast_maximum_fusion.2
  119.1 1.8 %copy.96 = bf16[1,1,128,1024]{2,3,1,0:T(8,128)(2,1)} copy(bf16[1,1,128,1024]{3,2,1,0:T(8,128)(2,1)} %get-tuple-element.50) | data formatting | bytes 524288 | tf_op jit(solution)/shard_map/slice | solution.py:56
  120.9 1.8 %fusion.152 = (bf16[1,1,128,1024]{3,2,1,0:T(8,128)(2,1)}, bf16[1,1,128,1024]{3,2,1,0:T(8,128)(2,1)}) fusion(bf16[1,2,128,1024]{3,2,1,0:T(8,128)(2,1)} %collective-permute-done.6), kind=kLoop, calls=%fused_computation.262 | loop fusion | bytes 1048576 | tf_op jit(solution)/shard_map/slice | solution.py:56
  122.7 1.8 %copy.98 = bf16[1,1,128,1024]{2,3,1,0:T(8,128)(2,1)} copy(bf16[1,1,128,1024]{3,2,1,0:T(8,128)(2,1)} %get-tuple-element.49) | data formatting | bytes 524288 | tf_op jit(solution)/shard_map/slice | solution.py:55
  124.5 1.8 %copy.99 = bf16[1,1,128,1024]{2,3,1,0:T(8,128)(2,1)} copy(bf16[1,1,128,1024]{3,2,1,0:T(8,128)(2,1)} %get-tuple-element.48) | data formatting | bytes 524288 | tf_op jit(solution)/shard_map/slice | solution.py:56
  126.3 3.0 %fusion.161 = (f32[16,128]{1,0:T(8,128)}, f32[16,128,128]{1,2,0:T(8,128)}) fusion(bf16[128,16,64]{0,2,1:T(8,128)(2,1)S(1)} %bitcast.270, bf16[128,16,64]{0,2,1:T(8,128)(2,1)} %bitcast.290, pred[128,128]{0,1:T(8,128)(4,1)} %get-tuple-element.72), kind=kOutput, calls=%fused_computation.271 | convolution fusion | flops 34338816 | bytes 1597440 | tf_op jit(solution)/shard_map/qhd,khd->hqk/dot_general | solution.py:27
  129.3 1.8 %fusion.151 = (bf16[1,1,128,1024]{3,2,1,0:T(8,128)(2,1)}, bf16[1,1,128,1024]{3,2,1,0:T(8,128)(2,1)}) fusion(bf16[1,2,128,1024]{3,2,1,0:T(8,128)(2,1)} %collective-permute-done.7), kind=kLoop, calls=%fused_computation.261 | loop fusion | bytes 1048576 | tf_op jit(solution)/shard_map/slice | solution.py:56
  131.1 1.8 %copy.101 = bf16[1,1,128,1024]{2,3,1,0:T(8,128)(2,1)} copy(bf16[1,1,128,1024]{3,2,1,0:T(8,128)(2,1)} %get-tuple-element.47) | data formatting | bytes 524288 | tf_op jit(solution)/shard_map/slice | solution.py:55
  132.9 1.8 %copy.102 = bf16[1,1,128,1024]{2,3,1,0:T(8,128)(2,1)} copy(bf16[1,1,128,1024]{3,2,1,0:T(8,128)(2,1)} %get-tuple-element.46) | data formatting | bytes 524288 | tf_op jit(solution)/shard_map/slice | solution.py:56
  134.7 2.9 %fusion.160 = (f32[16,128]{1,0:T(8,128)}, f32[16,128,128]{1,2,0:T(8,128)}) fusion(bf16[128,16,64]{0,2,1:T(8,128)(2,1)S(1)} %bitcast.271, bf16[128,16,64]{0,2,1:T(8,128)(2,1)} %bitcast.286, pred[128,128]{0,1:T(8,128)(4,1)} %get-tuple-element.68), kind=kOutput, calls=%fused_computation.270 | convolution fusion | flops 34338816 | bytes 1597440 | tf_op jit(solution)/shard_map/qhd,khd->hqk/dot_general | solution.py:27
  137.6 4.6 %fusion.150 = (bf16[1,1,1024,1024]{3,2,1,0:T(8,128)(2,1)}, bf16[1,1,1024,1024]{3,2,1,0:T(8,128)(2,1)}) fusion(bf16[1,2,1024,1024]{3,2,1,0:T(8,128)(2,1)} %all-gather.2.cloned.1.call-done), kind=kLoop, calls=%fused_computation.260 | loop fusion | bytes 8388608 | tf_op jit(solution)/shard_map/slice | solution.py:74
  142.2 4.0 %copy.105 = bf16[1,1,1024,1024]{2,3,1,0:T(8,128)(2,1)} copy(bf16[1,1,1024,1024]{3,2,1,0:T(8,128)(2,1)} %get-tuple-element.45) | data formatting | bytes 4194304 | tf_op jit(solution)/shard_map/slice | solution.py:75
  146.1 4.0 %copy.104 = bf16[1,1,1024,1024]{2,3,1,0:T(8,128)(2,1)} copy(bf16[1,1,1024,1024]{3,2,1,0:T(8,128)(2,1)} %get-tuple-element.44) | data formatting | bytes 4194304 | tf_op jit(solution)/shard_map/slice | solution.py:74
  150.2 3.3 %fusion = (f32[16,128]{1,0:T(8,128)S(1)}, f32[16,128,1024]{2,1,0:T(8,128)S(1)}) fusion(pred[128,1024]{1,0:T(8,128)(4,1)S(1)} %iota_compare_fusion, bf16[128,16,64]{0,2,1:T(8,128)(2,1)S(1)} %bitcast.272, bf16[1024,16,64]{0,2,1:T(8,128)(2,1)} %bitcast.273), kind=kOutput, calls=%fused_computation.2 | convolution fusion | flops 274724864 | bytes 10887168 | tf_op jit(solution)/shard_map/qhd,khd->hqk/dot_general | solution.py:27
  153.6 2.5 %fusion.1 = f32[16,128]{1,0:T(8,128)S(1)} fusion(f32[16,128,1024]{2,1,0:T(8,128)S(1)} %get-tuple-element.77, f32[16,128]{1,0:T(8,128)S(1)} %get-tuple-element.35, pred[128,1024]{1,0:T(8,128)(4,1)S(1)} %iota_compare_fusion), kind=kLoop, calls=%fused_computation.3 | loop fusion | flops 10483712 | bytes 8536064 | tf_op jit(solution)/shard_map/reduce_sum | solution.py:32
  156.3 2.2 %fusion.15 = f32[128,16,64]{0,2,1:T(8,128)S(1)} fusion(bf16[1024,16,64]{0,2,1:T(8,128)(2,1)S(1)} %bitcast.274, f32[16,128,1024]{2,1,0:T(8,128)S(1)} %get-tuple-element.77, f32[16,128]{1,0:T(8,128)S(1)} %get-tuple-element.35, pred[128,1024]{1,0:T(8,128)(4,1)S(1)} %iota_compare_fusion), kind=kOutput, calls=%fused_computation.25 | convolution fusion | flops 278921216 | bytes 11149312 | tf_op jit(solution)/shard_map/hqk,khd->hqd/dot_general | solution.py:34
  160.6 0.3 fusion.19
  161.0 0.3 fusion.21
  161.3 0.3 fusion.23
  161.6 0.3 fusion.25
  161.9 0.3 fusion.27
  162.2 0.3 fusion.29
  162.5 0.3 fusion.31
  162.8 0.3 fusion.33
  163.1 0.3 fusion.38
  163.4 0.9 copy.106
  (134 shorter events, 2.8 us)
Async XLA Ops:
  6.5 131.0 %all-gather.2.cloned.1.call-start = ((), (), s32[]{:S(2)}) async-start(), calls=%async_computation | async-start | bytes 4456448 | tf_op jit(solution)/shard_map/all_gather | solution.py:70
  7.3 4.3 %collective-permute-start = (bf16[1,2,128,1024]{3,2,1,0:T(8,128)(2,1)}, bf16[1,2,128,1024]{3,2,1,0:T(8,128)(2,1)S(1)}, u32[]{:S(2)}, u32[]{:S(2)}) collective-permute-start(bf16[1,2,128,1024]{3,2,1,0:T(8,128)(2,1)} %param.5), channel_id=1, source_target_pairs={{0,1},{1,2},{2,3},{3,4},{4,5},{5,6},{6,7},{7,8},{8,9},{9,10},{10,1... | collective-permute-start | bytes 1572872 | tf_op jit(solution)/shard_map/ppermute | solution.py:14
  11.6 11.3 %collective-permute-start.1 = (bf16[1,2,128,1024]{3,2,1,0:T(8,128)(2,1)S(1)}, bf16[1,2,128,1024]{3,2,1,0:T(8,128)(2,1)S(1)}, u32[]{:S(2)}, u32[]{:S(2)}) collective-permute-start(bf16[1,2,128,1024]{3,2,1,0:T(8,128)(2,1)S(1)} %collective-permute-done), channel_id=1, source_target_pairs={{0,1},{1,2},{2,3},{3,4},{4,5},{5,6},{6,7},{7,8},{8,9},{9,10},{10,1... | collective-permute-start | bytes 1572872 | tf_op jit(solution)/shard_map/ppermute | solution.py:14
  21.8 38.2 %copy-start.21 = (pred[128,128]{0,1:T(8,128)(4,1)}, pred[128,128]{0,1:T(8,128)(4,1)S(1)}, u32[]{:S(2)}) copy-start(pred[128,128]{0,1:T(8,128)(4,1)S(1)} %get-tuple-element.69) | copy-start | bytes 49156
  21.8 38.2 %copy-start.23 = (pred[128,128]{0,1:T(8,128)(4,1)}, pred[128,128]{0,1:T(8,128)(4,1)S(1)}, u32[]{:S(2)}) copy-start(pred[128,128]{0,1:T(8,128)(4,1)S(1)} %get-tuple-element.67) | copy-start | bytes 49156
  22.9 19.7 %copy-start.15 = (bf16[1,2,128,1024]{3,2,1,0:T(8,128)(2,1)}, bf16[1,2,128,1024]{3,2,1,0:T(8,128)(2,1)S(1)}, u32[]{:S(2)}) copy-start(bf16[1,2,128,1024]{3,2,1,0:T(8,128)(2,1)S(1)} %collective-permute-done.1) | copy-start | bytes 1572868
  22.9 13.3 %collective-permute-start.2 = (bf16[1,2,128,1024]{3,2,1,0:T(8,128)(2,1)S(1)}, bf16[1,2,128,1024]{3,2,1,0:T(8,128)(2,1)}, u32[]{:S(2)}, u32[]{:S(2)}) collective-permute-start(bf16[1,2,128,1024]{3,2,1,0:T(8,128)(2,1)S(1)} %collective-permute-done.1), channel_id=1, source_target_pairs={{0,1},{1,2},{2,3},{3,4},{4,5},{5,6},{6,7},{7,8},{8,9},{9,10},{10,1... | collective-permute-start | bytes 1572872 | tf_op jit(solution)/shard_map/ppermute | solution.py:14
  36.1 11.0 %collective-permute-start.3 = (bf16[1,2,128,1024]{3,2,1,0:T(8,128)(2,1)}, bf16[1,2,128,1024]{3,2,1,0:T(8,128)(2,1)}, u32[]{:S(2)}, u32[]{:S(2)}) collective-permute-start(bf16[1,2,128,1024]{3,2,1,0:T(8,128)(2,1)} %collective-permute-done.2), channel_id=1, source_target_pairs={{0,1},{1,2},{2,3},{3,4},{4,5},{5,6},{6,7},{7,8},{8,9},{9,10},{10,1... | collective-permute-start | bytes 1572872 | tf_op jit(solution)/shard_map/ppermute | solution.py:14
  47.2 24.9 %collective-permute-start.4 = (bf16[1,2,128,1024]{3,2,1,0:T(8,128)(2,1)}, bf16[1,2,128,1024]{3,2,1,0:T(8,128)(2,1)}, u32[]{:S(2)}, u32[]{:S(2)}) collective-permute-start(bf16[1,2,128,1024]{3,2,1,0:T(8,128)(2,1)} %collective-permute-done.3), channel_id=1, source_target_pairs={{0,1},{1,2},{2,3},{3,4},{4,5},{5,6},{6,7},{7,8},{8,9},{9,10},{10,1... | collective-permute-start | bytes 1572872 | tf_op jit(solution)/shard_map/ppermute | solution.py:14
  72.1 22.6 %collective-permute-start.5 = (bf16[1,2,128,1024]{3,2,1,0:T(8,128)(2,1)}, bf16[1,2,128,1024]{3,2,1,0:T(8,128)(2,1)}, u32[]{:S(2)}, u32[]{:S(2)}) collective-permute-start(bf16[1,2,128,1024]{3,2,1,0:T(8,128)(2,1)} %collective-permute-done.4), channel_id=1, source_target_pairs={{0,1},{1,2},{2,3},{3,4},{4,5},{5,6},{6,7},{7,8},{8,9},{9,10},{10,1... | collective-permute-start | bytes 1572872 | tf_op jit(solution)/shard_map/ppermute | solution.py:14
  94.6 17.7 %collective-permute-start.6 = (bf16[1,2,128,1024]{3,2,1,0:T(8,128)(2,1)}, bf16[1,2,128,1024]{3,2,1,0:T(8,128)(2,1)}, u32[]{:S(2)}, u32[]{:S(2)}) collective-permute-start(bf16[1,2,128,1024]{3,2,1,0:T(8,128)(2,1)} %collective-permute-done.5), channel_id=1, source_target_pairs={{0,1},{1,2},{2,3},{3,4},{4,5},{5,6},{6,7},{7,8},{8,9},{9,10},{10,1... | collective-permute-start | bytes 1572872 | tf_op jit(solution)/shard_map/ppermute | solution.py:14
  112.4 5.3 %copy-start.33 = (f32[16,128]{1,0:T(8,128)}, f32[16,128]{1,0:T(8,128)S(1)}, u32[]{:S(2)}) copy-start(f32[16,128]{1,0:T(8,128)S(1)} %get-tuple-element.82) | copy-start | bytes 24580
  112.4 16.9 %collective-permute-start.7 = (bf16[1,2,128,1024]{3,2,1,0:T(8,128)(2,1)}, bf16[1,2,128,1024]{3,2,1,0:T(8,128)(2,1)}, u32[]{:S(2)}, u32[]{:S(2)}) collective-permute-start(bf16[1,2,128,1024]{3,2,1,0:T(8,128)(2,1)} %collective-permute-done.6), channel_id=1, source_target_pairs={{0,1},{1,2},{2,3},{3,4},{4,5},{5,6},{6,7},{7,8},{8,9},{9,10},{10,1... | collective-permute-start | bytes 1572872 | tf_op jit(solution)/shard_map/ppermute | solution.py:14
  150.1 3.4 %copy-start.27 = (f32[16,128]{1,0:T(8,128)S(1)}, f32[16,128]{1,0:T(8,128)}, u32[]{:S(2)}) copy-start(f32[16,128]{1,0:T(8,128)} %get-tuple-element.94) | copy-start | bytes 24580
  150.1 3.4 %copy-start.28 = (f32[16,128]{1,0:T(8,128)S(1)}, f32[16,128]{1,0:T(8,128)}, u32[]{:S(2)}) copy-start(f32[16,128]{1,0:T(8,128)} %get-tuple-element.92) | copy-start | bytes 24580
  150.1 3.4 %copy-start.29 = (f32[16,128]{1,0:T(8,128)S(1)}, f32[16,128]{1,0:T(8,128)}, u32[]{:S(2)}) copy-start(f32[16,128]{1,0:T(8,128)} %get-tuple-element.88) | copy-start | bytes 24580
  150.1 3.4 %copy-start.30 = (f32[16,128]{1,0:T(8,128)S(1)}, f32[16,128]{1,0:T(8,128)}, u32[]{:S(2)}) copy-start(f32[16,128]{1,0:T(8,128)} %get-tuple-element.84) | copy-start | bytes 24580
  150.1 3.5 %copy-start.31 = (f32[16,128]{1,0:T(8,128)S(1)}, f32[16,128]{1,0:T(8,128)}, u32[]{:S(2)}) copy-start(f32[16,128]{1,0:T(8,128)} %get-tuple-element.90) | copy-start | bytes 24580
  150.1 3.5 %copy-start.32 = (f32[16,128]{1,0:T(8,128)S(1)}, f32[16,128]{1,0:T(8,128)}, u32[]{:S(2)}) copy-start(f32[16,128]{1,0:T(8,128)} %get-tuple-element.86) | copy-start | bytes 24580
  150.1 3.5 %copy-start.34 = (f32[16,128]{1,0:T(8,128)S(1)}, f32[16,128]{1,0:T(8,128)}, u32[]{:S(2)}) copy-start(f32[16,128]{1,0:T(8,128)} %copy-done.33) | copy-start | bytes 24580
  150.1 3.5 %copy-start.35 = (f32[16,128]{1,0:T(8,128)S(1)}, f32[16,128]{1,0:T(8,128)}, u32[]{:S(2)}) copy-start(f32[16,128]{1,0:T(8,128)} %get-tuple-element.80) | copy-start | bytes 24580
  150.1 3.5 %copy-start.36 = (f32[16,128]{1,0:T(8,128)S(1)}, f32[16,128]{1,0:T(8,128)}, u32[]{:S(2)}) copy-start(f32[16,128]{1,0:T(8,128)} %get-tuple-element.78) | copy-start | bytes 24580
  150.2 6.0 %copy-start.6 = (bf16[1,1,1024,1024]{2,3,1,0:T(8,128)(2,1)S(1)}, bf16[1,1,1024,1024]{2,3,1,0:T(8,128)(2,1)}, u32[]{:S(2)}) copy-start(bf16[1,1,1024,1024]{2,3,1,0:T(8,128)(2,1)} %copy.105) | copy-start | bytes 6291460
  156.2 2.4 %copy-start.5 = (f32[16,128,128]{1,2,0:T(8,128)S(1)}, f32[16,128,128]{1,2,0:T(8,128)}, u32[]{:S(2)}) copy-start(f32[16,128,128]{1,2,0:T(8,128)} %get-tuple-element.79) | copy-start | bytes 3145732
  156.2 2.4 %copy-start.26 = (pred[128,128]{0,1:T(8,128)(4,1)S(1)}, pred[128,128]{0,1:T(8,128)(4,1)}, u32[]{:S(2)}) copy-start(pred[128,128]{0,1:T(8,128)(4,1)} %get-tuple-element.68) | copy-start | bytes 49156
  156.2 2.6 %copy-start.4 = (f32[16,128,128]{1,2,0:T(8,128)S(1)}, f32[16,128,128]{1,2,0:T(8,128)}, u32[]{:S(2)}) copy-start(f32[16,128,128]{1,2,0:T(8,128)} %get-tuple-element.81) | copy-start | bytes 3145732
  156.2 2.6 %copy-start.18 = (pred[128,128]{0,1:T(8,128)(4,1)S(1)}, pred[128,128]{0,1:T(8,128)(4,1)}, u32[]{:S(2)}) copy-start(pred[128,128]{0,1:T(8,128)(4,1)} %get-tuple-element.72) | copy-start | bytes 49156
  156.2 2.8 %copy-start.3 = (f32[16,128,128]{1,2,0:T(8,128)S(1)}, f32[16,128,128]{1,2,0:T(8,128)}, u32[]{:S(2)}) copy-start(f32[16,128,128]{1,2,0:T(8,128)} %get-tuple-element.83) | copy-start | bytes 3145732
  156.2 3.1 %copy-start.2 = (f32[16,128,128]{1,2,0:T(8,128)S(1)}, f32[16,128,128]{1,2,0:T(8,128)}, u32[]{:S(2)}) copy-start(f32[16,128,128]{1,2,0:T(8,128)} %get-tuple-element.85) | copy-start | bytes 3145732
  156.2 3.1 %copy-start.19 = (pred[128,128]{0,1:T(8,128)(4,1)S(1)}, pred[128,128]{0,1:T(8,128)(4,1)}, u32[]{:S(2)}) copy-start(pred[128,128]{0,1:T(8,128)(4,1)} %get-tuple-element.70) | copy-start | bytes 49156
  156.2 3.3 %copy-start.1 = (f32[16,128,128]{1,2,0:T(8,128)S(1)}, f32[16,128,128]{1,2,0:T(8,128)}, u32[]{:S(2)}) copy-start(f32[16,128,128]{1,2,0:T(8,128)} %get-tuple-element.87) | copy-start | bytes 3145732
  156.2 3.3 %copy-start.16 = (pred[128,128]{0,1:T(8,128)(4,1)S(1)}, pred[128,128]{0,1:T(8,128)(4,1)}, u32[]{:S(2)}) copy-start(pred[128,128]{0,1:T(8,128)(4,1)} %get-tuple-element.75) | copy-start | bytes 49156
  156.2 3.5 %copy-start = (f32[16,128,128]{1,2,0:T(8,128)S(1)}, f32[16,128,128]{1,2,0:T(8,128)}, u32[]{:S(2)}) copy-start(f32[16,128,128]{1,2,0:T(8,128)} %get-tuple-element.89) | copy-start | bytes 3145732
  156.3 3.5 %copy-start.17 = (pred[128,128]{0,1:T(8,128)(4,1)S(1)}, pred[128,128]{0,1:T(8,128)(4,1)}, u32[]{:S(2)}) copy-start(pred[128,128]{0,1:T(8,128)(4,1)} %get-tuple-element.73) | copy-start | bytes 49156
  156.3 3.7 %copy-start.20 = (pred[128,128]{0,1:T(8,128)(4,1)S(1)}, pred[128,128]{0,1:T(8,128)(4,1)}, u32[]{:S(2)}) copy-start(pred[128,128]{0,1:T(8,128)(4,1)} %get-tuple-element.71) | copy-start | bytes 49156
  156.3 3.9 %copy-start.22 = (pred[128,128]{0,1:T(8,128)(4,1)S(1)}, pred[128,128]{0,1:T(8,128)(4,1)}, u32[]{:S(2)}) copy-start(pred[128,128]{0,1:T(8,128)(4,1)} %copy-done.21) | copy-start | bytes 49156
  158.5 1.9 %copy-start.24 = (pred[128,128]{0,1:T(8,128)(4,1)S(1)}, pred[128,128]{0,1:T(8,128)(4,1)}, u32[]{:S(2)}) copy-start(pred[128,128]{0,1:T(8,128)(4,1)} %copy-done.23) | copy-start | bytes 49156
  158.5 2.1 %copy-start.8 = (bf16[1,1,128,1024]{2,3,1,0:T(8,128)(2,1)S(1)}, bf16[1,1,128,1024]{2,3,1,0:T(8,128)(2,1)}, u32[]{:S(2)}) copy-start(bf16[1,1,128,1024]{2,3,1,0:T(8,128)(2,1)} %copy.78) | copy-start | bytes 786436
  158.5 2.1 %copy-start.37 = (f32[128,16]{0,1:T(8,128)S(1)}, f32[128,16]{0,1:T(8,128)}, u32[]{:S(2)}) copy-start(f32[128,16]{0,1:T(8,128)} %get-tuple-element.64) | copy-start | bytes 24580
  158.5 2.1 %copy-start.38 = (f32[128,16]{0,1:T(8,128)S(1)}, f32[128,16]{0,1:T(8,128)}, u32[]{:S(2)}) copy-start(f32[128,16]{0,1:T(8,128)} %get-tuple-element.65) | copy-start | bytes 24580
  158.5 2.4 %copy-start.39 = (f32[128,16]{0,1:T(8,128)S(1)}, f32[128,16]{0,1:T(8,128)}, u32[]{:S(2)}) copy-start(f32[128,16]{0,1:T(8,128)} %get-tuple-element.32) | copy-start | bytes 24580
  158.5 2.4 %copy-start.40 = (f32[128,16]{0,1:T(8,128)S(1)}, f32[128,16]{0,1:T(8,128)}, u32[]{:S(2)}) copy-start(f32[128,16]{0,1:T(8,128)} %get-tuple-element.33) | copy-start | bytes 24580
  158.6 2.4 %copy-start.41 = (f32[128,16]{0,1:T(8,128)S(1)}, f32[128,16]{0,1:T(8,128)}, u32[]{:S(2)}) copy-start(f32[128,16]{0,1:T(8,128)} %get-tuple-element.34) | copy-start | bytes 24580
  158.6 2.5 %copy-start.7 = (bf16[1,1,128,1024]{2,3,1,0:T(8,128)(2,1)S(1)}, bf16[1,1,128,1024]{2,3,1,0:T(8,128)(2,1)}, u32[]{:S(2)}) copy-start(bf16[1,1,128,1024]{2,3,1,0:T(8,128)(2,1)} %copy.81) | copy-start | bytes 786436
  158.6 2.7 %copy-start.9 = (bf16[1,1,128,1024]{2,3,1,0:T(8,128)(2,1)S(1)}, bf16[1,1,128,1024]{2,3,1,0:T(8,128)(2,1)}, u32[]{:S(2)}) copy-start(bf16[1,1,128,1024]{2,3,1,0:T(8,128)(2,1)} %copy.84) | copy-start | bytes 786436
  158.6 3.0 %copy-start.10 = (bf16[1,1,128,1024]{2,3,1,0:T(8,128)(2,1)S(1)}, bf16[1,1,128,1024]{2,3,1,0:T(8,128)(2,1)}, u32[]{:S(2)}) copy-start(bf16[1,1,128,1024]{2,3,1,0:T(8,128)(2,1)} %copy.87) | copy-start | bytes 786436
  159.1 2.9 %copy-start.11 = (bf16[1,1,128,1024]{2,3,1,0:T(8,128)(2,1)S(1)}, bf16[1,1,128,1024]{2,3,1,0:T(8,128)(2,1)}, u32[]{:S(2)}) copy-start(bf16[1,1,128,1024]{2,3,1,0:T(8,128)(2,1)} %copy.90) | copy-start | bytes 786436
  159.5 2.7 %copy-start.12 = (bf16[1,1,128,1024]{2,3,1,0:T(8,128)(2,1)S(1)}, bf16[1,1,128,1024]{2,3,1,0:T(8,128)(2,1)}, u32[]{:S(2)}) copy-start(bf16[1,1,128,1024]{2,3,1,0:T(8,128)(2,1)} %copy.93) | copy-start | bytes 786436
  160.2 2.4 %copy-start.13 = (bf16[1,1,128,1024]{2,3,1,0:T(8,128)(2,1)S(1)}, bf16[1,1,128,1024]{2,3,1,0:T(8,128)(2,1)}, u32[]{:S(2)}) copy-start(bf16[1,1,128,1024]{2,3,1,0:T(8,128)(2,1)} %copy.96) | copy-start | bytes 786436
  160.6 2.2 %copy-start.14 = (bf16[1,1,128,1024]{2,3,1,0:T(8,128)(2,1)S(1)}, bf16[1,1,128,1024]{2,3,1,0:T(8,128)(2,1)}, u32[]{:S(2)}) copy-start(bf16[1,1,128,1024]{2,3,1,0:T(8,128)(2,1)} %copy.99) | copy-start | bytes 786436
  161.0 2.1 %copy-start.25 = (bf16[1,1,128,1024]{2,3,1,0:T(8,128)(2,1)S(1)}, bf16[1,1,128,1024]{2,3,1,0:T(8,128)(2,1)}, u32[]{:S(2)}) copy-start(bf16[1,1,128,1024]{2,3,1,0:T(8,128)(2,1)} %copy.102) | copy-start | bytes 786436
Sparse Core Ops, SparseCore 0:
  9.6 59.3 all-gather.1
where the time goes:
time: 173 us; the launch traced here: 171 us
  starting transfers between devices  62.8 us (36%)
  local copies, waits for them, and re-layouts  54.8 us (32%)
  matrix products  28.8 us (17%)
  between operations  14.4 us (8%)
  other arithmetic  9.62 us (6%)
    ppermute x8, starting transfers between devices, from_behind(): return lax.ppermute(block, axis, route)  62.8 us
    slice x18, local copies, waits for them, and re-layouts, near_block(): vals = block[0, 1].reshape(tok_rows, HEADS, HEAD)  28.2 us
    dot_general x10, matrix products, absorb(): jnp.einsum('qhd,khd->hqk', query, keys, preferred_element_type=jnp.float32)  24 us
    slice x9, local copies, waits for them, and re-layouts, near_block(): keys = block[0, 0].reshape(tok_rows, HEADS, HEAD)  11.9 us
    slice x2, local copies, waits for them, and re-layouts, on_device(): keys = piece[0, 0].reshape(count, HEADS, HEAD)  8.58 us
    dot_general x10, matrix products, absorb(): jnp.einsum('hqk,khd->hqd', rounded, vals, preferred_element_type=jnp.floa...  4.77 us
    reduce_sum x10, other arithmetic, absorb(): new_total = running_total * factor + jnp.sum(weight, axis=-1)  4.29 us
    slice x1, local copies, waits for them, and re-layouts, on_device(): vals = piece[0, 1].reshape(count, HEADS, HEAD)  3.95 us
  transfers between devices with their start and end apart: 9, of which 0 were waited for; matrix products, arithmetic and copies ran while one was open for 39% of the time, Pallas kernels for 0%

commit v1 on v0

v1 whole, which is shorter than its diff:
```python
import functools
import math

import jax
import jax.numpy as jnp
from jax import lax
from jax.experimental import pallas as pl
from jax.experimental.pallas import tpu as pltpu
from jax.sharding import PartitionSpec as P

HEADS = 16
HEAD = 64
WIN = 1024
SUB = 4
MINE = HEADS // SUB
WIDE = MINE * HEAD
ROWS = HEAD + 16
SCALE = 0.125 * math.log2(math.e)
LOW = -8e30
NEVER = -3e38

BF16 = jnp.bfloat16
F32 = jnp.float32


def place():
    position = lax.axis_index("req")
    return position // SUB, position % SUB


def partner(sub, distance):
    return jnp.bitwise_xor(sub, distance)


def columns(owner):
    return pl.ds(pl.multiple_of(owner * WIDE, WIDE), WIDE)


def params():
    return pltpu.CompilerParams(vmem_limit_bytes=48 * 1024 * 1024)


def vmem(count):
    return [pl.BlockSpec(memory_space=pltpu.VMEM)] * count


def cost(flops, moved, exps=0):
    return pl.CostEstimate(flops=flops, bytes_accessed=moved, transcendentals=exps)


def cut_kernel(parts, *refs):
    ins, outs = refs[:len(parts)], refs[len(parts):]
    _, sub = place()
    for distance in range(SUB):
        cols = columns(partner(sub, distance))
        at = 0
        for ref, count in zip(ins, parts):
            for part in range(count):
                outs[distance][at] = ref[0, part, :, cols]
                at += 1


def cut(*arrays):
    parts = [a.shape[1] for a in arrays]
    rows = arrays[0].shape[2]
    slab = jax.ShapeDtypeStruct((sum(parts), rows, WIDE), BF16)
    moved = 2 * sum(a.size * 2 for a in arrays)
    return pl.pallas_call(
        functools.partial(cut_kernel, parts),
        out_shape=[slab] * SUB,
        in_specs=vmem(len(arrays)),
        out_specs=vmem(SUB),
        compiler_params=params(),
        cost_estimate=cost(0, moved),
        name="cut",
    )(*arrays)


def exchange(slabs):
    count = lax.axis_size("req")
    got = [slabs[0]]
    for distance in range(1, SUB):
        route = [(i, i ^ distance) for i in range(count)]
        got.append(lax.ppermute(slabs[distance], "req", route))
    return got


def shift(block, blocks):
    count = lax.axis_size("req")
    route = [(i, i + SUB * blocks) for i in range(count) if 0 <= i + SUB * blocks < count]
    return lax.ppermute(block, "req", route)


def lay_kernel(*refs):
    ins, out = refs[:-1], refs[-1]
    _, sub = place()
    rows = ins[0].shape[1]
    for distance, ref in enumerate(ins):
        at = pl.ds(pl.multiple_of(partner(sub, distance) * rows, rows), rows)
        for part in range(ref.shape[0]):
            out[part, at, :] = ref[part]


def lay(slabs):
    parts, rows, width = slabs[0].shape
    return pl.pallas_call(
        lay_kernel,
        out_shape=jax.ShapeDtypeStruct((parts, rows * SUB, width), BF16),
        in_specs=vmem(SUB),
        out_specs=vmem(1)[0],
        compiler_params=params(),
        cost_estimate=cost(0, 4 * SUB * parts * rows * width),
        name="lay",
    )(*slabs)


def request_rows(lens, tokens):
    start = jnp.int32(0)
    found = jnp.zeros_like(tokens)
    for r in range(lens.shape[1]):
        found = jnp.where(tokens >= start, start, found)
        start = start + lens[0, r]
    return found


def request_start(lens, token):
    start = jnp.int32(0)
    found = jnp.int32(0)
    for r in range(lens.shape[1]):
        found = jnp.where(token >= start, start, found)
        start = start + lens[0, r]
    return found


def q_tile(tokens):
    return min(tokens, 256)


def absorb(qm, top, acc, keys, vals, first_key, lo, span, tile, at):
    count = keys.shape[0]
    cols = slice(at, at + tile)
    number = first_key + lax.broadcasted_iota(jnp.int32, (count, tile), 0)
    gap = number - lo
    allowed = (gap >= 0) & (gap <= span)
    turned = jnp.transpose(vals)
    ones = jnp.ones((ROWS - HEAD, count), BF16)
    for h in range(MINE):
        pair = slice(128 * (h // 2), 128 * (h // 2) + 128)
        score = jnp.dot(keys[:, pair], qm[h, :, cols], preferred_element_type=F32)
        score = jnp.where(allowed, score, NEVER)
        old = top[h:h + 1, cols]
        new = jnp.maximum(old, jnp.max(score, axis=0, keepdims=True))
        weight = jnp.exp2((score - new) * SCALE).astype(BF16)
        factor = jnp.exp2((old - new) * SCALE)
        value = jnp.concatenate([turned[h * HEAD:(h + 1) * HEAD], ones], axis=0)
        added = jnp.dot(value, weight, preferred_element_type=F32)
        acc[h, :, cols] = acc[h, :, cols] * factor + added
        top[h:h + 1, cols] = new


def over_suffix(lens, qm, top, acc, keys, vals, first_key, first_query):
    tokens = qm.shape[2]
    tile = q_tile(tokens)
    rows = keys.shape[0]
    piece = min(rows, 256)
    for at in range(0, tokens, tile):
        query = first_query + at
        token = query + lax.broadcasted_iota(jnp.int32, (1, tile), 1)
        lo = jnp.maximum(request_rows(lens, token), token - (WIN - 1))
        least = jnp.maximum(request_start(lens, query), query - (WIN - 1))
        for k in range(0, rows, piece):
            key = first_key + k

            @pl.when((key + piece > least) & (key < query + tile))
            def _():
                absorb(qm, top, acc, keys[k:k + piece], vals[k:k + piece], key, lo, token - lo, tile, at)


def over_prefix(lens, qm, top, acc, keys, vals, first_key, valid, first_query):
    tokens = qm.shape[2]
    tile = q_tile(tokens)
    rows = keys.shape[0]
    for at in range(0, tokens, tile):
        query = first_query + at
        token = query + lax.broadcasted_iota(jnp.int32, (1, tile), 1)
        off = token - request_rows(lens, token)
        start, last = request_start(lens, query), request_start(lens, query + tile - 1)
        least = jnp.where(start == last, query - start, 0)

        @pl.when(valid & (first_key + rows - 1 > least))
        def _():
            absorb(qm, top, acc, keys[...], vals[...], first_key, off + 1, jnp.full_like(off, WIN), tile, at)


def own_kernel(lens, s0, s1, s2, s3, own, qm, top, acc, held):
    block, sub = place()
    rows = s0.shape[1]
    tokens = rows * SUB
    for distance, ref in enumerate((s0, s1, s2, s3)):
        at = pl.ds(pl.multiple_of(partner(sub, distance) * rows, rows), rows)
        for part in range(3):
            held[part, at, :] = ref[part]
    turned = jnp.transpose(held[0])
    for h in range(MINE):
        mine, other = HEAD * (h % 2), HEAD * (1 - h % 2)
        qm[h, mine:mine + HEAD, :] = turned[h * HEAD:(h + 1) * HEAD]
        qm[h, other:other + HEAD, :] = jnp.zeros((HEAD, tokens), BF16)
    top[...] = jnp.full(top.shape, LOW, F32)
    acc[...] = jnp.zeros(acc.shape, F32)
    first = block * tokens
    over_suffix(lens, qm, top, acc, held.at[1], held.at[2], first, first)
    over_prefix(lens, qm, top, acc, own.at[0], own.at[1], block * own.shape[1], True, first)


def begin(lengths, slabs, own):
    rows = slabs[0].shape[1]
    tokens = rows * SUB
    scores = tokens * (tokens + own.shape[1]) * MINE
    return pl.pallas_call(
        own_kernel,
        out_shape=[
            jax.ShapeDtypeStruct((MINE, 2 * HEAD, tokens), BF16),
            jax.ShapeDtypeStruct((8, tokens), F32),
            jax.ShapeDtypeStruct((MINE, ROWS, tokens), F32),
        ],
        in_specs=[pl.BlockSpec(memory_space=pltpu.SMEM)] + vmem(SUB + 1),
        out_specs=vmem(3),
        scratch_shapes=[pltpu.VMEM((3, tokens, WIDE), BF16)],
        compiler_params=params(),
        cost_estimate=cost(4 * HEAD * scores, 4 << 20, scores),
        name="own",
    )(lengths, *slabs, own)


def hop_step(distance, lens, qm, top, acc, left, right):
    block, _ = place()
    blocks = lax.axis_size("req") // SUB
    first = block * qm.shape[2]
    for ref, source in ((left, block - distance), (right, block + distance)):
        valid = (source >= 0) & (source < blocks)
        over_prefix(lens, qm, top, acc, ref.at[0], ref.at[1], source * ref.shape[1], valid, first)


def hop_kernel(distance, lens, qm, top_in, acc_in, left, right, top, acc):
    top[...] = top_in[...]
    acc[...] = acc_in[...]
    hop_step(distance, lens, qm, top, acc, left, right)


def halo_kernel(distance, lens, qm, top_in, acc_in, s0, s1, s2, s3, top, acc, held):
    block, sub = place()
    rows = s0.shape[1]
    for back, ref in enumerate((s0, s1, s2, s3)):
        at = pl.ds(pl.multiple_of(partner(sub, back) * rows, rows), rows)
        for part in range(2):
            held[part, at, :] = ref[part]
    top[...] = top_in[...]
    acc[...] = acc_in[...]
    tokens = qm.shape[2]
    over_suffix(lens, qm, top, acc, held.at[0], held.at[1], (block - distance) * tokens, block * tokens)


def last_kernel(distance, lens, qm, top_in, acc_in, left, right, o0, o1, o2, o3, top, acc):
    _, sub = place()
    top[...] = top_in[...]
    acc[...] = acc_in[...]
    if distance:
        hop_step(distance, lens, qm, top, acc, left, right)
    whole = jnp.concatenate([acc[h, :HEAD] / acc[h, HEAD:HEAD + 1] for h in range(MINE)], axis=0)
    top_rows = jnp.transpose(whole.astype(BF16))
    rows = o0.shape[0]
    for source in range(SUB):
        for back, ref in enumerate((o0, o1, o2, o3)):

            @pl.when(partner(sub, back) == source)
            def _():
                ref[...] = top_rows[source * rows:(source + 1) * rows]


def carry_call(kernel, name, lengths, qm, top, acc, pieces, scratch, keys):
    scores = qm.shape[2] * keys * MINE
    return pl.pallas_call(
        kernel,
        out_shape=[jax.ShapeDtypeStruct(a.shape, a.dtype) for a in (top, acc)],
        in_specs=[pl.BlockSpec(memory_space=pltpu.SMEM)] + vmem(3 + len(pieces)),
        out_specs=vmem(2),
        scratch_shapes=scratch,
        compiler_params=params(),
        cost_estimate=cost(4 * HEAD * scores, 3 << 20, scores),
        name=name,
    )(lengths, qm, top, acc, *pieces)


def finish(distance, lengths, qm, top, acc, left, right):
    tokens = qm.shape[2]
    rows = tokens // SUB
    scores = tokens * left.shape[1] * MINE
    return pl.pallas_call(
        functools.partial(last_kernel, distance),
        out_shape=[jax.ShapeDtypeStruct((rows, WIDE), BF16)] * SUB,
        in_specs=[pl.BlockSpec(memory_space=pltpu.SMEM)] + vmem(5),
        out_specs=vmem(SUB),
        scratch_shapes=[pltpu.VMEM(top.shape, F32), pltpu.VMEM(acc.shape, F32)],
        compiler_params=params(),
        cost_estimate=cost(4 * HEAD * scores, 3 << 20, scores),
        name="last",
    )(lengths, qm, top, acc, left, right)


def join_kernel(s0, s1, s2, s3, out):
    _, sub = place()
    for distance, ref in enumerate((s0, s1, s2, s3)):
        out[0, :, columns(partner(sub, distance))] = ref[...]


def join(slabs):
    rows = slabs[0].shape[0]
    return pl.pallas_call(
        join_kernel,
        out_shape=jax.ShapeDtypeStruct((1, rows, WIDE * SUB), BF16),
        in_specs=vmem(SUB),
        out_specs=vmem(1)[0],
        compiler_params=params(),
        cost_estimate=cost(0, 4 * rows * WIDE * SUB),
        name="join",
    )(*slabs)


def on_device(queries, suffix_kv, prefix_kv, lengths):
    rows = queries.shape[1]
    count = lax.axis_size("req")
    blocks = count // SUB
    tokens = rows * SUB
    longest = count * rows // 4
    reach = -(-(min(WIN, longest) - 1) // tokens)
    reach = min(reach, blocks - 1)

    raw = [shift(suffix_kv, d) for d in range(1, reach + 1)]
    own = lay(exchange(cut(prefix_kv)))
    slabs = exchange(cut(queries[:, None], suffix_kv))
    left = right = own
    hops = []
    for distance in range(1, blocks):
        left, right = shift(left, 1), shift(right, -1)
        hops.append((left, right))
    qm, top, acc = begin(lengths, slabs, own)
    for distance in range(1, reach + 1):
        pieces = exchange(cut(raw[distance - 1]))
        held = pltpu.VMEM((2, tokens, WIDE), BF16)
        top, acc = carry_call(
            functools.partial(halo_kernel, distance), "halo", lengths, qm, top, acc, pieces, [held], tokens
        )
    for distance in range(1, blocks - 1):
        top, acc = carry_call(
            functools.partial(hop_kernel, distance), "hop", lengths, qm, top, acc, hops[distance - 1], [],
            2 * own.shape[1],
        )
    left, right = hops[-1] if hops else (own, own)
    mixed = finish(blocks - 1, lengths, qm, top, acc, left, right)
    return join(exchange(mixed))


def solution(mesh):
    in_specs = (
        P("grp", "req", None),
        P("grp", None, "req", None),
        P("grp", None, "req", None),
        P("grp", None),
    )
    out_specs = P("grp", "req", None)
    return jax.shard_map(
        on_device, mesh=mesh, in_specs=in_specs, out_specs=out_specs, check_vma=False
    )
```

time: 173 us -> 67 us (0.39)
  the two profiles are of different devices: /device:TPU:0 before, /device:TPU:17 now
where the time goes in v1:
time: 67 us; the launch traced here: 66.7 us
  starting transfers between devices  32 us (48%)
  Pallas kernels  20.5 us (31%)
  waiting for transfers between devices  13 us (19%)
  local copies, waits for them, and re-layouts  0.95 us (1%)
    ppermute x7, starting transfers between devices, shift(): return lax.ppermute(block, 'req', route)  19.3 us
    ppermute x12, starting transfers between devices, exchange(): got.append(lax.ppermute(slabs[distance], 'req', route))  12.8 us
    pallas_call x3, Pallas kernels, carry_call(): pl.pallas_call(kernel, out_shape=[jax.ShapeDtypeStruct(a.shape, a.dtype)...  11.8 us
    ppermute x12, waiting for transfers between devices, exchange(): got.append(lax.ppermute(slabs[distance], 'req', route))  7.61 us
    pallas_call x1, Pallas kernels, begin(): pl.pallas_call(own_kernel, out_shape=[jax.ShapeDtypeStruct((MINE, 2 * HEA...  6.82 us
    ppermute x7, waiting for transfers between devices, shift(): return lax.ppermute(block, 'req', route)  5.35 us
  transfers between devices with their start and end apart: 19, of which 7 were waited for; matrix products, arithmetic and copies ran while one was open for 0% of the time, Pallas kernels for 28%

profile of v1, /device:TPU:17, one launch (start us, length us, event | category | flops | bytes accessed | tf_op | source)
XLA Modules:
  0.0 66.7 jit_solution(15333944853456256607)
XLA Ops:
  0.0 0.0 copy-start
  0.0 3.3 %collective-permute-start.6 = (bf16[1,2,128,1024]{3,2,1,0:T(8,128)(2,1)}, bf16[1,2,128,1024]{3,2,1,0:T(8,128)(2,1)S(1)}, u32[]{:S(2)}, u32[]{:S(2)}) collective-permute-start(bf16[1,2,128,1024]{3,2,1,0:T(8,128)(2,1)} %refs_1_.1), channel_id=1, source_target_pairs={{0,4},{1,5},{2,6},{3,7},{4,8},{5,9},{6,10},{7,11},{8,12},{9,13},{1... | collective-permute-start | bytes 1572872 | tf_op jit(solution)/shard_map/ppermute | solution.py:91
  3.3 0.0 copy-start.2
  3.3 0.9 %copy-done.2 = bf16[1,2,64,1024]{3,2,1,0:T(8,128)(2,1)S(1)} copy-done((bf16[1,2,64,1024]{3,2,1,0:T(8,128)(2,1)S(1)}, bf16[1,2,64,1024]{3,2,1,0:T(8,128)(2,1)}, u32[]{:S(2)}) %copy-start.2) | copy-done | bytes 262168
  4.3 1.0 %collective-permute-start.3 = (bf16[2,64,256]{2,1,0:T(8,128)(2,1)S(1)}, bf16[2,64,256]{2,1,0:T(8,128)(2,1)S(1)}, u32[]{:S(2)}, u32[]{:S(2)}) collective-permute-start(bf16[2,64,256]{2,1,0:T(8,128)(2,1)S(1)} %get-tuple-element.35), channel_id=1, source_target_pairs={{0,1},{1,0},{2,3},{3,2},{4,5},{5,4},{6,7},{7,6},{8,9},{9,8},{10,11... | collective-permute-start | bytes 196616 | tf_op jit(solution)/shard_map/ppermute | solution.py:84
  5.3 1.3 %collective-permute-start.4 = (bf16[2,64,256]{2,1,0:T(8,128)(2,1)S(1)}, bf16[2,64,256]{2,1,0:T(8,128)(2,1)S(1)}, u32[]{:S(2)}, u32[]{:S(2)}) collective-permute-start(bf16[2,64,256]{2,1,0:T(8,128)(2,1)S(1)} %get-tuple-element.36), channel_id=1, source_target_pairs={{0,2},{1,3},{2,0},{3,1},{4,6},{5,7},{6,4},{7,5},{8,10},{9,11},{10,... | collective-permute-start | bytes 196616 | tf_op jit(solution)/shard_map/ppermute | solution.py:84
  6.6 0.5 collective-permute-start.5
  7.1 0.0 collective-permute-done.3.refs_1_
  7.1 2.0 %collective-permute-done.4.refs_2_ = bf16[2,64,256]{2,1,0:T(8,128)(2,1)S(1)} collective-permute-done((bf16[2,64,256]{2,1,0:T(8,128)(2,1)S(1)}, bf16[2,64,256]{2,1,0:T(8,128)(2,1)S(1)}, u32[]{:S(2)}, u32[]{:S(2)}) %collective-permute-start.4) | collective-permute-done | bytes 65568 | tf_op jit(solution)/shard_map/ppermute | solution.py:84
  9.0 1.9 %collective-permute-done.5.refs_3_ = bf16[2,64,256]{2,1,0:T(8,128)(2,1)S(1)} collective-permute-done((bf16[2,64,256]{2,1,0:T(8,128)(2,1)S(1)}, bf16[2,64,256]{2,1,0:T(8,128)(2,1)S(1)}, u32[]{:S(2)}, u32[]{:S(2)}) %collective-permute-start.5) | collective-permute-done | bytes 65568 | tf_op jit(solution)/shard_map/ppermute | solution.py:84
  10.9 0.0 copy-start.1
  11.0 2.1 %collective-permute-start.10 = (bf16[2,256,256]{2,1,0:T(8,128)(2,1)S(1)}, bf16[2,256,256]{2,1,0:T(8,128)(2,1)S(1)}, u32[]{:S(2)}, u32[]{:S(2)}) collective-permute-start(bf16[2,256,256]{2,1,0:T(8,128)(2,1)S(1)} %lay.1.own), channel_id=1, source_target_pairs={{0,4},{1,5},{2,6},{3,7},{4,8},{5,9},{6,10},{7,11},{8,12},{9,13},{1... | collective-permute-start | bytes 786440 | tf_op jit(solution)/shard_map/ppermute | solution.py:91
  13.0 3.4 %collective-permute-start.11 = (bf16[2,256,256]{2,1,0:T(8,128)(2,1)S(1)}, bf16[2,256,256]{2,1,0:T(8,128)(2,1)S(1)}, u32[]{:S(2)}, u32[]{:S(2)}) collective-permute-start(bf16[2,256,256]{2,1,0:T(8,128)(2,1)S(1)} %lay.1.own), channel_id=1, source_target_pairs={{4,0},{5,1},{6,2},{7,3},{8,4},{9,5},{10,6},{11,7},{12,8},{13,9},{1... | collective-permute-start | bytes 786440 | tf_op jit(solution)/shard_map/ppermute | solution.py:91
  16.4 5.0 %collective-permute-done.10.left = bf16[2,256,256]{2,1,0:T(8,128)(2,1)S(1)} collective-permute-done((bf16[2,256,256]{2,1,0:T(8,128)(2,1)S(1)}, bf16[2,256,256]{2,1,0:T(8,128)(2,1)S(1)}, u32[]{:S(2)}, u32[]{:S(2)}) %collective-permute-start.10) | collective-permute-done | bytes 262176 | tf_op jit(solution)/shard_map/ppermute | solution.py:91
  21.4 2.4 %collective-permute-start.12 = (bf16[2,256,256]{2,1,0:T(8,128)(2,1)S(1)}, bf16[2,256,256]{2,1,0:T(8,128)(2,1)S(1)}, u32[]{:S(2)}, u32[]{:S(2)}) collective-permute-start(bf16[2,256,256]{2,1,0:T(8,128)(2,1)S(1)} %collective-permute-done.10.left), channel_id=1, source_target_pairs={{0,4},{1,5},{2,6},{3,7},{4,8},{5,9},{6,10},{7,11},{8,12},{9,13},{1... | collective-permute-start | bytes 786440 | tf_op jit(solution)/shard_map/ppermute | solution.py:91
  23.8 0.0 collective-permute-done.11.right
  23.8 2.8 %collective-permute-start.13 = (bf16[2,256,256]{2,1,0:T(8,128)(2,1)S(1)}, bf16[2,256,256]{2,1,0:T(8,128)(2,1)S(1)}, u32[]{:S(2)}, u32[]{:S(2)}) collective-permute-start(bf16[2,256,256]{2,1,0:T(8,128)(2,1)S(1)} %collective-permute-done.11.right), channel_id=1, source_target_pairs={{4,0},{5,1},{6,2},{7,3},{8,4},{9,5},{10,6},{11,7},{12,8},{13,9},{1... | collective-permute-start | bytes 786440 | tf_op jit(solution)/shard_map/ppermute | solution.py:91
  26.7 0.0 copy-done
  26.7 0.0 copy-done.1
  26.7 0.1 cut.3
  26.8 1.4 %collective-permute-start = (bf16[3,128,256]{2,1,0:T(8,128)(2,1)S(1)}, bf16[3,128,256]{2,1,0:T(8,128)(2,1)S(1)}, u32[]{:S(2)}, u32[]{:S(2)}) collective-permute-start(bf16[3,128,256]{2,1,0:T(8,128)(2,1)S(1)} %get-tuple-element.31), channel_id=1, source_target_pairs={{0,1},{1,0},{2,3},{3,2},{4,5},{5,4},{6,7},{7,6},{8,9},{9,8},{10,11... | collective-permute-start | bytes 589832 | tf_op jit(solution)/shard_map/ppermute | solution.py:84
  28.3 1.3 %collective-permute-start.1 = (bf16[3,128,256]{2,1,0:T(8,128)(2,1)S(1)}, bf16[3,128,256]{2,1,0:T(8,128)(2,1)S(1)}, u32[]{:S(2)}, u32[]{:S(2)}) collective-permute-start(bf16[3,128,256]{2,1,0:T(8,128)(2,1)S(1)} %get-tuple-element.32), channel_id=1, source_target_pairs={{0,2},{1,3},{2,0},{3,1},{4,6},{5,7},{6,4},{7,5},{8,10},{9,11},{10,... | collective-permute-start | bytes 589832 | tf_op jit(solution)/shard_map/ppermute | solution.py:84
  29.5 0.0 collective-permute-done.6.refs_0_
  29.5 0.5 collective-permute-start.2
  30.0 0.4 collective-permute-done.12.left
  30.3 2.9 %collective-permute-start.14 = (bf16[2,256,256]{2,1,0:T(8,128)(2,1)S(1)}, bf16[2,256,256]{2,1,0:T(8,128)(2,1)S(1)}, u32[]{:S(2)}, u32[]{:S(2)}) collective-permute-start(bf16[2,256,256]{2,1,0:T(8,128)(2,1)S(1)} %collective-permute-done.12.left), channel_id=1, source_target_pairs={{0,4},{1,5},{2,6},{3,7},{4,8},{5,9},{6,10},{7,11},{8,12},{9,13},{1... | collective-permute-start | bytes 786440 | tf_op jit(solution)/shard_map/ppermute | solution.py:91
  33.2 0.0 collective-permute-done.13.right
  33.2 2.4 %collective-permute-start.15 = (bf16[2,256,256]{2,1,0:T(8,128)(2,1)S(1)}, bf16[2,256,256]{2,1,0:T(8,128)(2,1)S(1)}, u32[]{:S(2)}, u32[]{:S(2)}) collective-permute-start(bf16[2,256,256]{2,1,0:T(8,128)(2,1)S(1)} %collective-permute-done.13.right), channel_id=1, source_target_pairs={{4,0},{5,1},{6,2},{7,3},{8,4},{9,5},{10,6},{11,7},{12,8},{13,9},{1... | collective-permute-start | bytes 786440 | tf_op jit(solution)/shard_map/ppermute | solution.py:91
  35.6 0.1 cut.5
  35.7 0.0 collective-permute-done.s1
  35.7 2.3 %collective-permute-start.7 = (bf16[2,128,256]{2,1,0:T(8,128)(2,1)S(1)}, bf16[2,128,256]{2,1,0:T(8,128)(2,1)S(1)}, u32[]{:S(2)}, u32[]{:S(2)}) collective-permute-start(bf16[2,128,256]{2,1,0:T(8,128)(2,1)S(1)} %get-tuple-element.42), channel_id=1, source_target_pairs={{0,1},{1,0},{2,3},{3,2},{4,5},{5,4},{6,7},{7,6},{8,9},{9,8},{10,11... | collective-permute-start | bytes 393224 | tf_op jit(solution)/shard_map/ppermute | solution.py:84
  38.0 0.0 collective-permute-done.1.s2
  38.0 1.2 %collective-permute-start.8 = (bf16[2,128,256]{2,1,0:T(8,128)(2,1)S(1)}, bf16[2,128,256]{2,1,0:T(8,128)(2,1)S(1)}, u32[]{:S(2)}, u32[]{:S(2)}) collective-permute-start(bf16[2,128,256]{2,1,0:T(8,128)(2,1)S(1)} %get-tuple-element.43), channel_id=1, source_target_pairs={{0,2},{1,3},{2,0},{3,1},{4,6},{5,7},{6,4},{7,5},{8,10},{9,11},{10,... | collective-permute-start | bytes 393224 | tf_op jit(solution)/shard_map/ppermute | solution.py:84
  39.2 0.2 collective-permute-done.2.s3
  39.4 0.0 copy-start.3
  39.4 1.1 %collective-permute-start.9 = (bf16[2,128,256]{2,1,0:T(8,128)(2,1)S(1)}, bf16[2,128,256]{2,1,0:T(8,128)(2,1)S(1)}, u32[]{:S(2)}, u32[]{:S(2)}) collective-permute-start(bf16[2,128,256]{2,1,0:T(8,128)(2,1)S(1)} %get-tuple-element.44), channel_id=1, source_target_pairs={{0,3},{1,2},{2,1},{3,0},{4,7},{5,6},{6,5},{7,4},{8,11},{9,10},{10,... | collective-permute-start | bytes 393224 | tf_op jit(solution)/shard_map/ppermute | solution.py:84
  40.5 0.0 copy-done.3
  40.5 6.8 %own.1 = (bf16[4,128,512]{2,1,0:T(8,128)(2,1)S(1)}, f32[8,512]{1,0:T(8,128)S(1)}, f32[4,80,512]{2,1,0:T(8,128)S(1)}) custom-call(s32[1,12]{1,0:T(1,128)S(1)} %copy-done.3, bf16[3,128,256]{2,1,0:T(8,128)(2,1)S(1)} %get-tuple-element.30.s0, bf16[3,128,256]{2,1,0:T(8,128)(2,1)S(1)} %collective-permute-done.s1, ...), custom_call_target="tpu_custom_call" | custom-call | flops 402653184 | bytes 4194304 | tf_op jit(solution)/shard_map/own/pallas_call | solution.py:219
  47.3 0.0 collective-permute-done.7.s1
  47.3 0.0 collective-permute-done.8.s2
  47.3 0.0 collective-permute-done.9.s3
  47.3 3.1 %halo.1 = (f32[8,512]{1,0:T(8,128)S(1)}, f32[4,80,512]{2,1,0:T(8,128)S(1)}) custom-call(s32[1,12]{1,0:T(1,128)S(1)} %copy-done.3, bf16[4,128,512]{2,1,0:T(8,128)(2,1)S(1)} %get-tuple-element.38.qm, f32[8,512]{1,0:T(8,128)S(1)} %get-tuple-element.39.top_in, f32[4,80,512]{2,1,0:T(8,128)S(1)} %get-tuple-element.40.acc_in, ...), custom_call_target="tpu_custom_call" | custom-call | flops 268435456 | bytes 3145728 | tf_op jit(solution)/shard_map/halo/pallas_call | solution.py:282
  50.4 5.5 %hop.2 = (f32[8,512]{1,0:T(8,128)S(1)}, f32[4,80,512]{2,1,0:T(8,128)S(1)}) custom-call(s32[1,12]{1,0:T(1,128)S(1)} %copy-done.3, bf16[4,128,512]{2,1,0:T(8,128)(2,1)S(1)} %get-tuple-element.38.qm, f32[8,512]{1,0:T(8,128)S(1)} %get-tuple-element.45.top_in, f32[4,80,512]{2,1,0:T(8,128)S(1)} %get-tuple-element.46.acc_in, ...), custom_call_target="tpu_custom_call" | custom-call | flops 268435456 | bytes 3145728 | tf_op jit(solution)/shard_map/hop/pallas_call | solution.py:282
  55.9 3.3 %hop.3 = (f32[8,512]{1,0:T(8,128)S(1)}, f32[4,80,512]{2,1,0:T(8,128)S(1)}) custom-call(s32[1,12]{1,0:T(1,128)S(1)} %copy-done.3, bf16[4,128,512]{2,1,0:T(8,128)(2,1)S(1)} %get-tuple-element.38.qm, f32[8,512]{1,0:T(8,128)S(1)} %get-tuple-element.47.top_in, f32[4,80,512]{2,1,0:T(8,128)S(1)} %get-tuple-element.48.acc_in, ...), custom_call_target="tpu_custom_call" | custom-call | flops 268435456 | bytes 3145728 | tf_op jit(solution)/shard_map/hop/pallas_call | solution.py:282
  59.2 0.0 collective-permute-done.14.left
  59.2 0.0 collective-permute-done.15.right
  59.2 0.9 %last.1 = (bf16[128,256]{1,0:T(8,128)(2,1)S(1)}, bf16[128,256]{1,0:T(8,128)(2,1)S(1)}, bf16[128,256]{1,0:T(8,128)(2,1)S(1)}, bf16[128,256]{1,0:T(8,128)(2,1)S(1)}) custom-call(s32[1,12]{1,0:T(1,128)S(1)} %copy-done.3, bf16[4,128,512]{2,1,0:T(8,128)(2,1)S(1)} %get-tuple-element.38.qm, f32[8,512]{1,0:T(8,128)S(1)} %get-tuple-element.49.top_in, ...), custom_call_target="tpu_custom_call" | custom-call | flops 134217728 | bytes 3145728 | tf_op jit(solution)/shard_map/last/pallas_call | solution.py:298
  60.1 0.6 collective-permute-start.16
  60.7 0.3 collective-permute-start.17
  61.1 1.4 %collective-permute-start.18 = (bf16[128,256]{1,0:T(8,128)(2,1)S(1)}, bf16[128,256]{1,0:T(8,128)(2,1)S(1)}, u32[]{:S(2)}, u32[]{:S(2)}) collective-permute-start(bf16[128,256]{1,0:T(8,128)(2,1)S(1)} %get-tuple-element.54), channel_id=1, source_target_pairs={{0,3},{1,2},{2,1},{3,0},{4,7},{5,6},{6,5},{7,4},{8,11},{9,10},{10,... | collective-permute-start | bytes 196616 | tf_op jit(solution)/shard_map/ppermute | solution.py:84
  62.4 0.0 collective-permute-done.16.s1
  62.4 2.0 %collective-permute-done.17.s2 = bf16[128,256]{1,0:T(8,128)(2,1)S(1)} collective-permute-done((bf16[128,256]{1,0:T(8,128)(2,1)S(1)}, bf16[128,256]{1,0:T(8,128)(2,1)S(1)}, u32[]{:S(2)}, u32[]{:S(2)}) %collective-permute-start.17) | collective-permute-done | bytes 65568 | tf_op jit(solution)/shard_map/ppermute | solution.py:84
  64.4 1.6 %collective-permute-done.18.s3 = bf16[128,256]{1,0:T(8,128)(2,1)S(1)} collective-permute-done((bf16[128,256]{1,0:T(8,128)(2,1)S(1)}, bf16[128,256]{1,0:T(8,128)(2,1)S(1)}, u32[]{:S(2)}, u32[]{:S(2)}) %collective-permute-start.18) | collective-permute-done | bytes 65568 | tf_op jit(solution)/shard_map/ppermute | solution.py:84
  66.0 0.7 %join.1 = bf16[1,128,1024]{2,1,0:T(8,128)(2,1)} custom-call(bf16[128,256]{1,0:T(8,128)(2,1)S(1)} %get-tuple-element.51.s0, bf16[128,256]{1,0:T(8,128)(2,1)S(1)} %collective-permute-done.16.s1, bf16[128,256]{1,0:T(8,128)(2,1)S(1)} %collective-permute-done.17.s2, bf16[128,256]{1,0:T(8,128)(2,1)S(1)} %collective-permute-done.18.s3), custom_call_target="tpu_custom_call" | custom-call | bytes 524288 | tf_op jit(solution)/shard_map/join/pallas_call | solution.py:318
  (2 shorter events, 0.1 us)
Async XLA Ops:
  0.0 26.7 %copy-start = (bf16[1,2,128,1024]{3,2,1,0:T(8,128)(2,1)S(1)}, bf16[1,2,128,1024]{3,2,1,0:T(8,128)(2,1)}, u32[]{:S(2)}) copy-start(bf16[1,2,128,1024]{3,2,1,0:T(8,128)(2,1)} %refs_1_.1) | copy-start | bytes 1572868
  0.0 29.5 %collective-permute-start.6 = (bf16[1,2,128,1024]{3,2,1,0:T(8,128)(2,1)}, bf16[1,2,128,1024]{3,2,1,0:T(8,128)(2,1)S(1)}, u32[]{:S(2)}, u32[]{:S(2)}) collective-permute-start(bf16[1,2,128,1024]{3,2,1,0:T(8,128)(2,1)} %refs_1_.1), channel_id=1, source_target_pairs={{0,4},{1,5},{2,6},{3,7},{4,8},{5,9},{6,10},{7,11},{8,12},{9,13},{1... | collective-permute-start | bytes 1572872 | tf_op jit(solution)/shard_map/ppermute | solution.py:91
  3.3 1.0 %copy-start.2 = (bf16[1,2,64,1024]{3,2,1,0:T(8,128)(2,1)S(1)}, bf16[1,2,64,1024]{3,2,1,0:T(8,128)(2,1)}, u32[]{:S(2)}) copy-start(bf16[1,2,64,1024]{3,2,1,0:T(8,128)(2,1)} %refs_0_.1) | copy-start | bytes 786436
  4.3 2.7 %collective-permute-start.3 = (bf16[2,64,256]{2,1,0:T(8,128)(2,1)S(1)}, bf16[2,64,256]{2,1,0:T(8,128)(2,1)S(1)}, u32[]{:S(2)}, u32[]{:S(2)}) collective-permute-start(bf16[2,64,256]{2,1,0:T(8,128)(2,1)S(1)} %get-tuple-element.35), channel_id=1, source_target_pairs={{0,1},{1,0},{2,3},{3,2},{4,5},{5,4},{6,7},{7,6},{8,9},{9,8},{10,11... | collective-permute-start | bytes 196616 | tf_op jit(solution)/shard_map/ppermute | solution.py:84
  5.3 3.7 %collective-permute-start.4 = (bf16[2,64,256]{2,1,0:T(8,128)(2,1)S(1)}, bf16[2,64,256]{2,1,0:T(8,128)(2,1)S(1)}, u32[]{:S(2)}, u32[]{:S(2)}) collective-permute-start(bf16[2,64,256]{2,1,0:T(8,128)(2,1)S(1)} %get-tuple-element.36), channel_id=1, source_target_pairs={{0,2},{1,3},{2,0},{3,1},{4,6},{5,7},{6,4},{7,5},{8,10},{9,11},{10,... | collective-permute-start | bytes 196616 | tf_op jit(solution)/shard_map/ppermute | solution.py:84
  6.6 4.3 %collective-permute-start.5 = (bf16[2,64,256]{2,1,0:T(8,128)(2,1)S(1)}, bf16[2,64,256]{2,1,0:T(8,128)(2,1)S(1)}, u32[]{:S(2)}, u32[]{:S(2)}) collective-permute-start(bf16[2,64,256]{2,1,0:T(8,128)(2,1)S(1)} %get-tuple-element.37), channel_id=1, source_target_pairs={{0,3},{1,2},{2,1},{3,0},{4,7},{5,6},{6,5},{7,4},{8,11},{9,10},{10,... | collective-permute-start | bytes 196616 | tf_op jit(solution)/shard_map/ppermute | solution.py:84
  10.9 15.8 %copy-start.1 = (bf16[1,128,1024]{2,1,0:T(8,128)(2,1)S(1)}, bf16[1,128,1024]{2,1,0:T(8,128)(2,1)}, u32[]{:S(2)}) copy-start(bf16[1,128,1024]{2,1,0:T(8,128)(2,1)} %param.4) | copy-start | bytes 786436
  11.0 10.4 %collective-permute-start.10 = (bf16[2,256,256]{2,1,0:T(8,128)(2,1)S(1)}, bf16[2,256,256]{2,1,0:T(8,128)(2,1)S(1)}, u32[]{:S(2)}, u32[]{:S(2)}) collective-permute-start(bf16[2,256,256]{2,1,0:T(8,128)(2,1)S(1)} %lay.1.own), channel_id=1, source_target_pairs={{0,4},{1,5},{2,6},{3,7},{4,8},{5,9},{6,10},{7,11},{8,12},{9,13},{1... | collective-permute-start | bytes 786440 | tf_op jit(solution)/shard_map/ppermute | solution.py:91
  13.0 10.8 %collective-permute-start.11 = (bf16[2,256,256]{2,1,0:T(8,128)(2,1)S(1)}, bf16[2,256,256]{2,1,0:T(8,128)(2,1)S(1)}, u32[]{:S(2)}, u32[]{:S(2)}) collective-permute-start(bf16[2,256,256]{2,1,0:T(8,128)(2,1)S(1)} %lay.1.own), channel_id=1, source_target_pairs={{4,0},{5,1},{6,2},{7,3},{8,4},{9,5},{10,6},{11,7},{12,8},{13,9},{1... | collective-permute-start | bytes 786440 | tf_op jit(solution)/shard_map/ppermute | solution.py:91
  21.4 8.9 %collective-permute-start.12 = (bf16[2,256,256]{2,1,0:T(8,128)(2,1)S(1)}, bf16[2,256,256]{2,1,0:T(8,128)(2,1)S(1)}, u32[]{:S(2)}, u32[]{:S(2)}) collective-permute-start(bf16[2,256,256]{2,1,0:T(8,128)(2,1)S(1)} %collective-permute-done.10.left), channel_id=1, source_target_pairs={{0,4},{1,5},{2,6},{3,7},{4,8},{5,9},{6,10},{7,11},{8,12},{9,13},{1... | collective-permute-start | bytes 786440 | tf_op jit(solution)/shard_map/ppermute | solution.py:91
  23.8 9.3 %collective-permute-start.13 = (bf16[2,256,256]{2,1,0:T(8,128)(2,1)S(1)}, bf16[2,256,256]{2,1,0:T(8,128)(2,1)S(1)}, u32[]{:S(2)}, u32[]{:S(2)}) collective-permute-start(bf16[2,256,256]{2,1,0:T(8,128)(2,1)S(1)} %collective-permute-done.11.right), channel_id=1, source_target_pairs={{4,0},{5,1},{6,2},{7,3},{8,4},{9,5},{10,6},{11,7},{12,8},{13,9},{1... | collective-permute-start | bytes 786440 | tf_op jit(solution)/shard_map/ppermute | solution.py:91
  26.8 8.9 %collective-permute-start = (bf16[3,128,256]{2,1,0:T(8,128)(2,1)S(1)}, bf16[3,128,256]{2,1,0:T(8,128)(2,1)S(1)}, u32[]{:S(2)}, u32[]{:S(2)}) collective-permute-start(bf16[3,128,256]{2,1,0:T(8,128)(2,1)S(1)} %get-tuple-element.31), channel_id=1, source_target_pairs={{0,1},{1,0},{2,3},{3,2},{4,5},{5,4},{6,7},{7,6},{8,9},{9,8},{10,11... | collective-permute-start | bytes 589832 | tf_op jit(solution)/shard_map/ppermute | solution.py:84
  28.3 9.8 %collective-permute-start.1 = (bf16[3,128,256]{2,1,0:T(8,128)(2,1)S(1)}, bf16[3,128,256]{2,1,0:T(8,128)(2,1)S(1)}, u32[]{:S(2)}, u32[]{:S(2)}) collective-permute-start(bf16[3,128,256]{2,1,0:T(8,128)(2,1)S(1)} %get-tuple-element.32), channel_id=1, source_target_pairs={{0,2},{1,3},{2,0},{3,1},{4,6},{5,7},{6,4},{7,5},{8,10},{9,11},{10,... | collective-permute-start | bytes 589832 | tf_op jit(solution)/shard_map/ppermute | solution.py:84
  29.5 9.9 %collective-permute-start.2 = (bf16[3,128,256]{2,1,0:T(8,128)(2,1)S(1)}, bf16[3,128,256]{2,1,0:T(8,128)(2,1)S(1)}, u32[]{:S(2)}, u32[]{:S(2)}) collective-permute-start(bf16[3,128,256]{2,1,0:T(8,128)(2,1)S(1)} %get-tuple-element.33), channel_id=1, source_target_pairs={{0,3},{1,2},{2,1},{3,0},{4,7},{5,6},{6,5},{7,4},{8,11},{9,10},{10,... | collective-permute-start | bytes 589832 | tf_op jit(solution)/shard_map/ppermute | solution.py:84
  30.3 28.9 %collective-permute-start.14 = (bf16[2,256,256]{2,1,0:T(8,128)(2,1)S(1)}, bf16[2,256,256]{2,1,0:T(8,128)(2,1)S(1)}, u32[]{:S(2)}, u32[]{:S(2)}) collective-permute-start(bf16[2,256,256]{2,1,0:T(8,128)(2,1)S(1)} %collective-permute-done.12.left), channel_id=1, source_target_pairs={{0,4},{1,5},{2,6},{3,7},{4,8},{5,9},{6,10},{7,11},{8,12},{9,13},{1... | collective-permute-start | bytes 786440 | tf_op jit(solution)/shard_map/ppermute | solution.py:91
  33.2 26.0 %collective-permute-start.15 = (bf16[2,256,256]{2,1,0:T(8,128)(2,1)S(1)}, bf16[2,256,256]{2,1,0:T(8,128)(2,1)S(1)}, u32[]{:S(2)}, u32[]{:S(2)}) collective-permute-start(bf16[2,256,256]{2,1,0:T(8,128)(2,1)S(1)} %collective-permute-done.13.right), channel_id=1, source_target_pairs={{4,0},{5,1},{6,2},{7,3},{8,4},{9,5},{10,6},{11,7},{12,8},{13,9},{1... | collective-permute-start | bytes 786440 | tf_op jit(solution)/shard_map/ppermute | solution.py:91
  35.7 11.6 %collective-permute-start.7 = (bf16[2,128,256]{2,1,0:T(8,128)(2,1)S(1)}, bf16[2,128,256]{2,1,0:T(8,128)(2,1)S(1)}, u32[]{:S(2)}, u32[]{:S(2)}) collective-permute-start(bf16[2,128,256]{2,1,0:T(8,128)(2,1)S(1)} %get-tuple-element.42), channel_id=1, source_target_pairs={{0,1},{1,0},{2,3},{3,2},{4,5},{5,4},{6,7},{7,6},{8,9},{9,8},{10,11... | collective-permute-start | bytes 393224 | tf_op jit(solution)/shard_map/ppermute | solution.py:84
  38.0 9.3 %collective-permute-start.8 = (bf16[2,128,256]{2,1,0:T(8,128)(2,1)S(1)}, bf16[2,128,256]{2,1,0:T(8,128)(2,1)S(1)}, u32[]{:S(2)}, u32[]{:S(2)}) collective-permute-start(bf16[2,128,256]{2,1,0:T(8,128)(2,1)S(1)} %get-tuple-element.43), channel_id=1, source_target_pairs={{0,2},{1,3},{2,0},{3,1},{4,6},{5,7},{6,4},{7,5},{8,10},{9,11},{10,... | collective-permute-start | bytes 393224 | tf_op jit(solution)/shard_map/ppermute | solution.py:84
  39.4 1.1 %copy-start.3 = (s32[1,12]{1,0:T(1,128)S(1)}, s32[1,12]{1,0:T(1,128)}, u32[]{:S(2)}) copy-start(s32[1,12]{1,0:T(1,128)} %lens.9) | copy-start | bytes 148
  39.4 7.9 %collective-permute-start.9 = (bf16[2,128,256]{2,1,0:T(8,128)(2,1)S(1)}, bf16[2,128,256]{2,1,0:T(8,128)(2,1)S(1)}, u32[]{:S(2)}, u32[]{:S(2)}) collective-permute-start(bf16[2,128,256]{2,1,0:T(8,128)(2,1)S(1)} %get-tuple-element.44), channel_id=1, source_target_pairs={{0,3},{1,2},{2,1},{3,0},{4,7},{5,6},{6,5},{7,4},{8,11},{9,10},{10,... | collective-permute-start | bytes 393224 | tf_op jit(solution)/shard_map/ppermute | solution.py:84
  60.1 2.4 %collective-permute-start.16 = (bf16[128,256]{1,0:T(8,128)(2,1)S(1)}, bf16[128,256]{1,0:T(8,128)(2,1)S(1)}, u32[]{:S(2)}, u32[]{:S(2)}) collective-permute-start(bf16[128,256]{1,0:T(8,128)(2,1)S(1)} %get-tuple-element.52), channel_id=1, source_target_pairs={{0,1},{1,0},{2,3},{3,2},{4,5},{5,4},{6,7},{7,6},{8,9},{9,8},{10,11... | collective-permute-start | bytes 196616 | tf_op jit(solution)/shard_map/ppermute | solution.py:84
  60.7 3.7 %collective-permute-start.17 = (bf16[128,256]{1,0:T(8,128)(2,1)S(1)}, bf16[128,256]{1,0:T(8,128)(2,1)S(1)}, u32[]{:S(2)}, u32[]{:S(2)}) collective-permute-start(bf16[128,256]{1,0:T(8,128)(2,1)S(1)} %get-tuple-element.53), channel_id=1, source_target_pairs={{0,2},{1,3},{2,0},{3,1},{4,6},{5,7},{6,4},{7,5},{8,10},{9,11},{10,... | collective-permute-start | bytes 196616 | tf_op jit(solution)/shard_map/ppermute | solution.py:84
  61.1 4.9 %collective-permute-start.18 = (bf16[128,256]{1,0:T(8,128)(2,1)S(1)}, bf16[128,256]{1,0:T(8,128)(2,1)S(1)}, u32[]{:S(2)}, u32[]{:S(2)}) collective-permute-start(bf16[128,256]{1,0:T(8,128)(2,1)S(1)} %get-tuple-element.54), channel_id=1, source_target_pairs={{0,3},{1,2},{2,1},{3,0},{4,7},{5,6},{6,5},{7,4},{8,11},{9,10},{10,... | collective-permute-start | bytes 196616 | tf_op jit(solution)/shard_map/ppermute | solution.py:84

commit v2 on v1

--- a/solution.py
+++ b/solution.py
@@ -85,10 +85,37 @@
     return got
 
 
-def shift(block, blocks):
-    count = lax.axis_size("req")
-    route = [(i, i + SUB * blocks) for i in range(count) if 0 <= i + SUB * blocks < count]
-    return lax.ppermute(block, "req", route)
+def between(block, routes):
+    return lax.ppermute(block, "req", [(SUB * a + s, SUB * b + s) for a, b in routes for s in range(SUB)])
+
+
+def shift(block, blocks, since=0):
+    last = lax.axis_size("req") // SUB - 1
+    low, high = (since, last - blocks) if blocks > 0 else (-blocks, last - since)
+    return between(block, [(b, b + blocks) for b in range(low, high + 1)])
+
+
+def gather_four(own):
+    two = between(own, [(0, 2), (2, 0), (1, 3), (3, 1)])
+    one = between(own, [(0, 1), (1, 0), (2, 3), (3, 2)])
+    middle = between(own, [(1, 2), (2, 1)])
+    ends = between(two, [(2, 3), (1, 0)])
+    return [
+        (one, lambda b: jnp.bitwise_xor(b, 1)),
+        (two, lambda b: jnp.bitwise_xor(b, 2)),
+        (middle, lambda b: jnp.where((b == 1) | (b == 2), 3 - b, -1)),
+        (ends, lambda b: jnp.where((b == 0) | (b == 3), 3 - b, -1)),
+    ]
+
+
+def gather_row(own, blocks):
+    pieces = []
+    left = right = own
+    for distance in range(1, blocks):
+        left, right = shift(left, 1, distance - 1), shift(right, -1, distance - 1)
+        pieces.append((left, lambda b, d=distance: b - d))
+        pieces.append((right, lambda b, d=distance: b + d))
+    return pieces
 
 
 def lay_kernel(*refs):
@@ -132,64 +159,63 @@
     return found
 
 
-def q_tile(tokens):
-    return min(tokens, 256)
-
-
-def absorb(qm, top, acc, keys, vals, first_key, lo, span, tile, at):
+def absorb(qm, top, acc, keys, vals, first_key, lo, span, at, tile):
     count = keys.shape[0]
     cols = slice(at, at + tile)
-    number = first_key + lax.broadcasted_iota(jnp.int32, (count, tile), 0)
-    gap = number - lo
-    allowed = (gap >= 0) & (gap <= span)
+    heads = range(MINE)
     turned = jnp.transpose(vals)
     ones = jnp.ones((ROWS - HEAD, count), BF16)
-    for h in range(MINE):
-        pair = slice(128 * (h // 2), 128 * (h // 2) + 128)
-        score = jnp.dot(keys[:, pair], qm[h, :, cols], preferred_element_type=F32)
-        score = jnp.where(allowed, score, NEVER)
-        old = top[h:h + 1, cols]
-        new = jnp.maximum(old, jnp.max(score, axis=0, keepdims=True))
-        weight = jnp.exp2((score - new) * SCALE).astype(BF16)
-        factor = jnp.exp2((old - new) * SCALE)
-        value = jnp.concatenate([turned[h * HEAD:(h + 1) * HEAD], ones], axis=0)
-        added = jnp.dot(value, weight, preferred_element_type=F32)
-        acc[h, :, cols] = acc[h, :, cols] * factor + added
-        top[h:h + 1, cols] = new
-
-
-def over_suffix(lens, qm, top, acc, keys, vals, first_key, first_query):
+    score = [
+        jnp.dot(keys[:, 128 * (h // 2):128 * (h // 2) + 128], qm[h, :, cols], preferred_element_type=F32)
+        for h in heads
+    ]
+    number = first_key + lax.broadcasted_iota(jnp.int32, (count, tile), 0)
+    allowed = number >= lo
+    if span is not None:
+        allowed = allowed & (number - lo <= span)
+    score = [jnp.where(allowed, s, NEVER) for s in score]
+    old = [top[h:h + 1, cols] for h in heads]
+    new = [jnp.maximum(o, jnp.max(s, axis=0, keepdims=True)) for o, s in zip(old, score)]
+    weight = [jnp.exp2((s - n) * SCALE).astype(BF16) for s, n in zip(score, new)]
+    factor = [jnp.exp2((o - n) * SCALE) for o, n in zip(old, new)]
+    value = [jnp.concatenate([turned[h * HEAD:(h + 1) * HEAD], ones], axis=0) for h in heads]
+    added = [jnp.dot(v, w, preferred_element_type=F32) for v, w in zip(value, weight)]
+    held = [acc[h, :, cols] for h in heads]
+    for h in heads:
+        acc[h, :, cols] = held[h] * factor[h] + added[h]
+    for h in heads:
+        top[h:h + 1, cols] = new[h]
+
+
+def over_suffix(lens, qm, top, acc, keys, vals, first_key, first_query, causal):
     tokens = qm.shape[2]
-    tile = q_tile(tokens)
     rows = keys.shape[0]
     piece = min(rows, 256)
-    for at in range(0, tokens, tile):
-        query = first_query + at
-        token = query + lax.broadcasted_iota(jnp.int32, (1, tile), 1)
-        lo = jnp.maximum(request_rows(lens, token), token - (WIN - 1))
-        least = jnp.maximum(request_start(lens, query), query - (WIN - 1))
-        for k in range(0, rows, piece):
-            key = first_key + k
-
-            @pl.when((key + piece > least) & (key < query + tile))
+    for k in range(0, rows, piece):
+        key = first_key + k
+        spots = [(k, tokens - k)] if causal else [(at, piece) for at in range(0, tokens, piece)]
+        for at, tile in spots:
+            query = first_query + at
+            least = jnp.maximum(request_start(lens, query), query - (WIN - 1))
+
+            @pl.when(key + piece > least)
             def _():
-                absorb(qm, top, acc, keys[k:k + piece], vals[k:k + piece], key, lo, token - lo, tile, at)
+                token = query + lax.broadcasted_iota(jnp.int32, (1, tile), 1)
+                lo = jnp.maximum(request_rows(lens, token), token - (WIN - 1))
+                absorb(qm, top, acc, keys[k:k + piece], vals[k:k + piece], key, lo, token - lo, at, tile)
 
 
 def over_prefix(lens, qm, top, acc, keys, vals, first_key, valid, first_query):
     tokens = qm.shape[2]
-    tile = q_tile(tokens)
     rows = keys.shape[0]
-    for at in range(0, tokens, tile):
-        query = first_query + at
-        token = query + lax.broadcasted_iota(jnp.int32, (1, tile), 1)
+    start, last = request_start(lens, first_query), request_start(lens, first_query + tokens - 1)
+    least = jnp.where(start == last, first_query - start, 0)
+
+    @pl.when(valid & (first_key + rows - 1 > least))
+    def _():
+        token = first_query + lax.broadcasted_iota(jnp.int32, (1, tokens), 1)
         off = token - request_rows(lens, token)
-        start, last = request_start(lens, query), request_start(lens, query + tile - 1)
-        least = jnp.where(start == last, query - start, 0)
-
-        @pl.when(valid & (first_key + rows - 1 > least))
-        def _():
-            absorb(qm, top, acc, keys[...], vals[...], first_key, off + 1, jnp.full_like(off, WIN), tile, at)
+        absorb(qm, top, acc, keys[...], vals[...], first_key, off + 1, None, 0, tokens)
 
 
 def own_kernel(lens, s0, s1, s2, s3, own, qm, top, acc, held):
@@ -208,7 +234,7 @@
     top[...] = jnp.full(top.shape, LOW, F32)
     acc[...] = jnp.zeros(acc.shape, F32)
     first = block * tokens
-    over_suffix(lens, qm, top, acc, held.at[1], held.at[2], first, first)
+    over_suffix(lens, qm, top, acc, held.at[1], held.at[2], first, first, True)
     over_prefix(lens, qm, top, acc, own.at[0], own.at[1], block * own.shape[1], True, first)
 
 
@@ -232,19 +258,21 @@
     )(lengths, *slabs, own)
 
 
-def hop_step(distance, lens, qm, top, acc, left, right):
+def pieces_step(sources, lens, qm, top, acc, refs):
     block, _ = place()
     blocks = lax.axis_size("req") // SUB
     first = block * qm.shape[2]
-    for ref, source in ((left, block - distance), (right, block + distance)):
-        valid = (source >= 0) & (source < blocks)
-        over_prefix(lens, qm, top, acc, ref.at[0], ref.at[1], source * ref.shape[1], valid, first)
-
-
-def hop_kernel(distance, lens, qm, top_in, acc_in, left, right, top, acc):
+    for ref, source in zip(refs, sources):
+        number = source(block)
+        valid = (number >= 0) & (number < blocks)
+        over_prefix(lens, qm, top, acc, ref.at[0], ref.at[1], number * ref.shape[1], valid, first)
+
+
+def pieces_kernel(sources, lens, qm, top_in, acc_in, *refs):
+    *refs, top, acc = refs
     top[...] = top_in[...]
     acc[...] = acc_in[...]
-    hop_step(distance, lens, qm, top, acc, left, right)
+    pieces_step(sources, lens, qm, top, acc, refs)
 
 
 def halo_kernel(distance, lens, qm, top_in, acc_in, s0, s1, s2, s3, top, acc, held):
@@ -257,24 +285,20 @@
     top[...] = top_in[...]
     acc[...] = acc_in[...]
     tokens = qm.shape[2]
-    over_suffix(lens, qm, top, acc, held.at[0], held.at[1], (block - distance) * tokens, block * tokens)
-
-
-def last_kernel(distance, lens, qm, top_in, acc_in, left, right, o0, o1, o2, o3, top, acc):
+    over_suffix(lens, qm, top, acc, held.at[0], held.at[1], (block - distance) * tokens, block * tokens, False)
+
+
+def last_kernel(sources, lens, qm, top_in, acc_in, *refs):
+    *refs, o0, o1, o2, o3, top, acc, turned = refs
     _, sub = place()
     top[...] = top_in[...]
     acc[...] = acc_in[...]
-    if distance:
-        hop_step(distance, lens, qm, top, acc, left, right)
-    whole = jnp.concatenate([acc[h, :HEAD] / acc[h, HEAD:HEAD + 1] for h in range(MINE)], axis=0)
-    top_rows = jnp.transpose(whole.astype(BF16))
+    pieces_step(sources, lens, qm, top, acc, refs)
+    whole = jnp.concatenate([acc[h, :HEAD] * (1.0 / acc[h, HEAD:HEAD + 1]) for h in range(MINE)], axis=0)
+    turned[...] = jnp.transpose(whole.astype(BF16))
     rows = o0.shape[0]
-    for source in range(SUB):
-        for back, ref in enumerate((o0, o1, o2, o3)):
-
-            @pl.when(partner(sub, back) == source)
-            def _():
-                ref[...] = top_rows[source * rows:(source + 1) * rows]
+    for back, ref in enumerate((o0, o1, o2, o3)):
+        ref[...] = turned[pl.ds(pl.multiple_of(partner(sub, back) * rows, rows), rows)]
 
 
 def carry_call(kernel, name, lengths, qm, top, acc, pieces, scratch, keys):
@@ -291,20 +315,31 @@
     )(lengths, qm, top, acc, *pieces)
 
 
-def finish(distance, lengths, qm, top, acc, left, right):
+def prefix_call(lengths, qm, top, acc, pieces):
+    return carry_call(
+        functools.partial(pieces_kernel, [p[1] for p in pieces]), "prefix", lengths, qm, top, acc,
+        [p[0] for p in pieces], [], sum(p[0].shape[1] for p in pieces),
+    )
+
+
+def finish(lengths, qm, top, acc, pieces):
     tokens = qm.shape[2]
     rows = tokens // SUB
-    scores = tokens * left.shape[1] * MINE
-    return pl.pallas_call(
-        functools.partial(last_kernel, distance),
+    scores = tokens * sum(p[0].shape[1] for p in pieces) * MINE
+    return pl.pallas_call(
+        functools.partial(last_kernel, [p[1] for p in pieces]),
         out_shape=[jax.ShapeDtypeStruct((rows, WIDE), BF16)] * SUB,
-        in_specs=[pl.BlockSpec(memory_space=pltpu.SMEM)] + vmem(5),
+        in_specs=[pl.BlockSpec(memory_space=pltpu.SMEM)] + vmem(3 + len(pieces)),
         out_specs=vmem(SUB),
-        scratch_shapes=[pltpu.VMEM(top.shape, F32), pltpu.VMEM(acc.shape, F32)],
+        scratch_shapes=[
+            pltpu.VMEM(top.shape, F32),
+            pltpu.VMEM(acc.shape, F32),
+            pltpu.VMEM((tokens, WIDE), BF16),
+        ],
         compiler_params=params(),
         cost_estimate=cost(4 * HEAD * scores, 3 << 20, scores),
         name="last",
-    )(lengths, qm, top, acc, left, right)
+    )(lengths, qm, top, acc, *[p[0] for p in pieces])
 
 
 def join_kernel(s0, s1, s2, s3, out):
@@ -338,25 +373,17 @@
     raw = [shift(suffix_kv, d) for d in range(1, reach + 1)]
     own = lay(exchange(cut(prefix_kv)))
     slabs = exchange(cut(queries[:, None], suffix_kv))
-    left = right = own
-    hops = []
-    for distance in range(1, blocks):
-        left, right = shift(left, 1), shift(right, -1)
-        hops.append((left, right))
+    pieces = gather_four(own) if blocks == 4 else gather_row(own, blocks)
     qm, top, acc = begin(lengths, slabs, own)
-    for distance in range(1, reach + 1):
-        pieces = exchange(cut(raw[distance - 1]))
-        held = pltpu.VMEM((2, tokens, WIDE), BF16)
+    held = pltpu.VMEM((2, tokens, WIDE), BF16)
+    early = pieces[:len(pieces) // 2]
+    top, acc = prefix_call(lengths, qm, top, acc, early)
+    for back in range(1, reach + 1):
+        halo = exchange(cut(raw[back - 1]))
         top, acc = carry_call(
-            functools.partial(halo_kernel, distance), "halo", lengths, qm, top, acc, pieces, [held], tokens
+            functools.partial(halo_kernel, back), "halo", lengths, qm, top, acc, halo, [held], tokens
         )
-    for distance in range(1, blocks - 1):
-        top, acc = carry_call(
-            functools.partial(hop_kernel, distance), "hop", lengths, qm, top, acc, hops[distance - 1], [],
-            2 * own.shape[1],
-        )
-    left, right = hops[-1] if hops else (own, own)
-    mixed = finish(blocks - 1, lengths, qm, top, acc, left, right)
+    mixed = finish(lengths, qm, top, acc, pieces[len(early):])
     return join(exchange(mixed))
 
 

time: 67 us -> 51.5 us (0.77)
  Pallas kernels: 20.5 us -> 10.9 us
  starting transfers between devices: 32 us -> 23.5 us
  local copies, waits for them, and re-layouts: 0.95 us -> 2.64 us
  waiting for transfers between devices: 13 us -> 14 us
    pallas_call x3 -> x2, Pallas kernels: 11.8 us -> 4.6 us  [carry_call(): pl.pallas_call(kernel, out_shape=[jax.ShapeDtypeStruct(a.shape, a.dtype)...]
    ppermute x7 -> x5, starting transfers between devices: 19.3 us -> 12.5 us  [between(): lax.ppermute(block, 'req', [(SUB * a + s, SUB * b + s) for a, b in routes...]
    pallas_call x1, Pallas kernels: 6.82 us -> 3.55 us  [begin(): pl.pallas_call(own_kernel, out_shape=[jax.ShapeDtypeStruct((MINE, 2 * HEA...]
    ppermute x7 -> x5, waiting for transfers between devices: 5.35 us -> 7.67 us  [between(): lax.ppermute(block, 'req', [(SUB * a + s, SUB * b + s) for a, b in routes...]
    ppermute x12, starting transfers between devices: 12.8 us -> 11 us  [exchange(): got.append(lax.ppermute(slabs[distance], 'req', route))]
    unnamed x8, local copies, waits for them, and re-layouts: 0.95 us -> 2.64 us
    ppermute x12, waiting for transfers between devices: 7.61 us -> 6.37 us  [exchange(): got.append(lax.ppermute(slabs[distance], 'req', route))]
    pallas_call x1, Pallas kernels: 0.88 us -> 1.79 us  [finish(): pl.pallas_call(functools.partial(last_kernel, [p[1] for p in pieces]), ou...]
  transfers between devices with their start and end apart: 19 -> 17, of which waited for: 7 -> 5; matrix products, arithmetic and copies ran while one was open for 0% -> 0% of each run, Pallas kernels for 28% -> 16%
where the time goes in v2:
time: 51.5 us; the launch traced here: 51.3 us
  starting transfers between devices  23.5 us (46%)
  waiting for transfers between devices  14 us (27%)
  Pallas kernels  10.9 us (21%)
  local copies, waits for them, and re-layouts  2.64 us (5%)
    ppermute x5, starting transfers between devices, between(): lax.ppermute(block, 'req', [(SUB * a + s, SUB * b + s) for a, b in routes...  12.5 us
    ppermute x12, starting transfers between devices, exchange(): got.append(lax.ppermute(slabs[distance], 'req', route))  11 us
    ppermute x5, waiting for transfers between devices, between(): lax.ppermute(block, 'req', [(SUB * a + s, SUB * b + s) for a, b in routes...  7.67 us
    ppermute x12, waiting for transfers between devices, exchange(): got.append(lax.ppermute(slabs[distance], 'req', route))  6.37 us
    pallas_call x2, Pallas kernels, carry_call(): pl.pallas_call(kernel, out_shape=[jax.ShapeDtypeStruct(a.shape, a.dtype)...  4.6 us
    pallas_call x1, Pallas kernels, begin(): pl.pallas_call(own_kernel, out_shape=[jax.ShapeDtypeStruct((MINE, 2 * HEA...  3.55 us
    unnamed x8, local copies, waits for them, and re-layouts  2.64 us
    pallas_call x1, Pallas kernels, finish(): pl.pallas_call(functools.partial(last_kernel, [p[1] for p in pieces]), ou...  1.79 us
  transfers between devices with their start and end apart: 17, of which 5 were waited for; matrix products, arithmetic and copies ran while one was open for 0% of the time, Pallas kernels for 16%

profile of v2, /device:TPU:17, one launch (start us, length us, event | category | flops | bytes accessed | tf_op | source)
XLA Modules:
  0.0 51.3 jit_solution(15338605509329099874)
XLA Ops:
  0.0 0.0 copy-start.1
  0.0 3.3 %collective-permute-start.8 = (bf16[1,2,128,1024]{3,2,1,0:T(8,128)(2,1)}, bf16[1,2,128,1024]{3,2,1,0:T(8,128)(2,1)S(1)}, u32[]{:S(2)}, u32[]{:S(2)}) collective-permute-start(bf16[1,2,128,1024]{3,2,1,0:T(8,128)(2,1)} %refs_1_.1), channel_id=1, source_target_pairs={{0,4},{1,5},{2,6},{3,7},{4,8},{5,9},{6,10},{7,11},{8,12},{9,13},{1... | collective-permute-start | bytes 1572872 | tf_op jit(solution)/shard_map/ppermute | solution.py:89
  3.3 0.0 copy-start.2
  3.3 0.9 %copy-done.2 = bf16[1,2,64,1024]{3,2,1,0:T(8,128)(2,1)S(1)} copy-done((bf16[1,2,64,1024]{3,2,1,0:T(8,128)(2,1)S(1)}, bf16[1,2,64,1024]{3,2,1,0:T(8,128)(2,1)}, u32[]{:S(2)}) %copy-start.2) | copy-done | bytes 262168
  4.3 1.0 %collective-permute-start.3 = (bf16[2,64,256]{2,1,0:T(8,128)(2,1)S(1)}, bf16[2,64,256]{2,1,0:T(8,128)(2,1)S(1)}, u32[]{:S(2)}, u32[]{:S(2)}) collective-permute-start(bf16[2,64,256]{2,1,0:T(8,128)(2,1)S(1)} %get-tuple-element.33), channel_id=1, source_target_pairs={{0,1},{1,0},{2,3},{3,2},{4,5},{5,4},{6,7},{7,6},{8,9},{9,8},{10,11... | collective-permute-start | bytes 196616 | tf_op jit(solution)/shard_map/ppermute | solution.py:84
  5.3 1.3 %collective-permute-start.4 = (bf16[2,64,256]{2,1,0:T(8,128)(2,1)S(1)}, bf16[2,64,256]{2,1,0:T(8,128)(2,1)S(1)}, u32[]{:S(2)}, u32[]{:S(2)}) collective-permute-start(bf16[2,64,256]{2,1,0:T(8,128)(2,1)S(1)} %get-tuple-element.34), channel_id=1, source_target_pairs={{0,2},{1,3},{2,0},{3,1},{4,6},{5,7},{6,4},{7,5},{8,10},{9,11},{10,... | collective-permute-start | bytes 196616 | tf_op jit(solution)/shard_map/ppermute | solution.py:84
  6.6 0.5 collective-permute-start.5
  7.1 0.0 copy-done.1
  7.1 0.0 copy-start
  7.1 1.0 %copy-done = bf16[1,2,128,1024]{3,2,1,0:T(8,128)(2,1)S(1)} copy-done((bf16[1,2,128,1024]{3,2,1,0:T(8,128)(2,1)S(1)}, bf16[1,2,128,1024]{3,2,1,0:T(8,128)(2,1)}, u32[]{:S(2)}) %copy-start) | copy-done | bytes 524312
  8.1 0.1 cut.3
  8.2 0.2 collective-permute-start
  8.4 0.0 collective-permute-done.3.refs_1_
  8.4 0.6 %collective-permute-done.4.refs_2_ = bf16[2,64,256]{2,1,0:T(8,128)(2,1)S(1)} collective-permute-done((bf16[2,64,256]{2,1,0:T(8,128)(2,1)S(1)}, bf16[2,64,256]{2,1,0:T(8,128)(2,1)S(1)}, u32[]{:S(2)}, u32[]{:S(2)}) %collective-permute-start.4) | collective-permute-done | bytes 65568 | tf_op jit(solution)/shard_map/ppermute | solution.py:84
  9.0 1.9 %collective-permute-done.5.refs_3_ = bf16[2,64,256]{2,1,0:T(8,128)(2,1)S(1)} collective-permute-done((bf16[2,64,256]{2,1,0:T(8,128)(2,1)S(1)}, bf16[2,64,256]{2,1,0:T(8,128)(2,1)S(1)}, u32[]{:S(2)}, u32[]{:S(2)}) %collective-permute-start.5) | collective-permute-done | bytes 65568 | tf_op jit(solution)/shard_map/ppermute | solution.py:84
  11.0 0.1 collective-permute-start.7
  11.1 1.3 %collective-permute-start.6 = (bf16[2,256,256]{2,1,0:T(8,128)(2,1)S(1)}, bf16[2,256,256]{2,1,0:T(8,128)(2,1)S(1)}, u32[]{:S(2)}, u32[]{:S(2)}) collective-permute-start(bf16[2,256,256]{2,1,0:T(8,128)(2,1)S(1)} %lay.1.own), channel_id=1, source_target_pairs={{0,4},{1,5},{2,6},{3,7},{4,0},{5,1},{6,2},{7,3},{8,12},{9,13},{10,... | collective-permute-start | bytes 786440 | tf_op jit(solution)/shard_map/ppermute | solution.py:89
  12.4 1.2 %collective-permute-start.1 = (bf16[3,128,256]{2,1,0:T(8,128)(2,1)S(1)}, bf16[3,128,256]{2,1,0:T(8,128)(2,1)S(1)}, u32[]{:S(2)}, u32[]{:S(2)}) collective-permute-start(bf16[3,128,256]{2,1,0:T(8,128)(2,1)S(1)} %get-tuple-element.30), channel_id=1, source_target_pairs={{0,2},{1,3},{2,0},{3,1},{4,6},{5,7},{6,4},{7,5},{8,10},{9,11},{10,... | collective-permute-start | bytes 589832 | tf_op jit(solution)/shard_map/ppermute | solution.py:84
  13.6 0.0 collective-permute-done.s1
  13.6 1.1 %collective-permute-start.2 = (bf16[3,128,256]{2,1,0:T(8,128)(2,1)S(1)}, bf16[3,128,256]{2,1,0:T(8,128)(2,1)S(1)}, u32[]{:S(2)}, u32[]{:S(2)}) collective-permute-start(bf16[3,128,256]{2,1,0:T(8,128)(2,1)S(1)} %get-tuple-element.31), channel_id=1, source_target_pairs={{0,3},{1,2},{2,1},{3,0},{4,7},{5,6},{6,5},{7,4},{8,11},{9,10},{10,... | collective-permute-start | bytes 589832 | tf_op jit(solution)/shard_map/ppermute | solution.py:84
  14.6 7.7 %collective-permute-done.7.refs_1_ = bf16[2,256,256]{2,1,0:T(8,128)(2,1)S(1)} collective-permute-done((bf16[2,256,256]{2,1,0:T(8,128)(2,1)S(1)}, bf16[2,256,256]{2,1,0:T(8,128)(2,1)S(1)}, u32[]{:S(2)}, u32[]{:S(2)}) %collective-permute-start.7) | collective-permute-done | bytes 262176 | tf_op jit(solution)/shard_map/ppermute | solution.py:89
  22.3 5.2 %collective-permute-start.12 = (bf16[2,256,256]{2,1,0:T(8,128)(2,1)S(1)}, bf16[2,256,256]{2,1,0:T(8,128)(2,1)S(1)}, u32[]{:S(2)}, u32[]{:S(2)}) collective-permute-start(bf16[2,256,256]{2,1,0:T(8,128)(2,1)S(1)} %lay.1.own), channel_id=1, source_target_pairs={{4,8},{5,9},{6,10},{7,11},{8,4},{9,5},{10,6},{11,7},{20,24},{21,25... | collective-permute-start | bytes 786440 | tf_op jit(solution)/shard_map/ppermute | solution.py:89
  27.5 0.0 collective-permute-done.8.refs_0_
  27.5 2.6 %collective-permute-start.13 = (bf16[2,256,256]{2,1,0:T(8,128)(2,1)S(1)}, bf16[2,256,256]{2,1,0:T(8,128)(2,1)S(1)}, u32[]{:S(2)}, u32[]{:S(2)}) collective-permute-start(bf16[2,256,256]{2,1,0:T(8,128)(2,1)S(1)} %collective-permute-done.7.refs_1_), channel_id=1, source_target_pairs={{8,12},{9,13},{10,14},{11,15},{4,0},{5,1},{6,2},{7,3},{24,28},{25,... | collective-permute-start | bytes 786440 | tf_op jit(solution)/shard_map/ppermute | solution.py:89
  30.1 0.1 cut.5
  30.2 0.0 collective-permute-done.1.s2
  30.2 1.3 %collective-permute-start.10 = (bf16[2,128,256]{2,1,0:T(8,128)(2,1)S(1)}, bf16[2,128,256]{2,1,0:T(8,128)(2,1)S(1)}, u32[]{:S(2)}, u32[]{:S(2)}) collective-permute-start(bf16[2,128,256]{2,1,0:T(8,128)(2,1)S(1)} %get-tuple-element.43), channel_id=1, source_target_pairs={{0,2},{1,3},{2,0},{3,1},{4,6},{5,7},{6,4},{7,5},{8,10},{9,11},{10,... | collective-permute-start | bytes 393224 | tf_op jit(solution)/shard_map/ppermute | solution.py:84
  31.5 0.0 collective-permute-done.2.s3
  31.5 2.3 %collective-permute-start.11 = (bf16[2,128,256]{2,1,0:T(8,128)(2,1)S(1)}, bf16[2,128,256]{2,1,0:T(8,128)(2,1)S(1)}, u32[]{:S(2)}, u32[]{:S(2)}) collective-permute-start(bf16[2,128,256]{2,1,0:T(8,128)(2,1)S(1)} %get-tuple-element.44), channel_id=1, source_target_pairs={{0,3},{1,2},{2,1},{3,0},{4,7},{5,6},{6,5},{7,4},{8,11},{9,10},{10,... | collective-permute-start | bytes 393224 | tf_op jit(solution)/shard_map/ppermute | solution.py:84
  33.8 0.0 collective-permute-done.6.refs_0_
  33.8 0.0 copy-start.3
  33.8 0.0 collective-permute-start.9
  33.8 0.6 %copy-done.3 = s32[1,12]{1,0:T(1,128)S(1)} copy-done((s32[1,12]{1,0:T(1,128)S(1)}, s32[1,12]{1,0:T(1,128)}, u32[]{:S(2)}) %copy-start.3) | copy-done | bytes 72
  34.4 3.6 %own.1 = (bf16[4,128,512]{2,1,0:T(8,128)(2,1)S(1)}, f32[8,512]{1,0:T(8,128)S(1)}, f32[4,80,512]{2,1,0:T(8,128)S(1)}) custom-call(s32[1,12]{1,0:T(1,128)S(1)} %copy-done.3, bf16[3,128,256]{2,1,0:T(8,128)(2,1)S(1)} %get-tuple-element.28.s0, bf16[3,128,256]{2,1,0:T(8,128)(2,1)S(1)} %collective-permute-done.s1, ...), custom_call_target="tpu_custom_call" | custom-call | flops 402653184 | bytes 4194304 | tf_op jit(solution)/shard_map/own/pallas_call | solution.py:245
  38.0 2.7 %prefix.1 = (f32[8,512]{1,0:T(8,128)S(1)}, f32[4,80,512]{2,1,0:T(8,128)S(1)}) custom-call(s32[1,12]{1,0:T(1,128)S(1)} %copy-done.3, bf16[4,128,512]{2,1,0:T(8,128)(2,1)S(1)} %get-tuple-element.36.qm, f32[8,512]{1,0:T(8,128)S(1)} %get-tuple-element.37.top_in, f32[4,80,512]{2,1,0:T(8,128)S(1)} %get-tuple-element.38.acc_in, ...), custom_call_target="tpu_custom_call" | custom-call | flops 268435456 | bytes 3145728 | tf_op jit(solution)/shard_map/prefix/pallas_call | solution.py:306
  40.7 0.0 collective-permute-done.10.s2
  40.7 0.0 collective-permute-done.11.s3
  40.7 0.0 collective-permute-done.9.s1
  40.7 1.9 %halo.1 = (f32[8,512]{1,0:T(8,128)S(1)}, f32[4,80,512]{2,1,0:T(8,128)S(1)}) custom-call(s32[1,12]{1,0:T(1,128)S(1)} %copy-done.3, bf16[4,128,512]{2,1,0:T(8,128)(2,1)S(1)} %get-tuple-element.36.qm, f32[8,512]{1,0:T(8,128)S(1)} %get-tuple-element.39.top_in, f32[4,80,512]{2,1,0:T(8,128)S(1)} %get-tuple-element.40.acc_in, ...), custom_call_target="tpu_custom_call" | custom-call | flops 268435456 | bytes 3145728 | tf_op jit(solution)/shard_map/halo/pallas_call | solution.py:306
  42.6 0.0 collective-permute-done.12.refs_0_
  42.7 0.0 collective-permute-done.13.refs_1_
  42.7 1.8 %last.1 = (bf16[128,256]{1,0:T(8,128)(2,1)S(1)}, bf16[128,256]{1,0:T(8,128)(2,1)S(1)}, bf16[128,256]{1,0:T(8,128)(2,1)S(1)}, bf16[128,256]{1,0:T(8,128)(2,1)S(1)}) custom-call(s32[1,12]{1,0:T(1,128)S(1)} %copy-done.3, bf16[4,128,512]{2,1,0:T(8,128)(2,1)S(1)} %get-tuple-element.36.qm, f32[8,512]{1,0:T(8,128)S(1)} %get-tuple-element.45.top_in, ...), custom_call_target="tpu_custom_call" | custom-call | flops 268435456 | bytes 3145728 | tf_op jit(solution)/shard_map/last/pallas_call | solution.py:329
  44.5 0.1 collective-permute-start.14
  44.5 1.3 %collective-permute-start.15 = (bf16[128,256]{1,0:T(8,128)(2,1)S(1)}, bf16[128,256]{1,0:T(8,128)(2,1)S(1)}, u32[]{:S(2)}, u32[]{:S(2)}) collective-permute-start(bf16[128,256]{1,0:T(8,128)(2,1)S(1)} %get-tuple-element.49), channel_id=1, source_target_pairs={{0,2},{1,3},{2,0},{3,1},{4,6},{5,7},{6,4},{7,5},{8,10},{9,11},{10,... | collective-permute-start | bytes 196616 | tf_op jit(solution)/shard_map/ppermute | solution.py:84
  45.9 0.8 %collective-permute-start.16 = (bf16[128,256]{1,0:T(8,128)(2,1)S(1)}, bf16[128,256]{1,0:T(8,128)(2,1)S(1)}, u32[]{:S(2)}, u32[]{:S(2)}) collective-permute-start(bf16[128,256]{1,0:T(8,128)(2,1)S(1)} %get-tuple-element.50), channel_id=1, source_target_pairs={{0,3},{1,2},{2,1},{3,0},{4,7},{5,6},{6,5},{7,4},{8,11},{9,10},{10,... | collective-permute-start | bytes 196616 | tf_op jit(solution)/shard_map/ppermute | solution.py:84
  46.7 0.0 collective-permute-done.14.s1
  46.7 1.0 %collective-permute-done.15.s2 = bf16[128,256]{1,0:T(8,128)(2,1)S(1)} collective-permute-done((bf16[128,256]{1,0:T(8,128)(2,1)S(1)}, bf16[128,256]{1,0:T(8,128)(2,1)S(1)}, u32[]{:S(2)}, u32[]{:S(2)}) %collective-permute-start.15) | collective-permute-done | bytes 65568 | tf_op jit(solution)/shard_map/ppermute | solution.py:84
  47.7 2.8 %collective-permute-done.16.s3 = bf16[128,256]{1,0:T(8,128)(2,1)S(1)} collective-permute-done((bf16[128,256]{1,0:T(8,128)(2,1)S(1)}, bf16[128,256]{1,0:T(8,128)(2,1)S(1)}, u32[]{:S(2)}, u32[]{:S(2)}) %collective-permute-start.16) | collective-permute-done | bytes 65568 | tf_op jit(solution)/shard_map/ppermute | solution.py:84
  50.5 0.7 %join.1 = bf16[1,128,1024]{2,1,0:T(8,128)(2,1)} custom-call(bf16[128,256]{1,0:T(8,128)(2,1)S(1)} %get-tuple-element.47.s0, bf16[128,256]{1,0:T(8,128)(2,1)S(1)} %collective-permute-done.14.s1, bf16[128,256]{1,0:T(8,128)(2,1)S(1)} %collective-permute-done.15.s2, bf16[128,256]{1,0:T(8,128)(2,1)S(1)} %collective-permute-done.16.s3), custom_call_target="tpu_custom_call" | custom-call | bytes 524288 | tf_op jit(solution)/shard_map/join/pallas_call | solution.py:353
  (2 shorter events, 0.1 us)
Async XLA Ops:
  0.0 7.1 %copy-start.1 = (bf16[1,128,1024]{2,1,0:T(8,128)(2,1)S(1)}, bf16[1,128,1024]{2,1,0:T(8,128)(2,1)}, u32[]{:S(2)}) copy-start(bf16[1,128,1024]{2,1,0:T(8,128)(2,1)} %param.4) | copy-start | bytes 786436
  0.0 27.5 %collective-permute-start.8 = (bf16[1,2,128,1024]{3,2,1,0:T(8,128)(2,1)}, bf16[1,2,128,1024]{3,2,1,0:T(8,128)(2,1)S(1)}, u32[]{:S(2)}, u32[]{:S(2)}) collective-permute-start(bf16[1,2,128,1024]{3,2,1,0:T(8,128)(2,1)} %refs_1_.1), channel_id=1, source_target_pairs={{0,4},{1,5},{2,6},{3,7},{4,8},{5,9},{6,10},{7,11},{8,12},{9,13},{1... | collective-permute-start | bytes 1572872 | tf_op jit(solution)/shard_map/ppermute | solution.py:89
  3.3 1.0 %copy-start.2 = (bf16[1,2,64,1024]{3,2,1,0:T(8,128)(2,1)S(1)}, bf16[1,2,64,1024]{3,2,1,0:T(8,128)(2,1)}, u32[]{:S(2)}) copy-start(bf16[1,2,64,1024]{3,2,1,0:T(8,128)(2,1)} %refs_0_.1) | copy-start | bytes 786436
  4.3 4.1 %collective-permute-start.3 = (bf16[2,64,256]{2,1,0:T(8,128)(2,1)S(1)}, bf16[2,64,256]{2,1,0:T(8,128)(2,1)S(1)}, u32[]{:S(2)}, u32[]{:S(2)}) collective-permute-start(bf16[2,64,256]{2,1,0:T(8,128)(2,1)S(1)} %get-tuple-element.33), channel_id=1, source_target_pairs={{0,1},{1,0},{2,3},{3,2},{4,5},{5,4},{6,7},{7,6},{8,9},{9,8},{10,11... | collective-permute-start | bytes 196616 | tf_op jit(solution)/shard_map/ppermute | solution.py:84
  5.3 3.7 %collective-permute-start.4 = (bf16[2,64,256]{2,1,0:T(8,128)(2,1)S(1)}, bf16[2,64,256]{2,1,0:T(8,128)(2,1)S(1)}, u32[]{:S(2)}, u32[]{:S(2)}) collective-permute-start(bf16[2,64,256]{2,1,0:T(8,128)(2,1)S(1)} %get-tuple-element.34), channel_id=1, source_target_pairs={{0,2},{1,3},{2,0},{3,1},{4,6},{5,7},{6,4},{7,5},{8,10},{9,11},{10,... | collective-permute-start | bytes 196616 | tf_op jit(solution)/shard_map/ppermute | solution.py:84
  6.6 4.3 %collective-permute-start.5 = (bf16[2,64,256]{2,1,0:T(8,128)(2,1)S(1)}, bf16[2,64,256]{2,1,0:T(8,128)(2,1)S(1)}, u32[]{:S(2)}, u32[]{:S(2)}) collective-permute-start(bf16[2,64,256]{2,1,0:T(8,128)(2,1)S(1)} %get-tuple-element.35), channel_id=1, source_target_pairs={{0,3},{1,2},{2,1},{3,0},{4,7},{5,6},{6,5},{7,4},{8,11},{9,10},{10,... | collective-permute-start | bytes 196616 | tf_op jit(solution)/shard_map/ppermute | solution.py:84
  7.1 1.0 %copy-start = (bf16[1,2,128,1024]{3,2,1,0:T(8,128)(2,1)S(1)}, bf16[1,2,128,1024]{3,2,1,0:T(8,128)(2,1)}, u32[]{:S(2)}) copy-start(bf16[1,2,128,1024]{3,2,1,0:T(8,128)(2,1)} %refs_1_.1) | copy-start | bytes 1572868
  8.2 5.4 %collective-permute-start = (bf16[3,128,256]{2,1,0:T(8,128)(2,1)S(1)}, bf16[3,128,256]{2,1,0:T(8,128)(2,1)S(1)}, u32[]{:S(2)}, u32[]{:S(2)}) collective-permute-start(bf16[3,128,256]{2,1,0:T(8,128)(2,1)S(1)} %get-tuple-element.29), channel_id=1, source_target_pairs={{0,1},{1,0},{2,3},{3,2},{4,5},{5,4},{6,7},{7,6},{8,9},{9,8},{10,11... | collective-permute-start | bytes 589832 | tf_op jit(solution)/shard_map/ppermute | solution.py:84
  11.0 11.3 %collective-permute-start.7 = (bf16[2,256,256]{2,1,0:T(8,128)(2,1)S(1)}, bf16[2,256,256]{2,1,0:T(8,128)(2,1)S(1)}, u32[]{:S(2)}, u32[]{:S(2)}) collective-permute-start(bf16[2,256,256]{2,1,0:T(8,128)(2,1)S(1)} %lay.1.own), channel_id=1, source_target_pairs={{0,8},{1,9},{2,10},{3,11},{8,0},{9,1},{10,2},{11,3},{4,12},{5,13},... | collective-permute-start | bytes 786440 | tf_op jit(solution)/shard_map/ppermute | solution.py:89
  11.1 22.7 %collective-permute-start.6 = (bf16[2,256,256]{2,1,0:T(8,128)(2,1)S(1)}, bf16[2,256,256]{2,1,0:T(8,128)(2,1)S(1)}, u32[]{:S(2)}, u32[]{:S(2)}) collective-permute-start(bf16[2,256,256]{2,1,0:T(8,128)(2,1)S(1)} %lay.1.own), channel_id=1, source_target_pairs={{0,4},{1,5},{2,6},{3,7},{4,0},{5,1},{6,2},{7,3},{8,12},{9,13},{10,... | collective-permute-start | bytes 786440 | tf_op jit(solution)/shard_map/ppermute | solution.py:89
  12.4 17.8 %collective-permute-start.1 = (bf16[3,128,256]{2,1,0:T(8,128)(2,1)S(1)}, bf16[3,128,256]{2,1,0:T(8,128)(2,1)S(1)}, u32[]{:S(2)}, u32[]{:S(2)}) collective-permute-start(bf16[3,128,256]{2,1,0:T(8,128)(2,1)S(1)} %get-tuple-element.30), channel_id=1, source_target_pairs={{0,2},{1,3},{2,0},{3,1},{4,6},{5,7},{6,4},{7,5},{8,10},{9,11},{10,... | collective-permute-start | bytes 589832 | tf_op jit(solution)/shard_map/ppermute | solution.py:84
  13.6 17.9 %collective-permute-start.2 = (bf16[3,128,256]{2,1,0:T(8,128)(2,1)S(1)}, bf16[3,128,256]{2,1,0:T(8,128)(2,1)S(1)}, u32[]{:S(2)}, u32[]{:S(2)}) collective-permute-start(bf16[3,128,256]{2,1,0:T(8,128)(2,1)S(1)} %get-tuple-element.31), channel_id=1, source_target_pairs={{0,3},{1,2},{2,1},{3,0},{4,7},{5,6},{6,5},{7,4},{8,11},{9,10},{10,... | collective-permute-start | bytes 589832 | tf_op jit(solution)/shard_map/ppermute | solution.py:84
  22.3 20.3 %collective-permute-start.12 = (bf16[2,256,256]{2,1,0:T(8,128)(2,1)S(1)}, bf16[2,256,256]{2,1,0:T(8,128)(2,1)S(1)}, u32[]{:S(2)}, u32[]{:S(2)}) collective-permute-start(bf16[2,256,256]{2,1,0:T(8,128)(2,1)S(1)} %lay.1.own), channel_id=1, source_target_pairs={{4,8},{5,9},{6,10},{7,11},{8,4},{9,5},{10,6},{11,7},{20,24},{21,25... | collective-permute-start | bytes 786440 | tf_op jit(solution)/shard_map/ppermute | solution.py:89
  27.5 15.2 %collective-permute-start.13 = (bf16[2,256,256]{2,1,0:T(8,128)(2,1)S(1)}, bf16[2,256,256]{2,1,0:T(8,128)(2,1)S(1)}, u32[]{:S(2)}, u32[]{:S(2)}) collective-permute-start(bf16[2,256,256]{2,1,0:T(8,128)(2,1)S(1)} %collective-permute-done.7.refs_1_), channel_id=1, source_target_pairs={{8,12},{9,13},{10,14},{11,15},{4,0},{5,1},{6,2},{7,3},{24,28},{25,... | collective-permute-start | bytes 786440 | tf_op jit(solution)/shard_map/ppermute | solution.py:89
  30.2 10.5 %collective-permute-start.10 = (bf16[2,128,256]{2,1,0:T(8,128)(2,1)S(1)}, bf16[2,128,256]{2,1,0:T(8,128)(2,1)S(1)}, u32[]{:S(2)}, u32[]{:S(2)}) collective-permute-start(bf16[2,128,256]{2,1,0:T(8,128)(2,1)S(1)} %get-tuple-element.43), channel_id=1, source_target_pairs={{0,2},{1,3},{2,0},{3,1},{4,6},{5,7},{6,4},{7,5},{8,10},{9,11},{10,... | collective-permute-start | bytes 393224 | tf_op jit(solution)/shard_map/ppermute | solution.py:84
  31.5 9.2 %collective-permute-start.11 = (bf16[2,128,256]{2,1,0:T(8,128)(2,1)S(1)}, bf16[2,128,256]{2,1,0:T(8,128)(2,1)S(1)}, u32[]{:S(2)}, u32[]{:S(2)}) collective-permute-start(bf16[2,128,256]{2,1,0:T(8,128)(2,1)S(1)} %get-tuple-element.44), channel_id=1, source_target_pairs={{0,3},{1,2},{2,1},{3,0},{4,7},{5,6},{6,5},{7,4},{8,11},{9,10},{10,... | collective-permute-start | bytes 393224 | tf_op jit(solution)/shard_map/ppermute | solution.py:84
  33.8 0.7 %copy-start.3 = (s32[1,12]{1,0:T(1,128)S(1)}, s32[1,12]{1,0:T(1,128)}, u32[]{:S(2)}) copy-start(s32[1,12]{1,0:T(1,128)} %lens.7) | copy-start | bytes 148
  33.8 6.9 %collective-permute-start.9 = (bf16[2,128,256]{2,1,0:T(8,128)(2,1)S(1)}, bf16[2,128,256]{2,1,0:T(8,128)(2,1)S(1)}, u32[]{:S(2)}, u32[]{:S(2)}) collective-permute-start(bf16[2,128,256]{2,1,0:T(8,128)(2,1)S(1)} %get-tuple-element.42), channel_id=1, source_target_pairs={{0,1},{1,0},{2,3},{3,2},{4,5},{5,4},{6,7},{7,6},{8,9},{9,8},{10,11... | collective-permute-start | bytes 393224 | tf_op jit(solution)/shard_map/ppermute | solution.py:84
  44.5 2.2 %collective-permute-start.14 = (bf16[128,256]{1,0:T(8,128)(2,1)S(1)}, bf16[128,256]{1,0:T(8,128)(2,1)S(1)}, u32[]{:S(2)}, u32[]{:S(2)}) collective-permute-start(bf16[128,256]{1,0:T(8,128)(2,1)S(1)} %get-tuple-element.48), channel_id=1, source_target_pairs={{0,1},{1,0},{2,3},{3,2},{4,5},{5,4},{6,7},{7,6},{8,9},{9,8},{10,11... | collective-permute-start | bytes 196616 | tf_op jit(solution)/shard_map/ppermute | solution.py:84
  44.5 3.2 %collective-permute-start.15 = (bf16[128,256]{1,0:T(8,128)(2,1)S(1)}, bf16[128,256]{1,0:T(8,128)(2,1)S(1)}, u32[]{:S(2)}, u32[]{:S(2)}) collective-permute-start(bf16[128,256]{1,0:T(8,128)(2,1)S(1)} %get-tuple-element.49), channel_id=1, source_target_pairs={{0,2},{1,3},{2,0},{3,1},{4,6},{5,7},{6,4},{7,5},{8,10},{9,11},{10,... | collective-permute-start | bytes 196616 | tf_op jit(solution)/shard_map/ppermute | solution.py:84
  45.9 4.7 %collective-permute-start.16 = (bf16[128,256]{1,0:T(8,128)(2,1)S(1)}, bf16[128,256]{1,0:T(8,128)(2,1)S(1)}, u32[]{:S(2)}, u32[]{:S(2)}) collective-permute-start(bf16[128,256]{1,0:T(8,128)(2,1)S(1)} %get-tuple-element.50), channel_id=1, source_target_pairs={{0,3},{1,2},{2,1},{3,0},{4,7},{5,6},{6,5},{7,4},{8,11},{9,10},{10,... | collective-permute-start | bytes 196616 | tf_op jit(solution)/shard_map/ppermute | solution.py:84

commit v3 on v2

--- a/solution.py
+++ b/solution.py
@@ -48,30 +48,28 @@
     return pl.CostEstimate(flops=flops, bytes_accessed=moved, transcendentals=exps)
 
 
-def cut_kernel(parts, *refs):
-    ins, outs = refs[:len(parts)], refs[len(parts):]
+def cut_kernel(*refs):
+    ins, outs = refs[:-SUB], refs[-SUB:]
     _, sub = place()
-    for distance in range(SUB):
+    for distance, out in enumerate(outs):
         cols = columns(partner(sub, distance))
         at = 0
-        for ref, count in zip(ins, parts):
-            for part in range(count):
-                outs[distance][at] = ref[0, part, :, cols]
-                at += 1
+        for ref in ins:
+            rows = ref.shape[2]
+            for part in range(ref.shape[1]):
+                out[at:at + rows] = ref[0, part, :, cols]
+                at += rows
 
 
 def cut(*arrays):
-    parts = [a.shape[1] for a in arrays]
-    rows = arrays[0].shape[2]
-    slab = jax.ShapeDtypeStruct((sum(parts), rows, WIDE), BF16)
-    moved = 2 * sum(a.size * 2 for a in arrays)
-    return pl.pallas_call(
-        functools.partial(cut_kernel, parts),
-        out_shape=[slab] * SUB,
+    rows = sum(a.shape[1] * a.shape[2] for a in arrays)
+    return pl.pallas_call(
+        cut_kernel,
+        out_shape=[jax.ShapeDtypeStruct((rows, WIDE), BF16)] * SUB,
         in_specs=vmem(len(arrays)),
         out_specs=vmem(SUB),
         compiler_params=params(),
-        cost_estimate=cost(0, moved),
+        cost_estimate=cost(0, 4 * SUB * rows * WIDE),
         name="cut",
     )(*arrays)
 
@@ -99,13 +97,16 @@
     two = between(own, [(0, 2), (2, 0), (1, 3), (3, 1)])
     one = between(own, [(0, 1), (1, 0), (2, 3), (3, 2)])
     middle = between(own, [(1, 2), (2, 1)])
-    ends = between(two, [(2, 3), (1, 0)])
     return [
         (one, lambda b: jnp.bitwise_xor(b, 1)),
+        (middle, lambda b: jnp.where((b == 1) | (b == 2), 3 - b, -1)),
         (two, lambda b: jnp.bitwise_xor(b, 2)),
-        (middle, lambda b: jnp.where((b == 1) | (b == 2), 3 - b, -1)),
-        (ends, lambda b: jnp.where((b == 0) | (b == 3), 3 - b, -1)),
     ]
+
+
+def pass_on(two):
+    ends = between(two, [(2, 3), (1, 0)])
+    return ends, lambda b: jnp.where((b == 0) | (b == 3), 3 - b, -1)
 
 
 def gather_row(own, blocks):
@@ -118,25 +119,74 @@
     return pieces
 
 
+def in_order(slabs, first, rows, out):
+    _, sub = place()
+    for distance, ref in enumerate(slabs):
+        at = pl.ds(pl.multiple_of(partner(sub, distance) * rows, rows), rows)
+        out[at, :] = ref[first:first + rows]
+
+
+def deal_kernel(*refs):
+    ins, (own, near, far) = refs[:-3], refs[-3:]
+    _, sub = place()
+    half = own.shape[0]
+    for distance, (out, at) in enumerate(((own, 0), (near, 0), (far, 0), (near, half))):
+        cols = columns(partner(sub, distance))
+        for ref in ins:
+            rows = ref.shape[2]
+            for part in range(ref.shape[1]):
+                out[at:at + rows] = ref[0, part, :, cols]
+                at += rows
+
+
+def pair_kernel(far, near, out):
+    rows = far.shape[0]
+    out[:rows] = far[...]
+    out[rows:] = near[rows:]
+
+
+def trade(*arrays):
+    rows = sum(a.shape[1] * a.shape[2] for a in arrays)
+    slab = jax.ShapeDtypeStruct((rows, WIDE), BF16)
+    slabs = jax.ShapeDtypeStruct((2 * rows, WIDE), BF16)
+    own, near, far = pl.pallas_call(
+        deal_kernel,
+        out_shape=[slab, slabs, slab],
+        in_specs=vmem(len(arrays)),
+        out_specs=vmem(3),
+        compiler_params=params(),
+        cost_estimate=cost(0, 4 * SUB * rows * WIDE),
+        name="deal",
+    )(*arrays)
+    count = lax.axis_size("req")
+    near = lax.ppermute(near, "req", [(i, i ^ 1) for i in range(count)])
+    far = pl.pallas_call(
+        pair_kernel,
+        out_shape=slabs,
+        in_specs=vmem(2),
+        out_specs=vmem(1)[0],
+        compiler_params=params(),
+        cost_estimate=cost(0, 8 * rows * WIDE),
+        name="pair",
+    )(far, near)
+    return own, near, lax.ppermute(far, "req", [(i, i ^ 2) for i in range(count)])
+
+
 def lay_kernel(*refs):
-    ins, out = refs[:-1], refs[-1]
-    _, sub = place()
-    rows = ins[0].shape[1]
-    for distance, ref in enumerate(ins):
-        at = pl.ds(pl.multiple_of(partner(sub, distance) * rows, rows), rows)
-        for part in range(ref.shape[0]):
-            out[part, at, :] = ref[part]
-
-
-def lay(slabs):
-    parts, rows, width = slabs[0].shape
+    *slabs, out = refs
+    rows = out.shape[1] // SUB
+    for part in range(2):
+        in_order(slabs, part * rows, rows, out.at[part])
+
+
+def lay(slabs, rows):
     return pl.pallas_call(
         lay_kernel,
-        out_shape=jax.ShapeDtypeStruct((parts, rows * SUB, width), BF16),
+        out_shape=jax.ShapeDtypeStruct((2, rows * SUB, WIDE), BF16),
         in_specs=vmem(SUB),
         out_specs=vmem(1)[0],
         compiler_params=params(),
-        cost_estimate=cost(0, 4 * SUB * parts * rows * width),
+        cost_estimate=cost(0, 8 * SUB * rows * WIDE),
         name="lay",
     )(*slabs)
 
@@ -218,32 +268,26 @@
         absorb(qm, top, acc, keys[...], vals[...], first_key, off + 1, None, 0, tokens)
 
 
-def own_kernel(lens, s0, s1, s2, s3, own, qm, top, acc, held):
-    block, sub = place()
-    rows = s0.shape[1]
-    tokens = rows * SUB
-    for distance, ref in enumerate((s0, s1, s2, s3)):
-        at = pl.ds(pl.multiple_of(partner(sub, distance) * rows, rows), rows)
-        for part in range(3):
-            held[part, at, :] = ref[part]
-    turned = jnp.transpose(held[0])
+def begin_kernel(lens, s0, s1, s2, s3, own, qm, top, acc, held):
+    block, _ = place()
+    tokens = held.shape[0]
+    rows = tokens // SUB
+    in_order((s0, s1, s2, s3), s0.shape[0] - rows, rows, held)
+    turned = jnp.transpose(held[...])
     for h in range(MINE):
         mine, other = HEAD * (h % 2), HEAD * (1 - h % 2)
         qm[h, mine:mine + HEAD, :] = turned[h * HEAD:(h + 1) * HEAD]
         qm[h, other:other + HEAD, :] = jnp.zeros((HEAD, tokens), BF16)
     top[...] = jnp.full(top.shape, LOW, F32)
     acc[...] = jnp.zeros(acc.shape, F32)
-    first = block * tokens
-    over_suffix(lens, qm, top, acc, held.at[1], held.at[2], first, first, True)
-    over_prefix(lens, qm, top, acc, own.at[0], own.at[1], block * own.shape[1], True, first)
-
-
-def begin(lengths, slabs, own):
-    rows = slabs[0].shape[1]
+    over_prefix(lens, qm, top, acc, own.at[0], own.at[1], block * own.shape[1], True, block * tokens)
+
+
+def begin(lengths, slabs, own, rows):
     tokens = rows * SUB
-    scores = tokens * (tokens + own.shape[1]) * MINE
-    return pl.pallas_call(
-        own_kernel,
+    scores = tokens * own.shape[1] * MINE
+    return pl.pallas_call(
+        begin_kernel,
         out_shape=[
             jax.ShapeDtypeStruct((MINE, 2 * HEAD, tokens), BF16),
             jax.ShapeDtypeStruct((8, tokens), F32),
@@ -251,10 +295,10 @@
         ],
         in_specs=[pl.BlockSpec(memory_space=pltpu.SMEM)] + vmem(SUB + 1),
         out_specs=vmem(3),
-        scratch_shapes=[pltpu.VMEM((3, tokens, WIDE), BF16)],
+        scratch_shapes=[pltpu.VMEM((tokens, WIDE), BF16)],
         compiler_params=params(),
         cost_estimate=cost(4 * HEAD * scores, 4 << 20, scores),
-        name="own",
+        name="begin",
     )(lengths, *slabs, own)
 
 
@@ -275,17 +319,21 @@
     pieces_step(sources, lens, qm, top, acc, refs)
 
 
-def halo_kernel(distance, lens, qm, top_in, acc_in, s0, s1, s2, s3, top, acc, held):
-    block, sub = place()
-    rows = s0.shape[1]
-    for back, ref in enumerate((s0, s1, s2, s3)):
-        at = pl.ds(pl.multiple_of(partner(sub, back) * rows, rows), rows)
-        for part in range(2):
-            held[part, at, :] = ref[part]
+def suffix_kernel(distances, lens, qm, top_in, acc_in, *refs):
+    *slabs, top, acc, held = refs
+    block, _ = place()
+    tokens = qm.shape[2]
+    rows = tokens // SUB
     top[...] = top_in[...]
     acc[...] = acc_in[...]
-    tokens = qm.shape[2]
-    over_suffix(lens, qm, top, acc, held.at[0], held.at[1], (block - distance) * tokens, block * tokens, False)
+    if len(slabs) < SUB:
+        half = slabs[0].shape[0]
+        slabs = [*slabs, slabs[2].at[pl.ds(half, half)]]
+    for number, distance in enumerate(distances):
+        for part in range(2):
+            in_order(slabs, (2 * number + part) * rows, rows, held.at[part])
+        first = (block - distance) * tokens
+        over_suffix(lens, qm, top, acc, held.at[0], held.at[1], first, block * tokens, distance == 0)
 
 
 def last_kernel(sources, lens, qm, top_in, acc_in, *refs):
@@ -322,6 +370,14 @@
     )
 
 
+def suffix_call(distances, lengths, qm, top, acc, slabs):
+    tokens = qm.shape[2]
+    return carry_call(
+        functools.partial(suffix_kernel, distances), "suffix", lengths, qm, top, acc, slabs,
+        [pltpu.VMEM((2, tokens, WIDE), BF16)], tokens * len(distances),
+    )
+
+
 def finish(lengths, qm, top, acc, pieces):
     tokens = qm.shape[2]
     rows = tokens // SUB
@@ -371,19 +427,21 @@
     reach = min(reach, blocks - 1)
 
     raw = [shift(suffix_kv, d) for d in range(1, reach + 1)]
-    own = lay(exchange(cut(prefix_kv)))
-    slabs = exchange(cut(queries[:, None], suffix_kv))
+    slabs = exchange(cut(prefix_kv, queries[:, None]))
+    near = trade(suffix_kv)
+    own = lay(slabs, prefix_kv.shape[2])
     pieces = gather_four(own) if blocks == 4 else gather_row(own, blocks)
-    qm, top, acc = begin(lengths, slabs, own)
-    held = pltpu.VMEM((2, tokens, WIDE), BF16)
-    early = pieces[:len(pieces) // 2]
-    top, acc = prefix_call(lengths, qm, top, acc, early)
+    qm, top, acc = begin(lengths, slabs, own, rows)
+    top, acc = suffix_call([0], lengths, qm, top, acc, near)
     for back in range(1, reach + 1):
         halo = exchange(cut(raw[back - 1]))
-        top, acc = carry_call(
-            functools.partial(halo_kernel, back), "halo", lengths, qm, top, acc, halo, [held], tokens
-        )
-    mixed = finish(lengths, qm, top, acc, pieces[len(early):])
+        top, acc = suffix_call([back], lengths, qm, top, acc, halo)
+    if blocks == 4:
+        two, where = pieces[-1]
+        two, top = lax.optimization_barrier((two, top))
+        pieces = pieces[:-1] + [(two, where), pass_on(two)]
+    top, acc = prefix_call(lengths, qm, top, acc, pieces[:3])
+    mixed = finish(lengths, qm, top, acc, pieces[3:])
     return join(exchange(mixed))
 
 

time: 51.5 us -> 49.9 us (0.969)
  the two profiles are of different devices: /device:TPU:17 before, /device:TPU:0 now
where the time goes in v3:
time: 49.9 us; the launch traced here: 49.7 us
  waiting for transfers between devices  18.7 us (37%)
  starting transfers between devices  18.6 us (37%)
  Pallas kernels  10.3 us (21%)
  local copies, waits for them, and re-layouts  1.94 us (4%)
    ppermute x5, starting transfers between devices, between(): lax.ppermute(block, 'req', [(SUB * a + s, SUB * b + s) for a, b in routes...  10.8 us
    ppermute x5, waiting for transfers between devices, between(): lax.ppermute(block, 'req', [(SUB * a + s, SUB * b + s) for a, b in routes...  10.1 us
    ppermute x9, waiting for transfers between devices, exchange(): got.append(lax.ppermute(slabs[distance], 'req', route))  8.57 us
    ppermute x9, starting transfers between devices, exchange(): got.append(lax.ppermute(slabs[distance], 'req', route))  6.19 us
    pallas_call x3, Pallas kernels, carry_call(): pl.pallas_call(kernel, out_shape=[jax.ShapeDtypeStruct(a.shape, a.dtype)...  5.82 us
    unnamed x8, local copies, waits for them, and re-layouts  1.94 us
    pallas_call x1, Pallas kernels, finish(): pl.pallas_call(functools.partial(last_kernel, [p[1] for p in pieces]), ou...  1.79 us
    pallas_call x1, Pallas kernels, begin(): pl.pallas_call(begin_kernel, out_shape=[jax.ShapeDtypeStruct((MINE, 2 * H...  1.74 us
  transfers between devices with their start and end apart: 16, of which 7 were waited for; matrix products, arithmetic and copies ran while one was open for 0% of the time, Pallas kernels for 16%

profile of v3, /device:TPU:0, one launch (start us, length us, event | category | flops | bytes accessed | tf_op | source)
XLA Modules:
  0.0 49.7 jit_solution(8339949470320122155)
XLA Ops:
  0.0 4.9 %collective-permute-start.6 = (bf16[1,2,128,1024]{3,2,1,0:T(8,128)(2,1)}, bf16[1,2,128,1024]{3,2,1,0:T(8,128)(2,1)S(1)}, u32[]{:S(2)}, u32[]{:S(2)}) collective-permute-start(bf16[1,2,128,1024]{3,2,1,0:T(8,128)(2,1)} %refs_0_.3), channel_id=1, source_target_pairs={{0,4},{1,5},{2,6},{3,7},{4,8},{5,9},{6,10},{7,11},{8,12},{9,13},{1... | collective-permute-start | bytes 1572872 | tf_op jit(solution)/shard_map/ppermute | solution.py:87
  5.0 0.0 copy-start
  5.0 1.1 %copy-done = bf16[1,2,128,1024]{3,2,1,0:T(8,128)(2,1)S(1)} copy-done((bf16[1,2,128,1024]{3,2,1,0:T(8,128)(2,1)S(1)}, bf16[1,2,128,1024]{3,2,1,0:T(8,128)(2,1)}, u32[]{:S(2)}) %copy-start) | copy-done | bytes 524312
  6.0 0.0 copy-start.1
  6.0 0.0 copy-start.2
  6.0 0.1 deal.1
  6.1 0.1 collective-permute-start.4
  6.2 0.8 %copy-done.1 = bf16[1,2,64,1024]{3,2,1,0:T(8,128)(2,1)S(1)} copy-done((bf16[1,2,64,1024]{3,2,1,0:T(8,128)(2,1)S(1)}, bf16[1,2,64,1024]{3,2,1,0:T(8,128)(2,1)}, u32[]{:S(2)}) %copy-start.1) | copy-done | bytes 262168
  7.0 0.1 copy-done.2
  7.0 0.1 cut.2
  7.1 0.1 collective-permute-start
  7.2 1.6 %collective-permute-start.1 = (bf16[256,256]{1,0:T(8,128)(2,1)S(1)}, bf16[256,256]{1,0:T(8,128)(2,1)S(1)}, u32[]{:S(2)}, u32[]{:S(2)}) collective-permute-start(bf16[256,256]{1,0:T(8,128)(2,1)S(1)} %get-tuple-element.33), channel_id=1, source_target_pairs={{0,2},{1,3},{2,0},{3,1},{4,6},{5,7},{6,4},{7,5},{8,10},{9,11},{10,... | collective-permute-start | bytes 393224 | tf_op jit(solution)/shard_map/ppermute | solution.py:82
  8.8 0.3 collective-permute-start.2
  9.1 0.0 collective-permute-done.4.near.refs_1_
  9.1 1.6 %collective-permute-start.5 = (bf16[512,256]{1,0:T(8,128)(2,1)S(1)}, bf16[512,256]{1,0:T(8,128)(2,1)S(1)}, u32[]{:S(2)}, u32[]{:S(2)}) collective-permute-start(bf16[512,256]{1,0:T(8,128)(2,1)S(1)} %pair.1), channel_id=1, source_target_pairs={{0,2},{1,3},{2,0},{3,1},{4,6},{5,7},{6,4},{7,5},{8,10},{9,11},{10,... | collective-permute-start | bytes 786440 | tf_op jit(solution)/shard_map/ppermute | solution.py:172
  10.7 0.0 collective-permute-done.refs_1_.s1
  10.7 2.9 %collective-permute-done.1.refs_2_.s2 = bf16[256,256]{1,0:T(8,128)(2,1)S(1)} collective-permute-done((bf16[256,256]{1,0:T(8,128)(2,1)S(1)}, bf16[256,256]{1,0:T(8,128)(2,1)S(1)}, u32[]{:S(2)}, u32[]{:S(2)}) %collective-permute-start.1) | collective-permute-done | bytes 131104 | tf_op jit(solution)/shard_map/ppermute | solution.py:82
  13.6 1.9 %collective-permute-done.2.refs_3_.s3 = bf16[256,256]{1,0:T(8,128)(2,1)S(1)} collective-permute-done((bf16[256,256]{1,0:T(8,128)(2,1)S(1)}, bf16[256,256]{1,0:T(8,128)(2,1)S(1)}, u32[]{:S(2)}, u32[]{:S(2)}) %collective-permute-start.2) | collective-permute-done | bytes 131104 | tf_op jit(solution)/shard_map/ppermute | solution.py:82
  15.5 2.6 %collective-permute-start.3 = (bf16[2,256,256]{2,1,0:T(8,128)(2,1)S(1)}, bf16[2,256,256]{2,1,0:T(8,128)(2,1)S(1)}, u32[]{:S(2)}, u32[]{:S(2)}) collective-permute-start(bf16[2,256,256]{2,1,0:T(8,128)(2,1)S(1)} %lay.1.own), channel_id=1, source_target_pairs={{0,8},{1,9},{2,10},{3,11},{8,0},{9,1},{10,2},{11,3},{4,12},{5,13},... | collective-permute-start | bytes 786440 | tf_op jit(solution)/shard_map/ppermute | solution.py:87
  18.1 0.0 collective-permute-done.6.refs_0_
  18.1 0.1 cut.3
  18.2 0.8 %collective-permute-start.7 = (bf16[256,256]{1,0:T(8,128)(2,1)S(1)}, bf16[256,256]{1,0:T(8,128)(2,1)S(1)}, u32[]{:S(2)}, u32[]{:S(2)}) collective-permute-start(bf16[256,256]{1,0:T(8,128)(2,1)S(1)} %get-tuple-element.44), channel_id=1, source_target_pairs={{0,1},{1,0},{2,3},{3,2},{4,5},{5,4},{6,7},{7,6},{8,9},{9,8},{10,11... | collective-permute-start | bytes 393224 | tf_op jit(solution)/shard_map/ppermute | solution.py:82
  19.0 0.0 copy-start.3
  19.0 1.5 %collective-permute-start.8 = (bf16[256,256]{1,0:T(8,128)(2,1)S(1)}, bf16[256,256]{1,0:T(8,128)(2,1)S(1)}, u32[]{:S(2)}, u32[]{:S(2)}) collective-permute-start(bf16[256,256]{1,0:T(8,128)(2,1)S(1)} %get-tuple-element.45), channel_id=1, source_target_pairs={{0,2},{1,3},{2,0},{3,1},{4,6},{5,7},{6,4},{7,5},{8,10},{9,11},{10,... | collective-permute-start | bytes 393224 | tf_op jit(solution)/shard_map/ppermute | solution.py:82
  20.5 0.0 collective-permute-start.9
  20.5 0.0 copy-done.3
  20.5 1.7 %begin.1 = (bf16[4,128,512]{2,1,0:T(8,128)(2,1)S(1)}, f32[8,512]{1,0:T(8,128)S(1)}, f32[4,80,512]{2,1,0:T(8,128)S(1)}) custom-call(s32[1,12]{1,0:T(1,128)S(1)} %copy-done.3, bf16[256,256]{1,0:T(8,128)(2,1)S(1)} %get-tuple-element.31.refs_0_.s0, bf16[256,256]{1,0:T(8,128)(2,1)S(1)} %collective-permute-done.refs_1_.s1, ...), custom_call_target="tpu_custom_call" | custom-call | flops 134217728 | bytes 4194304 | tf_op jit(solution)/shard_map/begin/pallas_call | solution.py:289
  22.3 0.0 collective-permute-done.5.refs_2_
  22.3 1.2 %collective-permute-start.10 = (bf16[2,256,256]{2,1,0:T(8,128)(2,1)S(1)}, bf16[2,256,256]{2,1,0:T(8,128)(2,1)S(1)}, u32[]{:S(2)}, u32[]{:S(2)}) collective-permute-start(bf16[2,256,256]{2,1,0:T(8,128)(2,1)S(1)} %lay.1.own), channel_id=1, source_target_pairs={{0,4},{1,5},{2,6},{3,7},{4,0},{5,1},{6,2},{7,3},{8,12},{9,13},{10,... | collective-permute-start | bytes 786440 | tf_op jit(solution)/shard_map/ppermute | solution.py:87
  23.5 0.0 collective-permute-done.7.refs_1_
  23.5 0.7 %collective-permute-start.11 = (bf16[2,256,256]{2,1,0:T(8,128)(2,1)S(1)}, bf16[2,256,256]{2,1,0:T(8,128)(2,1)S(1)}, u32[]{:S(2)}, u32[]{:S(2)}) collective-permute-start(bf16[2,256,256]{2,1,0:T(8,128)(2,1)S(1)} %lay.1.own), channel_id=1, source_target_pairs={{4,8},{5,9},{6,10},{7,11},{8,4},{9,5},{10,6},{11,7},{20,24},{21,25... | collective-permute-start | bytes 786440 | tf_op jit(solution)/shard_map/ppermute | solution.py:87
  24.2 2.4 %suffix.2 = (f32[8,512]{1,0:T(8,128)S(1)}, f32[4,80,512]{2,1,0:T(8,128)S(1)}) custom-call(s32[1,12]{1,0:T(1,128)S(1)} %copy-done.3, bf16[4,128,512]{2,1,0:T(8,128)(2,1)S(1)} %get-tuple-element.35.qm, f32[8,512]{1,0:T(8,128)S(1)} %get-tuple-element.36.top_in, f32[4,80,512]{2,1,0:T(8,128)S(1)} %get-tuple-element.37.acc_in, ...), custom_call_target="tpu_custom_call" | custom-call | flops 268435456 | bytes 3145728 | tf_op jit(solution)/shard_map/suffix/pallas_call | solution.py:354
  26.6 0.0 collective-permute-done.8.refs_2_
  26.6 0.0 collective-permute-done.9.refs_3_
  26.6 0.7 %suffix.3 = (f32[8,512]{1,0:T(8,128)S(1)}, f32[4,80,512]{2,1,0:T(8,128)S(1)}) custom-call(s32[1,12]{1,0:T(1,128)S(1)} %copy-done.3, bf16[4,128,512]{2,1,0:T(8,128)(2,1)S(1)} %get-tuple-element.35.qm, f32[8,512]{1,0:T(8,128)S(1)} %get-tuple-element.41.top_in, f32[4,80,512]{2,1,0:T(8,128)S(1)} %get-tuple-element.42.acc_in, ...), custom_call_target="tpu_custom_call" | custom-call | flops 268435456 | bytes 3145728 | tf_op jit(solution)/shard_map/suffix/pallas_call | solution.py:354
  27.3 4.0 %collective-permute-done.3.refs_2_ = bf16[2,256,256]{2,1,0:T(8,128)(2,1)S(1)} collective-permute-done((bf16[2,256,256]{2,1,0:T(8,128)(2,1)S(1)}, bf16[2,256,256]{2,1,0:T(8,128)(2,1)S(1)}, u32[]{:S(2)}, u32[]{:S(2)}) %collective-permute-start.3) | collective-permute-done | bytes 262176 | tf_op jit(solution)/shard_map/ppermute | solution.py:87
  31.3 1.3 %collective-permute-start.12 = (bf16[2,256,256]{2,1,0:T(8,128)(2,1)S(1)}, bf16[2,256,256]{2,1,0:T(8,128)(2,1)S(1)}, u32[]{:S(2)}, u32[]{:S(2)}) collective-permute-start(bf16[2,256,256]{2,1,0:T(8,128)(2,1)S(1)} %collective-permute-done.3.refs_2_), channel_id=1, source_target_pairs={{8,12},{9,13},{10,14},{11,15},{4,0},{5,1},{6,2},{7,3},{24,28},{25,... | collective-permute-start | bytes 786440 | tf_op jit(solution)/shard_map/ppermute | solution.py:87
  32.6 3.1 %collective-permute-done.10.refs_0_ = bf16[2,256,256]{2,1,0:T(8,128)(2,1)S(1)} collective-permute-done((bf16[2,256,256]{2,1,0:T(8,128)(2,1)S(1)}, bf16[2,256,256]{2,1,0:T(8,128)(2,1)S(1)}, u32[]{:S(2)}, u32[]{:S(2)}) %collective-permute-start.10) | collective-permute-done | bytes 262176 | tf_op jit(solution)/shard_map/ppermute | solution.py:87
  35.7 0.0 collective-permute-done.11.refs_1_
  35.7 2.7 %prefix.1 = (f32[8,512]{1,0:T(8,128)S(1)}, f32[4,80,512]{2,1,0:T(8,128)S(1)}) custom-call(s32[1,12]{1,0:T(1,128)S(1)} %copy-done.3, bf16[4,128,512]{2,1,0:T(8,128)(2,1)S(1)} %get-tuple-element.35.qm, f32[8,512]{1,0:T(8,128)S(1)} %get-tuple-element.48.top_in, f32[4,80,512]{2,1,0:T(8,128)S(1)} %get-tuple-element.49.acc_in, ...), custom_call_target="tpu_custom_call" | custom-call | flops 402653184 | bytes 3145728 | tf_op jit(solution)/shard_map/prefix/pallas_call | solution.py:354
  38.4 3.0 %collective-permute-done.12.refs_0_ = bf16[2,256,256]{2,1,0:T(8,128)(2,1)S(1)} collective-permute-done((bf16[2,256,256]{2,1,0:T(8,128)(2,1)S(1)}, bf16[2,256,256]{2,1,0:T(8,128)(2,1)S(1)}, u32[]{:S(2)}, u32[]{:S(2)}) %collective-permute-start.12) | collective-permute-done | bytes 262176 | tf_op jit(solution)/shard_map/ppermute | solution.py:87
  41.4 1.8 %last.1 = (bf16[128,256]{1,0:T(8,128)(2,1)S(1)}, bf16[128,256]{1,0:T(8,128)(2,1)S(1)}, bf16[128,256]{1,0:T(8,128)(2,1)S(1)}, bf16[128,256]{1,0:T(8,128)(2,1)S(1)}) custom-call(s32[1,12]{1,0:T(1,128)S(1)} %copy-done.3, bf16[4,128,512]{2,1,0:T(8,128)(2,1)S(1)} %get-tuple-element.35.qm, f32[8,512]{1,0:T(8,128)S(1)} %get-tuple-element.51.top_in, ...), custom_call_target="tpu_custom_call" | custom-call | flops 134217728 | bytes 3145728 | tf_op jit(solution)/shard_map/last/pallas_call | solution.py:385
  43.2 0.1 collective-permute-start.13
  43.3 1.6 %collective-permute-start.14 = (bf16[128,256]{1,0:T(8,128)(2,1)S(1)}, bf16[128,256]{1,0:T(8,128)(2,1)S(1)}, u32[]{:S(2)}, u32[]{:S(2)}) collective-permute-start(bf16[128,256]{1,0:T(8,128)(2,1)S(1)} %get-tuple-element.55), channel_id=1, source_target_pairs={{0,2},{1,3},{2,0},{3,1},{4,6},{5,7},{6,4},{7,5},{8,10},{9,11},{10,... | collective-permute-start | bytes 196616 | tf_op jit(solution)/shard_map/ppermute | solution.py:82
  44.9 0.3 collective-permute-start.15
  45.2 0.0 collective-permute-done.13.s1
  45.2 2.6 %collective-permute-done.14.s2 = bf16[128,256]{1,0:T(8,128)(2,1)S(1)} collective-permute-done((bf16[128,256]{1,0:T(8,128)(2,1)S(1)}, bf16[128,256]{1,0:T(8,128)(2,1)S(1)}, u32[]{:S(2)}, u32[]{:S(2)}) %collective-permute-start.14) | collective-permute-done | bytes 65568 | tf_op jit(solution)/shard_map/ppermute | solution.py:82
  47.8 1.1 %collective-permute-done.15.s3 = bf16[128,256]{1,0:T(8,128)(2,1)S(1)} collective-permute-done((bf16[128,256]{1,0:T(8,128)(2,1)S(1)}, bf16[128,256]{1,0:T(8,128)(2,1)S(1)}, u32[]{:S(2)}, u32[]{:S(2)}) %collective-permute-start.15) | collective-permute-done | bytes 65568 | tf_op jit(solution)/shard_map/ppermute | solution.py:82
  49.0 0.7 %join.1 = bf16[1,128,1024]{2,1,0:T(8,128)(2,1)} custom-call(bf16[128,256]{1,0:T(8,128)(2,1)S(1)} %get-tuple-element.53.s0, bf16[128,256]{1,0:T(8,128)(2,1)S(1)} %collective-permute-done.13.s1, bf16[128,256]{1,0:T(8,128)(2,1)S(1)} %collective-permute-done.14.s2, bf16[128,256]{1,0:T(8,128)(2,1)S(1)} %collective-permute-done.15.s3), custom_call_target="tpu_custom_call" | custom-call | bytes 524288 | tf_op jit(solution)/shard_map/join/pallas_call | solution.py:409
  (2 shorter events, 0.0 us)
Async XLA Ops:
  0.0 18.1 %collective-permute-start.6 = (bf16[1,2,128,1024]{3,2,1,0:T(8,128)(2,1)}, bf16[1,2,128,1024]{3,2,1,0:T(8,128)(2,1)S(1)}, u32[]{:S(2)}, u32[]{:S(2)}) collective-permute-start(bf16[1,2,128,1024]{3,2,1,0:T(8,128)(2,1)} %refs_0_.3), channel_id=1, source_target_pairs={{0,4},{1,5},{2,6},{3,7},{4,8},{5,9},{6,10},{7,11},{8,12},{9,13},{1... | collective-permute-start | bytes 1572872 | tf_op jit(solution)/shard_map/ppermute | solution.py:87
  5.0 1.1 %copy-start = (bf16[1,2,128,1024]{3,2,1,0:T(8,128)(2,1)S(1)}, bf16[1,2,128,1024]{3,2,1,0:T(8,128)(2,1)}, u32[]{:S(2)}) copy-start(bf16[1,2,128,1024]{3,2,1,0:T(8,128)(2,1)} %refs_0_.3) | copy-start | bytes 1572868
  6.0 0.9 %copy-start.1 = (bf16[1,2,64,1024]{3,2,1,0:T(8,128)(2,1)S(1)}, bf16[1,2,64,1024]{3,2,1,0:T(8,128)(2,1)}, u32[]{:S(2)}) copy-start(bf16[1,2,64,1024]{3,2,1,0:T(8,128)(2,1)} %refs_0_.2) | copy-start | bytes 786436
  6.0 1.0 %copy-start.2 = (bf16[1,128,1024]{2,1,0:T(8,128)(2,1)S(1)}, bf16[1,128,1024]{2,1,0:T(8,128)(2,1)}, u32[]{:S(2)}) copy-start(bf16[1,128,1024]{2,1,0:T(8,128)(2,1)} %param.4) | copy-start | bytes 786436
  6.1 3.0 %collective-permute-start.4 = (bf16[512,256]{1,0:T(8,128)(2,1)S(1)}, bf16[512,256]{1,0:T(8,128)(2,1)S(1)}, u32[]{:S(2)}, u32[]{:S(2)}) collective-permute-start(bf16[512,256]{1,0:T(8,128)(2,1)S(1)} %get-tuple-element.39), channel_id=1, source_target_pairs={{0,1},{1,0},{2,3},{3,2},{4,5},{5,4},{6,7},{7,6},{8,9},{9,8},{10,11... | collective-permute-start | bytes 786440 | tf_op jit(solution)/shard_map/ppermute | solution.py:162
  7.1 3.6 %collective-permute-start = (bf16[256,256]{1,0:T(8,128)(2,1)S(1)}, bf16[256,256]{1,0:T(8,128)(2,1)S(1)}, u32[]{:S(2)}, u32[]{:S(2)}) collective-permute-start(bf16[256,256]{1,0:T(8,128)(2,1)S(1)} %get-tuple-element.32), channel_id=1, source_target_pairs={{0,1},{1,0},{2,3},{3,2},{4,5},{5,4},{6,7},{7,6},{8,9},{9,8},{10,11... | collective-permute-start | bytes 393224 | tf_op jit(solution)/shard_map/ppermute | solution.py:82
  7.2 6.4 %collective-permute-start.1 = (bf16[256,256]{1,0:T(8,128)(2,1)S(1)}, bf16[256,256]{1,0:T(8,128)(2,1)S(1)}, u32[]{:S(2)}, u32[]{:S(2)}) collective-permute-start(bf16[256,256]{1,0:T(8,128)(2,1)S(1)} %get-tuple-element.33), channel_id=1, source_target_pairs={{0,2},{1,3},{2,0},{3,1},{4,6},{5,7},{6,4},{7,5},{8,10},{9,11},{10,... | collective-permute-start | bytes 393224 | tf_op jit(solution)/shard_map/ppermute | solution.py:82
  8.8 6.7 %collective-permute-start.2 = (bf16[256,256]{1,0:T(8,128)(2,1)S(1)}, bf16[256,256]{1,0:T(8,128)(2,1)S(1)}, u32[]{:S(2)}, u32[]{:S(2)}) collective-permute-start(bf16[256,256]{1,0:T(8,128)(2,1)S(1)} %get-tuple-element.34), channel_id=1, source_target_pairs={{0,3},{1,2},{2,1},{3,0},{4,7},{5,6},{6,5},{7,4},{8,11},{9,10},{10,... | collective-permute-start | bytes 393224 | tf_op jit(solution)/shard_map/ppermute | solution.py:82
  9.1 13.2 %collective-permute-start.5 = (bf16[512,256]{1,0:T(8,128)(2,1)S(1)}, bf16[512,256]{1,0:T(8,128)(2,1)S(1)}, u32[]{:S(2)}, u32[]{:S(2)}) collective-permute-start(bf16[512,256]{1,0:T(8,128)(2,1)S(1)} %pair.1), channel_id=1, source_target_pairs={{0,2},{1,3},{2,0},{3,1},{4,6},{5,7},{6,4},{7,5},{8,10},{9,11},{10,... | collective-permute-start | bytes 786440 | tf_op jit(solution)/shard_map/ppermute | solution.py:172
  15.5 15.8 %collective-permute-start.3 = (bf16[2,256,256]{2,1,0:T(8,128)(2,1)S(1)}, bf16[2,256,256]{2,1,0:T(8,128)(2,1)S(1)}, u32[]{:S(2)}, u32[]{:S(2)}) collective-permute-start(bf16[2,256,256]{2,1,0:T(8,128)(2,1)S(1)} %lay.1.own), channel_id=1, source_target_pairs={{0,8},{1,9},{2,10},{3,11},{8,0},{9,1},{10,2},{11,3},{4,12},{5,13},... | collective-permute-start | bytes 786440 | tf_op jit(solution)/shard_map/ppermute | solution.py:87
  18.2 5.3 %collective-permute-start.7 = (bf16[256,256]{1,0:T(8,128)(2,1)S(1)}, bf16[256,256]{1,0:T(8,128)(2,1)S(1)}, u32[]{:S(2)}, u32[]{:S(2)}) collective-permute-start(bf16[256,256]{1,0:T(8,128)(2,1)S(1)} %get-tuple-element.44), channel_id=1, source_target_pairs={{0,1},{1,0},{2,3},{3,2},{4,5},{5,4},{6,7},{7,6},{8,9},{9,8},{10,11... | collective-permute-start | bytes 393224 | tf_op jit(solution)/shard_map/ppermute | solution.py:82
  19.0 1.5 %copy-start.3 = (s32[1,12]{1,0:T(1,128)S(1)}, s32[1,12]{1,0:T(1,128)}, u32[]{:S(2)}) copy-start(s32[1,12]{1,0:T(1,128)} %lens.9) | copy-start | bytes 148
  19.0 7.6 %collective-permute-start.8 = (bf16[256,256]{1,0:T(8,128)(2,1)S(1)}, bf16[256,256]{1,0:T(8,128)(2,1)S(1)}, u32[]{:S(2)}, u32[]{:S(2)}) collective-permute-start(bf16[256,256]{1,0:T(8,128)(2,1)S(1)} %get-tuple-element.45), channel_id=1, source_target_pairs={{0,2},{1,3},{2,0},{3,1},{4,6},{5,7},{6,4},{7,5},{8,10},{9,11},{10,... | collective-permute-start | bytes 393224 | tf_op jit(solution)/shard_map/ppermute | solution.py:82
  20.5 6.1 %collective-permute-start.9 = (bf16[256,256]{1,0:T(8,128)(2,1)S(1)}, bf16[256,256]{1,0:T(8,128)(2,1)S(1)}, u32[]{:S(2)}, u32[]{:S(2)}) collective-permute-start(bf16[256,256]{1,0:T(8,128)(2,1)S(1)} %get-tuple-element.46), channel_id=1, source_target_pairs={{0,3},{1,2},{2,1},{3,0},{4,7},{5,6},{6,5},{7,4},{8,11},{9,10},{10,... | collective-permute-start | bytes 393224 | tf_op jit(solution)/shard_map/ppermute | solution.py:82
  22.3 13.4 %collective-permute-start.10 = (bf16[2,256,256]{2,1,0:T(8,128)(2,1)S(1)}, bf16[2,256,256]{2,1,0:T(8,128)(2,1)S(1)}, u32[]{:S(2)}, u32[]{:S(2)}) collective-permute-start(bf16[2,256,256]{2,1,0:T(8,128)(2,1)S(1)} %lay.1.own), channel_id=1, source_target_pairs={{0,4},{1,5},{2,6},{3,7},{4,0},{5,1},{6,2},{7,3},{8,12},{9,13},{10,... | collective-permute-start | bytes 786440 | tf_op jit(solution)/shard_map/ppermute | solution.py:87
  23.5 12.2 %collective-permute-start.11 = (bf16[2,256,256]{2,1,0:T(8,128)(2,1)S(1)}, bf16[2,256,256]{2,1,0:T(8,128)(2,1)S(1)}, u32[]{:S(2)}, u32[]{:S(2)}) collective-permute-start(bf16[2,256,256]{2,1,0:T(8,128)(2,1)S(1)} %lay.1.own), channel_id=1, source_target_pairs={{4,8},{5,9},{6,10},{7,11},{8,4},{9,5},{10,6},{11,7},{20,24},{21,25... | collective-permute-start | bytes 786440 | tf_op jit(solution)/shard_map/ppermute | solution.py:87
  31.3 10.1 %collective-permute-start.12 = (bf16[2,256,256]{2,1,0:T(8,128)(2,1)S(1)}, bf16[2,256,256]{2,1,0:T(8,128)(2,1)S(1)}, u32[]{:S(2)}, u32[]{:S(2)}) collective-permute-start(bf16[2,256,256]{2,1,0:T(8,128)(2,1)S(1)} %collective-permute-done.3.refs_2_), channel_id=1, source_target_pairs={{8,12},{9,13},{10,14},{11,15},{4,0},{5,1},{6,2},{7,3},{24,28},{25,... | collective-permute-start | bytes 786440 | tf_op jit(solution)/shard_map/ppermute | solution.py:87
  43.2 1.9 %collective-permute-start.13 = (bf16[128,256]{1,0:T(8,128)(2,1)S(1)}, bf16[128,256]{1,0:T(8,128)(2,1)S(1)}, u32[]{:S(2)}, u32[]{:S(2)}) collective-permute-start(bf16[128,256]{1,0:T(8,128)(2,1)S(1)} %get-tuple-element.54), channel_id=1, source_target_pairs={{0,1},{1,0},{2,3},{3,2},{4,5},{5,4},{6,7},{7,6},{8,9},{9,8},{10,11... | collective-permute-start | bytes 196616 | tf_op jit(solution)/shard_map/ppermute | solution.py:82
  43.3 4.5 %collective-permute-start.14 = (bf16[128,256]{1,0:T(8,128)(2,1)S(1)}, bf16[128,256]{1,0:T(8,128)(2,1)S(1)}, u32[]{:S(2)}, u32[]{:S(2)}) collective-permute-start(bf16[128,256]{1,0:T(8,128)(2,1)S(1)} %get-tuple-element.55), channel_id=1, source_target_pairs={{0,2},{1,3},{2,0},{3,1},{4,6},{5,7},{6,4},{7,5},{8,10},{9,11},{10,... | collective-permute-start | bytes 196616 | tf_op jit(solution)/shard_map/ppermute | solution.py:82
  44.9 4.0 %collective-permute-start.15 = (bf16[128,256]{1,0:T(8,128)(2,1)S(1)}, bf16[128,256]{1,0:T(8,128)(2,1)S(1)}, u32[]{:S(2)}, u32[]{:S(2)}) collective-permute-start(bf16[128,256]{1,0:T(8,128)(2,1)S(1)} %get-tuple-element.56), channel_id=1, source_target_pairs={{0,3},{1,2},{2,1},{3,0},{4,7},{5,6},{6,5},{7,4},{8,11},{9,10},{10,... | collective-permute-start | bytes 196616 | tf_op jit(solution)/shard_map/ppermute | solution.py:82

commit v4 on v3

--- a/solution.py
+++ b/solution.py
@@ -77,9 +77,9 @@
 def exchange(slabs):
     count = lax.axis_size("req")
     got = [slabs[0]]
-    for distance in range(1, SUB):
+    for distance in range(SUB - 1, 0, -1):
         route = [(i, i ^ distance) for i in range(count)]
-        got.append(lax.ppermute(slabs[distance], "req", route))
+        got.insert(1, lax.ppermute(slabs[distance], "req", route))
     return got
 
 
@@ -145,7 +145,7 @@
     out[rows:] = near[rows:]
 
 
-def trade(*arrays):
+def trade(*arrays, after=None):
     rows = sum(a.shape[1] * a.shape[2] for a in arrays)
     slab = jax.ShapeDtypeStruct((rows, WIDE), BF16)
     slabs = jax.ShapeDtypeStruct((2 * rows, WIDE), BF16)
@@ -160,6 +160,8 @@
     )(*arrays)
     count = lax.axis_size("req")
     near = lax.ppermute(near, "req", [(i, i ^ 1) for i in range(count)])
+    if after is not None:
+        near, _ = lax.optimization_barrier((near, after))
     far = pl.pallas_call(
         pair_kernel,
         out_shape=slabs,
@@ -302,10 +304,9 @@
     )(lengths, *slabs, own)
 
 
-def pieces_step(sources, lens, qm, top, acc, refs):
+def pieces_step(sources, lens, qm, top, acc, refs, first):
     block, _ = place()
     blocks = lax.axis_size("req") // SUB
-    first = block * qm.shape[2]
     for ref, source in zip(refs, sources):
         number = source(block)
         valid = (number >= 0) & (number < blocks)
@@ -316,7 +317,8 @@
     *refs, top, acc = refs
     top[...] = top_in[...]
     acc[...] = acc_in[...]
-    pieces_step(sources, lens, qm, top, acc, refs)
+    block, _ = place()
+    pieces_step(sources, lens, qm, top, acc, refs, block * qm.shape[2])
 
 
 def suffix_kernel(distances, lens, qm, top_in, acc_in, *refs):
@@ -336,17 +338,21 @@
         over_suffix(lens, qm, top, acc, held.at[0], held.at[1], first, block * tokens, distance == 0)
 
 
-def last_kernel(sources, lens, qm, top_in, acc_in, *refs):
-    *refs, o0, o1, o2, o3, top, acc, turned = refs
-    _, sub = place()
-    top[...] = top_in[...]
-    acc[...] = acc_in[...]
-    pieces_step(sources, lens, qm, top, acc, refs)
+def last_kernel(sources, other, lens, qm_in, top_in, acc_in, *refs):
+    *refs, straight, cross, qm, top, acc, turned = refs
+    block, sub = place()
+    half = top.shape[1]
+    at = jnp.bitwise_xor(sub // 2, other) * half
+    cols = pl.ds(pl.multiple_of(at, half), half)
+    qm[...] = qm_in[:, :, cols]
+    top[...] = top_in[:, cols]
+    acc[...] = acc_in[:, :, cols]
+    pieces_step(sources, lens, qm, top, acc, refs, block * 2 * half + at)
     whole = jnp.concatenate([acc[h, :HEAD] * (1.0 / acc[h, HEAD:HEAD + 1]) for h in range(MINE)], axis=0)
     turned[...] = jnp.transpose(whole.astype(BF16))
-    rows = o0.shape[0]
-    for back, ref in enumerate((o0, o1, o2, o3)):
-        ref[...] = turned[pl.ds(pl.multiple_of(partner(sub, back) * rows, rows), rows)]
+    rows = straight.shape[0]
+    for side, ref in enumerate((straight, cross)):
+        ref[...] = turned[pl.ds(pl.multiple_of(jnp.bitwise_xor(sub % 2, side) * rows, rows), rows)]
 
 
 def carry_call(kernel, name, lengths, qm, top, acc, pieces, scratch, keys):
@@ -378,22 +384,23 @@
     )
 
 
-def finish(lengths, qm, top, acc, pieces):
-    tokens = qm.shape[2]
-    rows = tokens // SUB
-    scores = tokens * sum(p[0].shape[1] for p in pieces) * MINE
-    return pl.pallas_call(
-        functools.partial(last_kernel, [p[1] for p in pieces]),
-        out_shape=[jax.ShapeDtypeStruct((rows, WIDE), BF16)] * SUB,
+def finish(other, lengths, qm, top, acc, pieces):
+    half = qm.shape[2] // 2
+    rows = half // 2
+    scores = half * sum(p[0].shape[1] for p in pieces) * MINE
+    return pl.pallas_call(
+        functools.partial(last_kernel, [p[1] for p in pieces], other),
+        out_shape=[jax.ShapeDtypeStruct((rows, WIDE), BF16)] * 2,
         in_specs=[pl.BlockSpec(memory_space=pltpu.SMEM)] + vmem(3 + len(pieces)),
-        out_specs=vmem(SUB),
+        out_specs=vmem(2),
         scratch_shapes=[
-            pltpu.VMEM(top.shape, F32),
-            pltpu.VMEM(acc.shape, F32),
-            pltpu.VMEM((tokens, WIDE), BF16),
+            pltpu.VMEM((MINE, 2 * HEAD, half), BF16),
+            pltpu.VMEM((8, half), F32),
+            pltpu.VMEM((MINE, ROWS, half), F32),
+            pltpu.VMEM((half, WIDE), BF16),
         ],
         compiler_params=params(),
-        cost_estimate=cost(4 * HEAD * scores, 3 << 20, scores),
+        cost_estimate=cost(4 * HEAD * scores, 2 << 20, scores),
         name="last",
     )(lengths, qm, top, acc, *[p[0] for p in pieces])
 
@@ -428,7 +435,7 @@
 
     raw = [shift(suffix_kv, d) for d in range(1, reach + 1)]
     slabs = exchange(cut(prefix_kv, queries[:, None]))
-    near = trade(suffix_kv)
+    near = trade(suffix_kv, after=slabs[1])
     own = lay(slabs, prefix_kv.shape[2])
     pieces = gather_four(own) if blocks == 4 else gather_row(own, blocks)
     qm, top, acc = begin(lengths, slabs, own, rows)
@@ -441,8 +448,9 @@
         two, top = lax.optimization_barrier((two, top))
         pieces = pieces[:-1] + [(two, where), pass_on(two)]
     top, acc = prefix_call(lengths, qm, top, acc, pieces[:3])
-    mixed = finish(lengths, qm, top, acc, pieces[3:])
-    return join(exchange(mixed))
+    far = finish(1, lengths, qm, top, acc, pieces[3:])
+    near = finish(0, lengths, qm, top, acc, pieces[3:])
+    return join(exchange([*near, *far]))
 
 
 def solution(mesh):

time: 49.9 us -> 49.5 us (level)
  waiting for transfers between devices: 18.7 us -> 17 us
  Pallas kernels: 10.3 us -> 11.2 us
    ppermute x9, waiting for transfers between devices: 8.57 us -> 6.93 us  [exchange(): got.insert(1, lax.ppermute(slabs[distance], 'req', route))]
    pallas_call x1 -> x2, Pallas kernels: 1.79 us -> 2.66 us  [finish(): pl.pallas_call(functools.partial(last_kernel, [p[1] for p in pieces], oth...]
  transfers between devices with their start and end apart: 16 -> 16, of which waited for: 7 -> 7; matrix products, arithmetic and copies ran while one was open for 0% -> 0% of each run, Pallas kernels for 16% -> 19%
where the time goes in v4:
time: 49.5 us; the launch traced here: 49.2 us
  starting transfers between devices  18.9 us (38%)
  waiting for transfers between devices  17 us (34%)
  Pallas kernels  11.2 us (23%)
  local copies, waits for them, and re-layouts  1.94 us (4%)
    ppermute x5, starting transfers between devices, between(): lax.ppermute(block, 'req', [(SUB * a + s, SUB * b + s) for a, b in routes...  10.8 us
    ppermute x5, waiting for transfers between devices, between(): lax.ppermute(block, 'req', [(SUB * a + s, SUB * b + s) for a, b in routes...  10.1 us
    ppermute x9, waiting for transfers between devices, exchange(): got.insert(1, lax.ppermute(slabs[distance], 'req', route))  6.93 us
    ppermute x9, starting transfers between devices, exchange(): got.insert(1, lax.ppermute(slabs[distance], 'req', route))  6.53 us
    pallas_call x3, Pallas kernels, carry_call(): pl.pallas_call(kernel, out_shape=[jax.ShapeDtypeStruct(a.shape, a.dtype)...  5.82 us
    pallas_call x2, Pallas kernels, finish(): pl.pallas_call(functools.partial(last_kernel, [p[1] for p in pieces], oth...  2.66 us
    unnamed x8, local copies, waits for them, and re-layouts  1.94 us
    pallas_call x1, Pallas kernels, begin(): pl.pallas_call(begin_kernel, out_shape=[jax.ShapeDtypeStruct((MINE, 2 * H...  1.74 us
  transfers between devices with their start and end apart: 16, of which 7 were waited for; matrix products, arithmetic and copies ran while one was open for 0% of the time, Pallas kernels for 19%

profile of v4, /device:TPU:0, one launch (start us, length us, event | category | flops | bytes accessed | tf_op | source)
XLA Modules:
  0.0 49.2 jit_solution(13218048914000395497)
XLA Ops:
  0.0 4.9 %collective-permute-start.6 = (bf16[1,2,128,1024]{3,2,1,0:T(8,128)(2,1)}, bf16[1,2,128,1024]{3,2,1,0:T(8,128)(2,1)S(1)}, u32[]{:S(2)}, u32[]{:S(2)}) collective-permute-start(bf16[1,2,128,1024]{3,2,1,0:T(8,128)(2,1)} %refs_0_.3), channel_id=1, source_target_pairs={{0,4},{1,5},{2,6},{3,7},{4,8},{5,9},{6,10},{7,11},{8,12},{9,13},{1... | collective-permute-start | bytes 1572872 | tf_op jit(solution)/shard_map/ppermute | solution.py:87
  5.0 0.0 copy-start
  5.0 1.1 %copy-done = bf16[1,2,128,1024]{3,2,1,0:T(8,128)(2,1)S(1)} copy-done((bf16[1,2,128,1024]{3,2,1,0:T(8,128)(2,1)S(1)}, bf16[1,2,128,1024]{3,2,1,0:T(8,128)(2,1)}, u32[]{:S(2)}) %copy-start) | copy-done | bytes 524312
  6.0 0.0 copy-start.1
  6.0 0.0 copy-start.2
  6.0 0.1 deal.1
  6.1 0.1 collective-permute-start.4
  6.2 0.8 %copy-done.1 = bf16[1,2,64,1024]{3,2,1,0:T(8,128)(2,1)S(1)} copy-done((bf16[1,2,64,1024]{3,2,1,0:T(8,128)(2,1)S(1)}, bf16[1,2,64,1024]{3,2,1,0:T(8,128)(2,1)}, u32[]{:S(2)}) %copy-start.1) | copy-done | bytes 262168
  7.0 0.1 copy-done.2
  7.0 0.1 cut.2
  7.1 0.1 collective-permute-start
  7.2 1.6 %collective-permute-start.1 = (bf16[256,256]{1,0:T(8,128)(2,1)S(1)}, bf16[256,256]{1,0:T(8,128)(2,1)S(1)}, u32[]{:S(2)}, u32[]{:S(2)}) collective-permute-start(bf16[256,256]{1,0:T(8,128)(2,1)S(1)} %get-tuple-element.34), channel_id=1, source_target_pairs={{0,2},{1,3},{2,0},{3,1},{4,6},{5,7},{6,4},{7,5},{8,10},{9,11},{10,... | collective-permute-start | bytes 393224 | tf_op jit(solution)/shard_map/ppermute | solution.py:82
  8.8 0.3 collective-permute-start.2
  9.1 0.0 collective-permute-done.refs_1_.s1
  9.1 0.0 collective-permute-done.4.near.refs_1_
  9.1 1.6 %collective-permute-start.5 = (bf16[512,256]{1,0:T(8,128)(2,1)S(1)}, bf16[512,256]{1,0:T(8,128)(2,1)S(1)}, u32[]{:S(2)}, u32[]{:S(2)}) collective-permute-start(bf16[512,256]{1,0:T(8,128)(2,1)S(1)} %pair.1), channel_id=1, source_target_pairs={{0,2},{1,3},{2,0},{3,1},{4,6},{5,7},{6,4},{7,5},{8,10},{9,11},{10,... | collective-permute-start | bytes 786440 | tf_op jit(solution)/shard_map/ppermute | solution.py:174
  10.7 2.9 %collective-permute-done.1.refs_2_.s2 = bf16[256,256]{1,0:T(8,128)(2,1)S(1)} collective-permute-done((bf16[256,256]{1,0:T(8,128)(2,1)S(1)}, bf16[256,256]{1,0:T(8,128)(2,1)S(1)}, u32[]{:S(2)}, u32[]{:S(2)}) %collective-permute-start.1) | collective-permute-done | bytes 131104 | tf_op jit(solution)/shard_map/ppermute | solution.py:82
  13.6 1.9 %collective-permute-done.2.refs_3_.s3 = bf16[256,256]{1,0:T(8,128)(2,1)S(1)} collective-permute-done((bf16[256,256]{1,0:T(8,128)(2,1)S(1)}, bf16[256,256]{1,0:T(8,128)(2,1)S(1)}, u32[]{:S(2)}, u32[]{:S(2)}) %collective-permute-start.2) | collective-permute-done | bytes 131104 | tf_op jit(solution)/shard_map/ppermute | solution.py:82
  15.5 2.6 %collective-permute-start.3 = (bf16[2,256,256]{2,1,0:T(8,128)(2,1)S(1)}, bf16[2,256,256]{2,1,0:T(8,128)(2,1)S(1)}, u32[]{:S(2)}, u32[]{:S(2)}) collective-permute-start(bf16[2,256,256]{2,1,0:T(8,128)(2,1)S(1)} %lay.1.own), channel_id=1, source_target_pairs={{0,8},{1,9},{2,10},{3,11},{8,0},{9,1},{10,2},{11,3},{4,12},{5,13},... | collective-permute-start | bytes 786440 | tf_op jit(solution)/shard_map/ppermute | solution.py:87
  18.1 0.0 collective-permute-done.6.refs_0_
  18.1 0.1 cut.3
  18.2 0.8 %collective-permute-start.7 = (bf16[256,256]{1,0:T(8,128)(2,1)S(1)}, bf16[256,256]{1,0:T(8,128)(2,1)S(1)}, u32[]{:S(2)}, u32[]{:S(2)}) collective-permute-start(bf16[256,256]{1,0:T(8,128)(2,1)S(1)} %get-tuple-element.46), channel_id=1, source_target_pairs={{0,1},{1,0},{2,3},{3,2},{4,5},{5,4},{6,7},{7,6},{8,9},{9,8},{10,11... | collective-permute-start | bytes 393224 | tf_op jit(solution)/shard_map/ppermute | solution.py:82
  19.0 0.0 copy-start.3
  19.0 1.5 %collective-permute-start.8 = (bf16[256,256]{1,0:T(8,128)(2,1)S(1)}, bf16[256,256]{1,0:T(8,128)(2,1)S(1)}, u32[]{:S(2)}, u32[]{:S(2)}) collective-permute-start(bf16[256,256]{1,0:T(8,128)(2,1)S(1)} %get-tuple-element.47), channel_id=1, source_target_pairs={{0,2},{1,3},{2,0},{3,1},{4,6},{5,7},{6,4},{7,5},{8,10},{9,11},{10,... | collective-permute-start | bytes 393224 | tf_op jit(solution)/shard_map/ppermute | solution.py:82
  20.5 0.0 collective-permute-start.9
  20.5 0.0 copy-done.3
  20.5 1.7 %begin.1 = (bf16[4,128,512]{2,1,0:T(8,128)(2,1)S(1)}, f32[8,512]{1,0:T(8,128)S(1)}, f32[4,80,512]{2,1,0:T(8,128)S(1)}) custom-call(s32[1,12]{1,0:T(1,128)S(1)} %copy-done.3, bf16[256,256]{1,0:T(8,128)(2,1)S(1)} %get-tuple-element.32.refs_0_.s0, bf16[256,256]{1,0:T(8,128)(2,1)S(1)} %collective-permute-done.refs_1_.s1, ...), custom_call_target="tpu_custom_call" | custom-call | flops 134217728 | bytes 4194304 | tf_op jit(solution)/shard_map/begin/pallas_call | solution.py:291
  22.3 0.0 collective-permute-done.5.refs_2_
  22.3 1.2 %collective-permute-start.10 = (bf16[2,256,256]{2,1,0:T(8,128)(2,1)S(1)}, bf16[2,256,256]{2,1,0:T(8,128)(2,1)S(1)}, u32[]{:S(2)}, u32[]{:S(2)}) collective-permute-start(bf16[2,256,256]{2,1,0:T(8,128)(2,1)S(1)} %lay.1.own), channel_id=1, source_target_pairs={{0,4},{1,5},{2,6},{3,7},{4,0},{5,1},{6,2},{7,3},{8,12},{9,13},{10,... | collective-permute-start | bytes 786440 | tf_op jit(solution)/shard_map/ppermute | solution.py:87
  23.5 0.0 collective-permute-done.7.refs_1_
  23.5 0.7 %collective-permute-start.11 = (bf16[2,256,256]{2,1,0:T(8,128)(2,1)S(1)}, bf16[2,256,256]{2,1,0:T(8,128)(2,1)S(1)}, u32[]{:S(2)}, u32[]{:S(2)}) collective-permute-start(bf16[2,256,256]{2,1,0:T(8,128)(2,1)S(1)} %lay.1.own), channel_id=1, source_target_pairs={{4,8},{5,9},{6,10},{7,11},{8,4},{9,5},{10,6},{11,7},{20,24},{21,25... | collective-permute-start | bytes 786440 | tf_op jit(solution)/shard_map/ppermute | solution.py:87
  24.2 2.4 %suffix.2 = (f32[8,512]{1,0:T(8,128)S(1)}, f32[4,80,512]{2,1,0:T(8,128)S(1)}) custom-call(s32[1,12]{1,0:T(1,128)S(1)} %copy-done.3, bf16[4,128,512]{2,1,0:T(8,128)(2,1)S(1)} %get-tuple-element.36.qm.qm_in, f32[8,512]{1,0:T(8,128)S(1)} %get-tuple-element.37.top_in, f32[4,80,512]{2,1,0:T(8,128)S(1)} %get-tuple-element.38.acc_in, ...), custom_call_target="tpu_custom_call" | custom-call | flops 268435456 | bytes 3145728 | tf_op jit(solution)/shard_map/suffix/pallas_call | solution.py:360
  26.6 0.0 collective-permute-done.8.refs_2_
  26.6 0.0 collective-permute-done.9.refs_3_
  26.6 0.7 %suffix.3 = (f32[8,512]{1,0:T(8,128)S(1)}, f32[4,80,512]{2,1,0:T(8,128)S(1)}) custom-call(s32[1,12]{1,0:T(1,128)S(1)} %copy-done.3, bf16[4,128,512]{2,1,0:T(8,128)(2,1)S(1)} %get-tuple-element.36.qm.qm_in, f32[8,512]{1,0:T(8,128)S(1)} %get-tuple-element.43.top_in, f32[4,80,512]{2,1,0:T(8,128)S(1)} %get-tuple-element.44.acc_in, ...), custom_call_target="tpu_custom_call" | custom-call | flops 268435456 | bytes 3145728 | tf_op jit(solution)/shard_map/suffix/pallas_call | solution.py:360
  27.3 4.0 %collective-permute-done.3.refs_2_ = bf16[2,256,256]{2,1,0:T(8,128)(2,1)S(1)} collective-permute-done((bf16[2,256,256]{2,1,0:T(8,128)(2,1)S(1)}, bf16[2,256,256]{2,1,0:T(8,128)(2,1)S(1)}, u32[]{:S(2)}, u32[]{:S(2)}) %collective-permute-start.3) | collective-permute-done | bytes 262176 | tf_op jit(solution)/shard_map/ppermute | solution.py:87
  31.3 1.3 %collective-permute-start.12 = (bf16[2,256,256]{2,1,0:T(8,128)(2,1)S(1)}, bf16[2,256,256]{2,1,0:T(8,128)(2,1)S(1)}, u32[]{:S(2)}, u32[]{:S(2)}) collective-permute-start(bf16[2,256,256]{2,1,0:T(8,128)(2,1)S(1)} %collective-permute-done.3.refs_2_), channel_id=1, source_target_pairs={{8,12},{9,13},{10,14},{11,15},{4,0},{5,1},{6,2},{7,3},{24,28},{25,... | collective-permute-start | bytes 786440 | tf_op jit(solution)/shard_map/ppermute | solution.py:87
  32.6 3.1 %collective-permute-done.10.refs_0_ = bf16[2,256,256]{2,1,0:T(8,128)(2,1)S(1)} collective-permute-done((bf16[2,256,256]{2,1,0:T(8,128)(2,1)S(1)}, bf16[2,256,256]{2,1,0:T(8,128)(2,1)S(1)}, u32[]{:S(2)}, u32[]{:S(2)}) %collective-permute-start.10) | collective-permute-done | bytes 262176 | tf_op jit(solution)/shard_map/ppermute | solution.py:87
  35.7 0.0 collective-permute-done.11.refs_1_
  35.7 2.7 %prefix.1 = (f32[8,512]{1,0:T(8,128)S(1)}, f32[4,80,512]{2,1,0:T(8,128)S(1)}) custom-call(s32[1,12]{1,0:T(1,128)S(1)} %copy-done.3, bf16[4,128,512]{2,1,0:T(8,128)(2,1)S(1)} %get-tuple-element.36.qm.qm_in, f32[8,512]{1,0:T(8,128)S(1)} %get-tuple-element.50.top_in, f32[4,80,512]{2,1,0:T(8,128)S(1)} %get-tuple-element.51.acc_in, ...), custom_call_target="tpu_custom_call" | custom-call | flops 402653184 | bytes 3145728 | tf_op jit(solution)/shard_map/prefix/pallas_call | solution.py:360
  38.4 3.0 %collective-permute-done.12.refs_0_ = bf16[2,256,256]{2,1,0:T(8,128)(2,1)S(1)} collective-permute-done((bf16[2,256,256]{2,1,0:T(8,128)(2,1)S(1)}, bf16[2,256,256]{2,1,0:T(8,128)(2,1)S(1)}, u32[]{:S(2)}, u32[]{:S(2)}) %collective-permute-start.12) | collective-permute-done | bytes 262176 | tf_op jit(solution)/shard_map/ppermute | solution.py:87
  41.4 1.3 %last.3 = (bf16[128,256]{1,0:T(8,128)(2,1)S(1)}, bf16[128,256]{1,0:T(8,128)(2,1)S(1)}) custom-call(s32[1,12]{1,0:T(1,128)S(1)} %copy-done.3, bf16[4,128,512]{2,1,0:T(8,128)(2,1)S(1)} %get-tuple-element.36.qm.qm_in, f32[8,512]{1,0:T(8,128)S(1)} %get-tuple-element.53.top_in, f32[4,80,512]{2,1,0:T(8,128)S(1)} %get-tuple-element.54.acc_in, ...), custom_call_target="tpu_custom_call" | custom-call | flops 67108864 | bytes 2097152 | tf_op jit(solution)/shard_map/last/pallas_call | solution.py:391
  42.8 1.6 %collective-permute-start.14 = (bf16[128,256]{1,0:T(8,128)(2,1)S(1)}, bf16[128,256]{1,0:T(8,128)(2,1)S(1)}, u32[]{:S(2)}, u32[]{:S(2)}) collective-permute-start(bf16[128,256]{1,0:T(8,128)(2,1)S(1)} %get-tuple-element.57), channel_id=1, source_target_pairs={{0,2},{1,3},{2,0},{3,1},{4,6},{5,7},{6,4},{7,5},{8,10},{9,11},{10,... | collective-permute-start | bytes 196616 | tf_op jit(solution)/shard_map/ppermute | solution.py:82
  44.4 0.0 collective-permute-start.15
  44.4 1.3 %last.2 = (bf16[128,256]{1,0:T(8,128)(2,1)S(1)}, bf16[128,256]{1,0:T(8,128)(2,1)S(1)}) custom-call(s32[1,12]{1,0:T(1,128)S(1)} %copy-done.3, bf16[4,128,512]{2,1,0:T(8,128)(2,1)S(1)} %get-tuple-element.36.qm.qm_in, f32[8,512]{1,0:T(8,128)S(1)} %get-tuple-element.53.top_in, f32[4,80,512]{2,1,0:T(8,128)S(1)} %get-tuple-element.54.acc_in, ...), custom_call_target="tpu_custom_call" | custom-call | flops 67108864 | bytes 2097152 | tf_op jit(solution)/shard_map/last/pallas_call | solution.py:391
  45.7 0.7 %collective-permute-start.13 = (bf16[128,256]{1,0:T(8,128)(2,1)S(1)}, bf16[128,256]{1,0:T(8,128)(2,1)S(1)}, u32[]{:S(2)}, u32[]{:S(2)}) collective-permute-start(bf16[128,256]{1,0:T(8,128)(2,1)S(1)} %get-tuple-element.56), channel_id=1, source_target_pairs={{0,1},{1,0},{2,3},{3,2},{4,5},{5,4},{6,7},{7,6},{8,9},{9,8},{10,11... | collective-permute-start | bytes 196616 | tf_op jit(solution)/shard_map/ppermute | solution.py:82
  46.4 0.7 %collective-permute-done.14.s2 = bf16[128,256]{1,0:T(8,128)(2,1)S(1)} collective-permute-done((bf16[128,256]{1,0:T(8,128)(2,1)S(1)}, bf16[128,256]{1,0:T(8,128)(2,1)S(1)}, u32[]{:S(2)}, u32[]{:S(2)}) %collective-permute-start.14) | collective-permute-done | bytes 65568 | tf_op jit(solution)/shard_map/ppermute | solution.py:82
  47.1 1.4 %collective-permute-done.15.s3 = bf16[128,256]{1,0:T(8,128)(2,1)S(1)} collective-permute-done((bf16[128,256]{1,0:T(8,128)(2,1)S(1)}, bf16[128,256]{1,0:T(8,128)(2,1)S(1)}, u32[]{:S(2)}, u32[]{:S(2)}) %collective-permute-start.15) | collective-permute-done | bytes 65568 | tf_op jit(solution)/shard_map/ppermute | solution.py:82
  48.5 0.0 collective-permute-done.13.s1
  48.5 0.7 %join.1 = bf16[1,128,1024]{2,1,0:T(8,128)(2,1)} custom-call(bf16[128,256]{1,0:T(8,128)(2,1)S(1)} %get-tuple-element.55.s0, bf16[128,256]{1,0:T(8,128)(2,1)S(1)} %collective-permute-done.13.s1, bf16[128,256]{1,0:T(8,128)(2,1)S(1)} %collective-permute-done.14.s2, bf16[128,256]{1,0:T(8,128)(2,1)S(1)} %collective-permute-done.15.s3), custom_call_target="tpu_custom_call" | custom-call | bytes 524288 | tf_op jit(solution)/shard_map/join/pallas_call | solution.py:416
  (2 shorter events, 0.0 us)
Async XLA Ops:
  0.0 18.1 %collective-permute-start.6 = (bf16[1,2,128,1024]{3,2,1,0:T(8,128)(2,1)}, bf16[1,2,128,1024]{3,2,1,0:T(8,128)(2,1)S(1)}, u32[]{:S(2)}, u32[]{:S(2)}) collective-permute-start(bf16[1,2,128,1024]{3,2,1,0:T(8,128)(2,1)} %refs_0_.3), channel_id=1, source_target_pairs={{0,4},{1,5},{2,6},{3,7},{4,8},{5,9},{6,10},{7,11},{8,12},{9,13},{1... | collective-permute-start | bytes 1572872 | tf_op jit(solution)/shard_map/ppermute | solution.py:87
  5.0 1.1 %copy-start = (bf16[1,2,128,1024]{3,2,1,0:T(8,128)(2,1)S(1)}, bf16[1,2,128,1024]{3,2,1,0:T(8,128)(2,1)}, u32[]{:S(2)}) copy-start(bf16[1,2,128,1024]{3,2,1,0:T(8,128)(2,1)} %refs_0_.3) | copy-start | bytes 1572868
  6.0 0.9 %copy-start.1 = (bf16[1,2,64,1024]{3,2,1,0:T(8,128)(2,1)S(1)}, bf16[1,2,64,1024]{3,2,1,0:T(8,128)(2,1)}, u32[]{:S(2)}) copy-start(bf16[1,2,64,1024]{3,2,1,0:T(8,128)(2,1)} %refs_0_.2) | copy-start | bytes 786436
  6.0 1.0 %copy-start.2 = (bf16[1,128,1024]{2,1,0:T(8,128)(2,1)S(1)}, bf16[1,128,1024]{2,1,0:T(8,128)(2,1)}, u32[]{:S(2)}) copy-start(bf16[1,128,1024]{2,1,0:T(8,128)(2,1)} %param.4) | copy-start | bytes 786436
  6.1 3.0 %collective-permute-start.4 = (bf16[512,256]{1,0:T(8,128)(2,1)S(1)}, bf16[512,256]{1,0:T(8,128)(2,1)S(1)}, u32[]{:S(2)}, u32[]{:S(2)}) collective-permute-start(bf16[512,256]{1,0:T(8,128)(2,1)S(1)} %get-tuple-element.40), channel_id=1, source_target_pairs={{0,1},{1,0},{2,3},{3,2},{4,5},{5,4},{6,7},{7,6},{8,9},{9,8},{10,11... | collective-permute-start | bytes 786440 | tf_op jit(solution)/shard_map/ppermute | solution.py:162
  7.1 1.9 %collective-permute-start = (bf16[256,256]{1,0:T(8,128)(2,1)S(1)}, bf16[256,256]{1,0:T(8,128)(2,1)S(1)}, u32[]{:S(2)}, u32[]{:S(2)}) collective-permute-start(bf16[256,256]{1,0:T(8,128)(2,1)S(1)} %get-tuple-element.33), channel_id=1, source_target_pairs={{0,1},{1,0},{2,3},{3,2},{4,5},{5,4},{6,7},{7,6},{8,9},{9,8},{10,11... | collective-permute-start | bytes 393224 | tf_op jit(solution)/shard_map/ppermute | solution.py:82
  7.2 6.4 %collective-permute-start.1 = (bf16[256,256]{1,0:T(8,128)(2,1)S(1)}, bf16[256,256]{1,0:T(8,128)(2,1)S(1)}, u32[]{:S(2)}, u32[]{:S(2)}) collective-permute-start(bf16[256,256]{1,0:T(8,128)(2,1)S(1)} %get-tuple-element.34), channel_id=1, source_target_pairs={{0,2},{1,3},{2,0},{3,1},{4,6},{5,7},{6,4},{7,5},{8,10},{9,11},{10,... | collective-permute-start | bytes 393224 | tf_op jit(solution)/shard_map/ppermute | solution.py:82
  8.8 6.7 %collective-permute-start.2 = (bf16[256,256]{1,0:T(8,128)(2,1)S(1)}, bf16[256,256]{1,0:T(8,128)(2,1)S(1)}, u32[]{:S(2)}, u32[]{:S(2)}) collective-permute-start(bf16[256,256]{1,0:T(8,128)(2,1)S(1)} %get-tuple-element.35), channel_id=1, source_target_pairs={{0,3},{1,2},{2,1},{3,0},{4,7},{5,6},{6,5},{7,4},{8,11},{9,10},{10,... | collective-permute-start | bytes 393224 | tf_op jit(solution)/shard_map/ppermute | solution.py:82
  9.1 13.2 %collective-permute-start.5 = (bf16[512,256]{1,0:T(8,128)(2,1)S(1)}, bf16[512,256]{1,0:T(8,128)(2,1)S(1)}, u32[]{:S(2)}, u32[]{:S(2)}) collective-permute-start(bf16[512,256]{1,0:T(8,128)(2,1)S(1)} %pair.1), channel_id=1, source_target_pairs={{0,2},{1,3},{2,0},{3,1},{4,6},{5,7},{6,4},{7,5},{8,10},{9,11},{10,... | collective-permute-start | bytes 786440 | tf_op jit(solution)/shard_map/ppermute | solution.py:174
  15.5 15.8 %collective-permute-start.3 = (bf16[2,256,256]{2,1,0:T(8,128)(2,1)S(1)}, bf16[2,256,256]{2,1,0:T(8,128)(2,1)S(1)}, u32[]{:S(2)}, u32[]{:S(2)}) collective-permute-start(bf16[2,256,256]{2,1,0:T(8,128)(2,1)S(1)} %lay.1.own), channel_id=1, source_target_pairs={{0,8},{1,9},{2,10},{3,11},{8,0},{9,1},{10,2},{11,3},{4,12},{5,13},... | collective-permute-start | bytes 786440 | tf_op jit(solution)/shard_map/ppermute | solution.py:87
  18.2 5.3 %collective-permute-start.7 = (bf16[256,256]{1,0:T(8,128)(2,1)S(1)}, bf16[256,256]{1,0:T(8,128)(2,1)S(1)}, u32[]{:S(2)}, u32[]{:S(2)}) collective-permute-start(bf16[256,256]{1,0:T(8,128)(2,1)S(1)} %get-tuple-element.46), channel_id=1, source_target_pairs={{0,1},{1,0},{2,3},{3,2},{4,5},{5,4},{6,7},{7,6},{8,9},{9,8},{10,11... | collective-permute-start | bytes 393224 | tf_op jit(solution)/shard_map/ppermute | solution.py:82
  19.0 1.5 %copy-start.3 = (s32[1,12]{1,0:T(1,128)S(1)}, s32[1,12]{1,0:T(1,128)}, u32[]{:S(2)}) copy-start(s32[1,12]{1,0:T(1,128)} %lens.11) | copy-start | bytes 148
  19.0 7.6 %collective-permute-start.8 = (bf16[256,256]{1,0:T(8,128)(2,1)S(1)}, bf16[256,256]{1,0:T(8,128)(2,1)S(1)}, u32[]{:S(2)}, u32[]{:S(2)}) collective-permute-start(bf16[256,256]{1,0:T(8,128)(2,1)S(1)} %get-tuple-element.47), channel_id=1, source_target_pairs={{0,2},{1,3},{2,0},{3,1},{4,6},{5,7},{6,4},{7,5},{8,10},{9,11},{10,... | collective-permute-start | bytes 393224 | tf_op jit(solution)/shard_map/ppermute | solution.py:82
  20.5 6.1 %collective-permute-start.9 = (bf16[256,256]{1,0:T(8,128)(2,1)S(1)}, bf16[256,256]{1,0:T(8,128)(2,1)S(1)}, u32[]{:S(2)}, u32[]{:S(2)}) collective-permute-start(bf16[256,256]{1,0:T(8,128)(2,1)S(1)} %get-tuple-element.48), channel_id=1, source_target_pairs={{0,3},{1,2},{2,1},{3,0},{4,7},{5,6},{6,5},{7,4},{8,11},{9,10},{10,... | collective-permute-start | bytes 393224 | tf_op jit(solution)/shard_map/ppermute | solution.py:82
  22.3 13.4 %collective-permute-start.10 = (bf16[2,256,256]{2,1,0:T(8,128)(2,1)S(1)}, bf16[2,256,256]{2,1,0:T(8,128)(2,1)S(1)}, u32[]{:S(2)}, u32[]{:S(2)}) collective-permute-start(bf16[2,256,256]{2,1,0:T(8,128)(2,1)S(1)} %lay.1.own), channel_id=1, source_target_pairs={{0,4},{1,5},{2,6},{3,7},{4,0},{5,1},{6,2},{7,3},{8,12},{9,13},{10,... | collective-permute-start | bytes 786440 | tf_op jit(solution)/shard_map/ppermute | solution.py:87
  23.5 12.2 %collective-permute-start.11 = (bf16[2,256,256]{2,1,0:T(8,128)(2,1)S(1)}, bf16[2,256,256]{2,1,0:T(8,128)(2,1)S(1)}, u32[]{:S(2)}, u32[]{:S(2)}) collective-permute-start(bf16[2,256,256]{2,1,0:T(8,128)(2,1)S(1)} %lay.1.own), channel_id=1, source_target_pairs={{4,8},{5,9},{6,10},{7,11},{8,4},{9,5},{10,6},{11,7},{20,24},{21,25... | collective-permute-start | bytes 786440 | tf_op jit(solution)/shard_map/ppermute | solution.py:87
  31.3 10.1 %collective-permute-start.12 = (bf16[2,256,256]{2,1,0:T(8,128)(2,1)S(1)}, bf16[2,256,256]{2,1,0:T(8,128)(2,1)S(1)}, u32[]{:S(2)}, u32[]{:S(2)}) collective-permute-start(bf16[2,256,256]{2,1,0:T(8,128)(2,1)S(1)} %collective-permute-done.3.refs_2_), channel_id=1, source_target_pairs={{8,12},{9,13},{10,14},{11,15},{4,0},{5,1},{6,2},{7,3},{24,28},{25,... | collective-permute-start | bytes 786440 | tf_op jit(solution)/shard_map/ppermute | solution.py:87
  42.8 4.3 %collective-permute-start.14 = (bf16[128,256]{1,0:T(8,128)(2,1)S(1)}, bf16[128,256]{1,0:T(8,128)(2,1)S(1)}, u32[]{:S(2)}, u32[]{:S(2)}) collective-permute-start(bf16[128,256]{1,0:T(8,128)(2,1)S(1)} %get-tuple-element.57), channel_id=1, source_target_pairs={{0,2},{1,3},{2,0},{3,1},{4,6},{5,7},{6,4},{7,5},{8,10},{9,11},{10,... | collective-permute-start | bytes 196616 | tf_op jit(solution)/shard_map/ppermute | solution.py:82
  44.4 4.2 %collective-permute-start.15 = (bf16[128,256]{1,0:T(8,128)(2,1)S(1)}, bf16[128,256]{1,0:T(8,128)(2,1)S(1)}, u32[]{:S(2)}, u32[]{:S(2)}) collective-permute-start(bf16[128,256]{1,0:T(8,128)(2,1)S(1)} %get-tuple-element.58), channel_id=1, source_target_pairs={{0,3},{1,2},{2,1},{3,0},{4,7},{5,6},{6,5},{7,4},{8,11},{9,10},{10,... | collective-permute-start | bytes 196616 | tf_op jit(solution)/shard_map/ppermute | solution.py:82
  45.7 2.8 %collective-permute-start.13 = (bf16[128,256]{1,0:T(8,128)(2,1)S(1)}, bf16[128,256]{1,0:T(8,128)(2,1)S(1)}, u32[]{:S(2)}, u32[]{:S(2)}) collective-permute-start(bf16[128,256]{1,0:T(8,128)(2,1)S(1)} %get-tuple-element.56), channel_id=1, source_target_pairs={{0,1},{1,0},{2,3},{3,2},{4,5},{5,4},{6,7},{7,6},{8,9},{9,8},{10,11... | collective-permute-start | bytes 196616 | tf_op jit(solution)/shard_map/ppermute | solution.py:82

commit v5 on v4

--- a/solution.py
+++ b/solution.py
@@ -74,13 +74,15 @@
     )(*arrays)
 
 
-def exchange(slabs):
+def exchange(slabs, nearest_after=None):
     count = lax.axis_size("req")
-    got = [slabs[0]]
-    for distance in range(SUB - 1, 0, -1):
-        route = [(i, i ^ distance) for i in range(count)]
-        got.insert(1, lax.ppermute(slabs[distance], "req", route))
-    return got
+    got = {0: slabs[0]}
+    for distance in (2, 3, 1):
+        slab = slabs[distance]
+        if distance == 1 and nearest_after is not None:
+            slab, _ = lax.optimization_barrier((slab, got[nearest_after]))
+        got[distance] = lax.ppermute(slab, "req", [(i, i ^ distance) for i in range(count)])
+    return [got[distance] for distance in range(SUB)]
 
 
 def between(block, routes):
@@ -93,8 +95,9 @@
     return between(block, [(b, b + blocks) for b in range(low, high + 1)])
 
 
-def gather_four(own):
+def gather_four(own, top):
     two = between(own, [(0, 2), (2, 0), (1, 3), (3, 1)])
+    own, _ = lax.optimization_barrier((own, top))
     one = between(own, [(0, 1), (1, 0), (2, 3), (3, 2)])
     middle = between(own, [(1, 2), (2, 1)])
     return [
@@ -434,19 +437,19 @@
     reach = min(reach, blocks - 1)
 
     raw = [shift(suffix_kv, d) for d in range(1, reach + 1)]
-    slabs = exchange(cut(prefix_kv, queries[:, None]))
-    near = trade(suffix_kv, after=slabs[1])
+    slabs = exchange(cut(prefix_kv, queries[:, None]), 2)
+    near = trade(suffix_kv)
     own = lay(slabs, prefix_kv.shape[2])
-    pieces = gather_four(own) if blocks == 4 else gather_row(own, blocks)
     qm, top, acc = begin(lengths, slabs, own, rows)
+    pieces = gather_four(own, top) if blocks == 4 else gather_row(own, blocks)
     top, acc = suffix_call([0], lengths, qm, top, acc, near)
-    for back in range(1, reach + 1):
-        halo = exchange(cut(raw[back - 1]))
-        top, acc = suffix_call([back], lengths, qm, top, acc, halo)
+    halo = [exchange(cut(r)) for r in raw]
     if blocks == 4:
         two, where = pieces[-1]
-        two, top = lax.optimization_barrier((two, top))
+        two, top, _ = lax.optimization_barrier((two, top, [h[2:] for h in halo]))
         pieces = pieces[:-1] + [(two, where), pass_on(two)]
+    for back in range(1, reach + 1):
+        top, acc = suffix_call([back], lengths, qm, top, acc, halo[back - 1])
     top, acc = prefix_call(lengths, qm, top, acc, pieces[:3])
     far = finish(1, lengths, qm, top, acc, pieces[3:])
     near = finish(0, lengths, qm, top, acc, pieces[3:])

time: 49.5 us -> 48.2 us (0.974)
  waiting for transfers between devices: 17 us -> 16.3 us
    ppermute x5, waiting for transfers between devices: 10.1 us -> 8.76 us  [between(): lax.ppermute(block, 'req', [(SUB * a + s, SUB * b + s) for a, b in routes...]
    ppermute x9, starting transfers between devices: 6.53 us -> 5.29 us  [exchange(): lax.ppermute(slab, 'req', [(i, i ^ distance) for i in range(count)])]
    ppermute x1, starting transfers between devices: 1.58 us -> 2.44 us  [trade(): lax.ppermute(far, 'req', [(i, i ^ 2) for i in range(count)])]
  transfers between devices with their start and end apart: 16 -> 16, of which waited for: 7 -> 8; matrix products, arithmetic and copies ran while one was open for 0% -> 0% of each run, Pallas kernels for 19% -> 19%
where the time goes in v5:
time: 48.2 us; the launch traced here: 48 us
  starting transfers between devices  18.5 us (38%)
  waiting for transfers between devices  16.3 us (34%)
  Pallas kernels  11.2 us (23%)
  local copies, waits for them, and re-layouts  1.94 us (4%)
    ppermute x5, starting transfers between devices, between(): lax.ppermute(block, 'req', [(SUB * a + s, SUB * b + s) for a, b in routes...  10.7 us
    ppermute x5, waiting for transfers between devices, between(): lax.ppermute(block, 'req', [(SUB * a + s, SUB * b + s) for a, b in routes...  8.76 us
    ppermute x9, waiting for transfers between devices, exchange(): lax.ppermute(slab, 'req', [(i, i ^ distance) for i in range(count)])  7.38 us
    pallas_call x3, Pallas kernels, carry_call(): pl.pallas_call(kernel, out_shape=[jax.ShapeDtypeStruct(a.shape, a.dtype)...  5.81 us
    ppermute x9, starting transfers between devices, exchange(): lax.ppermute(slab, 'req', [(i, i ^ distance) for i in range(count)])  5.29 us
    pallas_call x2, Pallas kernels, finish(): pl.pallas_call(functools.partial(last_kernel, [p[1] for p in pieces], oth...  2.65 us
    ppermute x1, starting transfers between devices, trade(): lax.ppermute(far, 'req', [(i, i ^ 2) for i in range(count)])  2.44 us
    unnamed x8, local copies, waits for them, and re-layouts  1.94 us
  transfers between devices with their start and end apart: 16, of which 8 were waited for; matrix products, arithmetic and copies ran while one was open for 0% of the time, Pallas kernels for 19%

profile of v5, /device:TPU:0, one launch (start us, length us, event | category | flops | bytes accessed | tf_op | source)
XLA Modules:
  0.0 48.0 jit_solution(7101237251881208088)
XLA Ops:
  0.0 4.9 %collective-permute-start.6 = (bf16[1,2,128,1024]{3,2,1,0:T(8,128)(2,1)}, bf16[1,2,128,1024]{3,2,1,0:T(8,128)(2,1)S(1)}, u32[]{:S(2)}, u32[]{:S(2)}) collective-permute-start(bf16[1,2,128,1024]{3,2,1,0:T(8,128)(2,1)} %refs_0_.3), channel_id=1, source_target_pairs={{0,4},{1,5},{2,6},{3,7},{4,8},{5,9},{6,10},{7,11},{8,12},{9,13},{1... | collective-permute-start | bytes 1572872 | tf_op jit(solution)/shard_map/ppermute | solution.py:89
  5.0 0.0 copy-start
  5.0 1.1 %copy-done = bf16[1,2,128,1024]{3,2,1,0:T(8,128)(2,1)S(1)} copy-done((bf16[1,2,128,1024]{3,2,1,0:T(8,128)(2,1)S(1)}, bf16[1,2,128,1024]{3,2,1,0:T(8,128)(2,1)}, u32[]{:S(2)}) %copy-start) | copy-done | bytes 524312
  6.0 0.0 copy-start.1
  6.0 0.0 copy-start.2
  6.0 0.1 deal.1
  6.1 0.1 collective-permute-start.4
  6.2 0.8 %copy-done.1 = bf16[1,2,64,1024]{3,2,1,0:T(8,128)(2,1)S(1)} copy-done((bf16[1,2,64,1024]{3,2,1,0:T(8,128)(2,1)S(1)}, bf16[1,2,64,1024]{3,2,1,0:T(8,128)(2,1)}, u32[]{:S(2)}) %copy-start.1) | copy-done | bytes 262168
  7.0 0.1 copy-done.2
  7.0 0.1 cut.2
  7.1 1.6 %collective-permute-start = (bf16[256,256]{1,0:T(8,128)(2,1)S(1)}, bf16[256,256]{1,0:T(8,128)(2,1)S(1)}, u32[]{:S(2)}, u32[]{:S(2)}) collective-permute-start(bf16[256,256]{1,0:T(8,128)(2,1)S(1)} %get-tuple-element.35), channel_id=1, source_target_pairs={{0,2},{1,3},{2,0},{3,1},{4,6},{5,7},{6,4},{7,5},{8,10},{9,11},{10,... | collective-permute-start | bytes 393224 | tf_op jit(solution)/shard_map/ppermute | solution.py:84
  8.7 0.0 collective-permute-start.2
  8.7 4.0 %collective-permute-done.refs_2_.s2 = bf16[256,256]{1,0:T(8,128)(2,1)S(1)} collective-permute-done((bf16[256,256]{1,0:T(8,128)(2,1)S(1)}, bf16[256,256]{1,0:T(8,128)(2,1)S(1)}, u32[]{:S(2)}, u32[]{:S(2)}) %collective-permute-start) | collective-permute-done | bytes 131104 | tf_op jit(solution)/shard_map/ppermute | solution.py:84
  12.7 0.0 collective-permute-start.1
  12.8 0.0 collective-permute-done.4.near.refs_1_
  12.8 2.4 %collective-permute-start.5 = (bf16[512,256]{1,0:T(8,128)(2,1)S(1)}, bf16[512,256]{1,0:T(8,128)(2,1)S(1)}, u32[]{:S(2)}, u32[]{:S(2)}) collective-permute-start(bf16[512,256]{1,0:T(8,128)(2,1)S(1)} %pair.1), channel_id=1, source_target_pairs={{0,2},{1,3},{2,0},{3,1},{4,6},{5,7},{6,4},{7,5},{8,10},{9,11},{10,... | collective-permute-start | bytes 786440 | tf_op jit(solution)/shard_map/ppermute | solution.py:177
  15.2 0.0 collective-permute-done.2.refs_3_.s3
  15.2 0.0 collective-permute-done.1.refs_1_.s1
  15.3 2.6 %collective-permute-start.3 = (bf16[2,256,256]{2,1,0:T(8,128)(2,1)S(1)}, bf16[2,256,256]{2,1,0:T(8,128)(2,1)S(1)}, u32[]{:S(2)}, u32[]{:S(2)}) collective-permute-start(bf16[2,256,256]{2,1,0:T(8,128)(2,1)S(1)} %lay.1.own), channel_id=1, source_target_pairs={{0,8},{1,9},{2,10},{3,11},{8,0},{9,1},{10,2},{11,3},{4,12},{5,13},... | collective-permute-start | bytes 786440 | tf_op jit(solution)/shard_map/ppermute | solution.py:89
  17.9 0.0 collective-permute-done.6.refs_0_
  17.9 0.1 cut.3
  17.9 0.0 copy-start.3
  18.0 1.3 %collective-permute-start.7 = (bf16[256,256]{1,0:T(8,128)(2,1)S(1)}, bf16[256,256]{1,0:T(8,128)(2,1)S(1)}, u32[]{:S(2)}, u32[]{:S(2)}) collective-permute-start(bf16[256,256]{1,0:T(8,128)(2,1)S(1)} %get-tuple-element.45), channel_id=1, source_target_pairs={{0,2},{1,3},{2,0},{3,1},{4,6},{5,7},{6,4},{7,5},{8,10},{9,11},{10,... | collective-permute-start | bytes 393224 | tf_op jit(solution)/shard_map/ppermute | solution.py:84
  19.3 0.1 collective-permute-start.8
  19.3 0.0 copy-done.3
  19.3 1.7 %begin.1 = (bf16[4,128,512]{2,1,0:T(8,128)(2,1)S(1)}, f32[8,512]{1,0:T(8,128)S(1)}, f32[4,80,512]{2,1,0:T(8,128)S(1)}) custom-call(s32[1,12]{1,0:T(1,128)S(1)} %copy-done.3, bf16[256,256]{1,0:T(8,128)(2,1)S(1)} %get-tuple-element.33.refs_0_.s0, bf16[256,256]{1,0:T(8,128)(2,1)S(1)} %collective-permute-done.1.refs_1_.s1, ...), custom_call_target="tpu_custom_call" | custom-call | flops 134217728 | bytes 4194304 | tf_op jit(solution)/shard_map/begin/pallas_call | solution.py:294
  21.1 1.2 %collective-permute-start.10 = (bf16[2,256,256]{2,1,0:T(8,128)(2,1)S(1)}, bf16[2,256,256]{2,1,0:T(8,128)(2,1)S(1)}, u32[]{:S(2)}, u32[]{:S(2)}) collective-permute-start(bf16[2,256,256]{2,1,0:T(8,128)(2,1)S(1)} %lay.1.own), channel_id=1, source_target_pairs={{0,4},{1,5},{2,6},{3,7},{4,0},{5,1},{6,2},{7,3},{8,12},{9,13},{10,... | collective-permute-start | bytes 786440 | tf_op jit(solution)/shard_map/ppermute | solution.py:89
  22.3 0.1 collective-permute-done.5.refs_2_
  22.4 0.7 %collective-permute-start.11 = (bf16[2,256,256]{2,1,0:T(8,128)(2,1)S(1)}, bf16[2,256,256]{2,1,0:T(8,128)(2,1)S(1)}, u32[]{:S(2)}, u32[]{:S(2)}) collective-permute-start(bf16[2,256,256]{2,1,0:T(8,128)(2,1)S(1)} %lay.1.own), channel_id=1, source_target_pairs={{4,8},{5,9},{6,10},{7,11},{8,4},{9,5},{10,6},{11,7},{20,24},{21,25... | collective-permute-start | bytes 786440 | tf_op jit(solution)/shard_map/ppermute | solution.py:89
  23.0 2.4 %suffix.2 = (f32[8,512]{1,0:T(8,128)S(1)}, f32[4,80,512]{2,1,0:T(8,128)S(1)}) custom-call(s32[1,12]{1,0:T(1,128)S(1)} %copy-done.3, bf16[4,128,512]{2,1,0:T(8,128)(2,1)S(1)} %get-tuple-element.38.qm.qm_in, f32[8,512]{1,0:T(8,128)S(1)} %get-tuple-element.39.top_in, f32[4,80,512]{2,1,0:T(8,128)S(1)} %get-tuple-element.40.acc_in, ...), custom_call_target="tpu_custom_call" | custom-call | flops 268435456 | bytes 3145728 | tf_op jit(solution)/shard_map/suffix/pallas_call | solution.py:363
  25.5 5.3 %collective-permute-done.3.refs_2_ = bf16[2,256,256]{2,1,0:T(8,128)(2,1)S(1)} collective-permute-done((bf16[2,256,256]{2,1,0:T(8,128)(2,1)S(1)}, bf16[2,256,256]{2,1,0:T(8,128)(2,1)S(1)}, u32[]{:S(2)}, u32[]{:S(2)}) %collective-permute-start.3) | collective-permute-done | bytes 262176 | tf_op jit(solution)/shard_map/ppermute | solution.py:89
  30.8 0.0 collective-permute-done.7.refs_2_
  30.8 0.0 collective-permute-done.8.refs_3_
  30.8 1.3 %collective-permute-start.12 = (bf16[2,256,256]{2,1,0:T(8,128)(2,1)S(1)}, bf16[2,256,256]{2,1,0:T(8,128)(2,1)S(1)}, u32[]{:S(2)}, u32[]{:S(2)}) collective-permute-start(bf16[2,256,256]{2,1,0:T(8,128)(2,1)S(1)} %collective-permute-done.3.refs_2_), channel_id=1, source_target_pairs={{8,12},{9,13},{10,14},{11,15},{4,0},{5,1},{6,2},{7,3},{24,28},{25,... | collective-permute-start | bytes 786440 | tf_op jit(solution)/shard_map/ppermute | solution.py:89
  32.1 0.1 collective-permute-start.9
  32.2 1.3 %collective-permute-done.9.refs_1_ = bf16[256,256]{1,0:T(8,128)(2,1)S(1)} collective-permute-done((bf16[256,256]{1,0:T(8,128)(2,1)S(1)}, bf16[256,256]{1,0:T(8,128)(2,1)S(1)}, u32[]{:S(2)}, u32[]{:S(2)}) %collective-permute-start.9) | collective-permute-done | bytes 131104 | tf_op jit(solution)/shard_map/ppermute | solution.py:84
  33.5 0.7 %suffix.3 = (f32[8,512]{1,0:T(8,128)S(1)}, f32[4,80,512]{2,1,0:T(8,128)S(1)}) custom-call(s32[1,12]{1,0:T(1,128)S(1)} %copy-done.3, bf16[4,128,512]{2,1,0:T(8,128)(2,1)S(1)} %get-tuple-element.38.qm.qm_in, f32[8,512]{1,0:T(8,128)S(1)} %get-tuple-element.47.top_in, f32[4,80,512]{2,1,0:T(8,128)S(1)} %get-tuple-element.48.acc_in, ...), custom_call_target="tpu_custom_call" | custom-call | flops 268435456 | bytes 3145728 | tf_op jit(solution)/shard_map/suffix/pallas_call | solution.py:363
  34.2 0.6 %collective-permute-done.10.refs_0_ = bf16[2,256,256]{2,1,0:T(8,128)(2,1)S(1)} collective-permute-done((bf16[2,256,256]{2,1,0:T(8,128)(2,1)S(1)}, bf16[2,256,256]{2,1,0:T(8,128)(2,1)S(1)}, u32[]{:S(2)}, u32[]{:S(2)}) %collective-permute-start.10) | collective-permute-done | bytes 262176 | tf_op jit(solution)/shard_map/ppermute | solution.py:89
  34.8 0.0 collective-permute-done.11.refs_1_
  34.9 2.7 %prefix.1 = (f32[8,512]{1,0:T(8,128)S(1)}, f32[4,80,512]{2,1,0:T(8,128)S(1)}) custom-call(s32[1,12]{1,0:T(1,128)S(1)} %copy-done.3, bf16[4,128,512]{2,1,0:T(8,128)(2,1)S(1)} %get-tuple-element.38.qm.qm_in, f32[8,512]{1,0:T(8,128)S(1)} %get-tuple-element.51.top_in, f32[4,80,512]{2,1,0:T(8,128)S(1)} %get-tuple-element.52.acc_in, ...), custom_call_target="tpu_custom_call" | custom-call | flops 402653184 | bytes 3145728 | tf_op jit(solution)/shard_map/prefix/pallas_call | solution.py:363
  37.6 2.8 %collective-permute-done.12.refs_0_ = bf16[2,256,256]{2,1,0:T(8,128)(2,1)S(1)} collective-permute-done((bf16[2,256,256]{2,1,0:T(8,128)(2,1)S(1)}, bf16[2,256,256]{2,1,0:T(8,128)(2,1)S(1)}, u32[]{:S(2)}, u32[]{:S(2)}) %collective-permute-start.12) | collective-permute-done | bytes 262176 | tf_op jit(solution)/shard_map/ppermute | solution.py:89
  40.3 1.3 %last.3 = (bf16[128,256]{1,0:T(8,128)(2,1)S(1)}, bf16[128,256]{1,0:T(8,128)(2,1)S(1)}) custom-call(s32[1,12]{1,0:T(1,128)S(1)} %copy-done.3, bf16[4,128,512]{2,1,0:T(8,128)(2,1)S(1)} %get-tuple-element.38.qm.qm_in, f32[8,512]{1,0:T(8,128)S(1)} %get-tuple-element.55.top_in, f32[4,80,512]{2,1,0:T(8,128)S(1)} %get-tuple-element.56.acc_in, ...), custom_call_target="tpu_custom_call" | custom-call | flops 67108864 | bytes 2097152 | tf_op jit(solution)/shard_map/last/pallas_call | solution.py:394
  41.7 1.3 %collective-permute-start.14 = (bf16[128,256]{1,0:T(8,128)(2,1)S(1)}, bf16[128,256]{1,0:T(8,128)(2,1)S(1)}, u32[]{:S(2)}, u32[]{:S(2)}) collective-permute-start(bf16[128,256]{1,0:T(8,128)(2,1)S(1)} %get-tuple-element.59), channel_id=1, source_target_pairs={{0,2},{1,3},{2,0},{3,1},{4,6},{5,7},{6,4},{7,5},{8,10},{9,11},{10,... | collective-permute-start | bytes 196616 | tf_op jit(solution)/shard_map/ppermute | solution.py:84
  42.9 0.0 collective-permute-start.15
  42.9 1.3 %last.2 = (bf16[128,256]{1,0:T(8,128)(2,1)S(1)}, bf16[128,256]{1,0:T(8,128)(2,1)S(1)}) custom-call(s32[1,12]{1,0:T(1,128)S(1)} %copy-done.3, bf16[4,128,512]{2,1,0:T(8,128)(2,1)S(1)} %get-tuple-element.38.qm.qm_in, f32[8,512]{1,0:T(8,128)S(1)} %get-tuple-element.55.top_in, f32[4,80,512]{2,1,0:T(8,128)S(1)} %get-tuple-element.56.acc_in, ...), custom_call_target="tpu_custom_call" | custom-call | flops 67108864 | bytes 2097152 | tf_op jit(solution)/shard_map/last/pallas_call | solution.py:394
  44.3 1.0 %collective-permute-start.13 = (bf16[128,256]{1,0:T(8,128)(2,1)S(1)}, bf16[128,256]{1,0:T(8,128)(2,1)S(1)}, u32[]{:S(2)}, u32[]{:S(2)}) collective-permute-start(bf16[128,256]{1,0:T(8,128)(2,1)S(1)} %get-tuple-element.58), channel_id=1, source_target_pairs={{0,1},{1,0},{2,3},{3,2},{4,5},{5,4},{6,7},{7,6},{8,9},{9,8},{10,11... | collective-permute-start | bytes 196616 | tf_op jit(solution)/shard_map/ppermute | solution.py:84
  45.3 0.9 %collective-permute-done.14.s2 = bf16[128,256]{1,0:T(8,128)(2,1)S(1)} collective-permute-done((bf16[128,256]{1,0:T(8,128)(2,1)S(1)}, bf16[128,256]{1,0:T(8,128)(2,1)S(1)}, u32[]{:S(2)}, u32[]{:S(2)}) %collective-permute-start.14) | collective-permute-done | bytes 65568 | tf_op jit(solution)/shard_map/ppermute | solution.py:84
  46.1 1.1 %collective-permute-done.15.s3 = bf16[128,256]{1,0:T(8,128)(2,1)S(1)} collective-permute-done((bf16[128,256]{1,0:T(8,128)(2,1)S(1)}, bf16[128,256]{1,0:T(8,128)(2,1)S(1)}, u32[]{:S(2)}, u32[]{:S(2)}) %collective-permute-start.15) | collective-permute-done | bytes 65568 | tf_op jit(solution)/shard_map/ppermute | solution.py:84
  47.3 0.0 collective-permute-done.13.s1
  47.3 0.7 %join.1 = bf16[1,128,1024]{2,1,0:T(8,128)(2,1)} custom-call(bf16[128,256]{1,0:T(8,128)(2,1)S(1)} %get-tuple-element.57.s0, bf16[128,256]{1,0:T(8,128)(2,1)S(1)} %collective-permute-done.13.s1, bf16[128,256]{1,0:T(8,128)(2,1)S(1)} %collective-permute-done.14.s2, bf16[128,256]{1,0:T(8,128)(2,1)S(1)} %collective-permute-done.15.s3), custom_call_target="tpu_custom_call" | custom-call | bytes 524288 | tf_op jit(solution)/shard_map/join/pallas_call | solution.py:419
  (2 shorter events, 0.0 us)
Async XLA Ops:
  0.0 17.9 %collective-permute-start.6 = (bf16[1,2,128,1024]{3,2,1,0:T(8,128)(2,1)}, bf16[1,2,128,1024]{3,2,1,0:T(8,128)(2,1)S(1)}, u32[]{:S(2)}, u32[]{:S(2)}) collective-permute-start(bf16[1,2,128,1024]{3,2,1,0:T(8,128)(2,1)} %refs_0_.3), channel_id=1, source_target_pairs={{0,4},{1,5},{2,6},{3,7},{4,8},{5,9},{6,10},{7,11},{8,12},{9,13},{1... | collective-permute-start | bytes 1572872 | tf_op jit(solution)/shard_map/ppermute | solution.py:89
  5.0 1.1 %copy-start = (bf16[1,2,128,1024]{3,2,1,0:T(8,128)(2,1)S(1)}, bf16[1,2,128,1024]{3,2,1,0:T(8,128)(2,1)}, u32[]{:S(2)}) copy-start(bf16[1,2,128,1024]{3,2,1,0:T(8,128)(2,1)} %refs_0_.3) | copy-start | bytes 1572868
  6.0 0.9 %copy-start.1 = (bf16[1,2,64,1024]{3,2,1,0:T(8,128)(2,1)S(1)}, bf16[1,2,64,1024]{3,2,1,0:T(8,128)(2,1)}, u32[]{:S(2)}) copy-start(bf16[1,2,64,1024]{3,2,1,0:T(8,128)(2,1)} %refs_0_.2) | copy-start | bytes 786436
  6.0 1.0 %copy-start.2 = (bf16[1,128,1024]{2,1,0:T(8,128)(2,1)S(1)}, bf16[1,128,1024]{2,1,0:T(8,128)(2,1)}, u32[]{:S(2)}) copy-start(bf16[1,128,1024]{2,1,0:T(8,128)(2,1)} %param.4) | copy-start | bytes 786436
  6.1 6.7 %collective-permute-start.4 = (bf16[512,256]{1,0:T(8,128)(2,1)S(1)}, bf16[512,256]{1,0:T(8,128)(2,1)S(1)}, u32[]{:S(2)}, u32[]{:S(2)}) collective-permute-start(bf16[512,256]{1,0:T(8,128)(2,1)S(1)} %get-tuple-element.42), channel_id=1, source_target_pairs={{0,1},{1,0},{2,3},{3,2},{4,5},{5,4},{6,7},{7,6},{8,9},{9,8},{10,11... | collective-permute-start | bytes 786440 | tf_op jit(solution)/shard_map/ppermute | solution.py:165
  7.1 5.6 %collective-permute-start = (bf16[256,256]{1,0:T(8,128)(2,1)S(1)}, bf16[256,256]{1,0:T(8,128)(2,1)S(1)}, u32[]{:S(2)}, u32[]{:S(2)}) collective-permute-start(bf16[256,256]{1,0:T(8,128)(2,1)S(1)} %get-tuple-element.35), channel_id=1, source_target_pairs={{0,2},{1,3},{2,0},{3,1},{4,6},{5,7},{6,4},{7,5},{8,10},{9,11},{10,... | collective-permute-start | bytes 393224 | tf_op jit(solution)/shard_map/ppermute | solution.py:84
  8.7 6.5 %collective-permute-start.2 = (bf16[256,256]{1,0:T(8,128)(2,1)S(1)}, bf16[256,256]{1,0:T(8,128)(2,1)S(1)}, u32[]{:S(2)}, u32[]{:S(2)}) collective-permute-start(bf16[256,256]{1,0:T(8,128)(2,1)S(1)} %get-tuple-element.37), channel_id=1, source_target_pairs={{0,3},{1,2},{2,1},{3,0},{4,7},{5,6},{6,5},{7,4},{8,11},{9,10},{10,... | collective-permute-start | bytes 393224 | tf_op jit(solution)/shard_map/ppermute | solution.py:84
  12.7 2.5 %collective-permute-start.1 = (bf16[256,256]{1,0:T(8,128)(2,1)S(1)}, bf16[256,256]{1,0:T(8,128)(2,1)S(1)}, u32[]{:S(2)}, u32[]{:S(2)}) collective-permute-start(bf16[256,256]{1,0:T(8,128)(2,1)S(1)} %get-tuple-element.36), channel_id=1, source_target_pairs={{0,1},{1,0},{2,3},{3,2},{4,5},{5,4},{6,7},{7,6},{8,9},{9,8},{10,11... | collective-permute-start | bytes 393224 | tf_op jit(solution)/shard_map/ppermute | solution.py:84
  12.8 9.6 %collective-permute-start.5 = (bf16[512,256]{1,0:T(8,128)(2,1)S(1)}, bf16[512,256]{1,0:T(8,128)(2,1)S(1)}, u32[]{:S(2)}, u32[]{:S(2)}) collective-permute-start(bf16[512,256]{1,0:T(8,128)(2,1)S(1)} %pair.1), channel_id=1, source_target_pairs={{0,2},{1,3},{2,0},{3,1},{4,6},{5,7},{6,4},{7,5},{8,10},{9,11},{10,... | collective-permute-start | bytes 786440 | tf_op jit(solution)/shard_map/ppermute | solution.py:177
  15.3 15.5 %collective-permute-start.3 = (bf16[2,256,256]{2,1,0:T(8,128)(2,1)S(1)}, bf16[2,256,256]{2,1,0:T(8,128)(2,1)S(1)}, u32[]{:S(2)}, u32[]{:S(2)}) collective-permute-start(bf16[2,256,256]{2,1,0:T(8,128)(2,1)S(1)} %lay.1.own), channel_id=1, source_target_pairs={{0,8},{1,9},{2,10},{3,11},{8,0},{9,1},{10,2},{11,3},{4,12},{5,13},... | collective-permute-start | bytes 786440 | tf_op jit(solution)/shard_map/ppermute | solution.py:89
  17.9 1.4 %copy-start.3 = (s32[1,12]{1,0:T(1,128)S(1)}, s32[1,12]{1,0:T(1,128)}, u32[]{:S(2)}) copy-start(s32[1,12]{1,0:T(1,128)} %lens.11) | copy-start | bytes 148
  18.0 12.8 %collective-permute-start.7 = (bf16[256,256]{1,0:T(8,128)(2,1)S(1)}, bf16[256,256]{1,0:T(8,128)(2,1)S(1)}, u32[]{:S(2)}, u32[]{:S(2)}) collective-permute-start(bf16[256,256]{1,0:T(8,128)(2,1)S(1)} %get-tuple-element.45), channel_id=1, source_target_pairs={{0,2},{1,3},{2,0},{3,1},{4,6},{5,7},{6,4},{7,5},{8,10},{9,11},{10,... | collective-permute-start | bytes 393224 | tf_op jit(solution)/shard_map/ppermute | solution.py:84
  19.3 11.5 %collective-permute-start.8 = (bf16[256,256]{1,0:T(8,128)(2,1)S(1)}, bf16[256,256]{1,0:T(8,128)(2,1)S(1)}, u32[]{:S(2)}, u32[]{:S(2)}) collective-permute-start(bf16[256,256]{1,0:T(8,128)(2,1)S(1)} %get-tuple-element.46), channel_id=1, source_target_pairs={{0,3},{1,2},{2,1},{3,0},{4,7},{5,6},{6,5},{7,4},{8,11},{9,10},{10,... | collective-permute-start | bytes 393224 | tf_op jit(solution)/shard_map/ppermute | solution.py:84
  21.1 13.8 %collective-permute-start.10 = (bf16[2,256,256]{2,1,0:T(8,128)(2,1)S(1)}, bf16[2,256,256]{2,1,0:T(8,128)(2,1)S(1)}, u32[]{:S(2)}, u32[]{:S(2)}) collective-permute-start(bf16[2,256,256]{2,1,0:T(8,128)(2,1)S(1)} %lay.1.own), channel_id=1, source_target_pairs={{0,4},{1,5},{2,6},{3,7},{4,0},{5,1},{6,2},{7,3},{8,12},{9,13},{10,... | collective-permute-start | bytes 786440 | tf_op jit(solution)/shard_map/ppermute | solution.py:89
  22.4 12.5 %collective-permute-start.11 = (bf16[2,256,256]{2,1,0:T(8,128)(2,1)S(1)}, bf16[2,256,256]{2,1,0:T(8,128)(2,1)S(1)}, u32[]{:S(2)}, u32[]{:S(2)}) collective-permute-start(bf16[2,256,256]{2,1,0:T(8,128)(2,1)S(1)} %lay.1.own), channel_id=1, source_target_pairs={{4,8},{5,9},{6,10},{7,11},{8,4},{9,5},{10,6},{11,7},{20,24},{21,25... | collective-permute-start | bytes 786440 | tf_op jit(solution)/shard_map/ppermute | solution.py:89
  30.8 9.5 %collective-permute-start.12 = (bf16[2,256,256]{2,1,0:T(8,128)(2,1)S(1)}, bf16[2,256,256]{2,1,0:T(8,128)(2,1)S(1)}, u32[]{:S(2)}, u32[]{:S(2)}) collective-permute-start(bf16[2,256,256]{2,1,0:T(8,128)(2,1)S(1)} %collective-permute-done.3.refs_2_), channel_id=1, source_target_pairs={{8,12},{9,13},{10,14},{11,15},{4,0},{5,1},{6,2},{7,3},{24,28},{25,... | collective-permute-start | bytes 786440 | tf_op jit(solution)/shard_map/ppermute | solution.py:89
  32.1 1.4 %collective-permute-start.9 = (bf16[256,256]{1,0:T(8,128)(2,1)S(1)}, bf16[256,256]{1,0:T(8,128)(2,1)S(1)}, u32[]{:S(2)}, u32[]{:S(2)}) collective-permute-start(bf16[256,256]{1,0:T(8,128)(2,1)S(1)} %get-tuple-element.50), channel_id=1, source_target_pairs={{0,1},{1,0},{2,3},{3,2},{4,5},{5,4},{6,7},{7,6},{8,9},{9,8},{10,11... | collective-permute-start | bytes 393224 | tf_op jit(solution)/shard_map/ppermute | solution.py:84
  41.7 4.5 %collective-permute-start.14 = (bf16[128,256]{1,0:T(8,128)(2,1)S(1)}, bf16[128,256]{1,0:T(8,128)(2,1)S(1)}, u32[]{:S(2)}, u32[]{:S(2)}) collective-permute-start(bf16[128,256]{1,0:T(8,128)(2,1)S(1)} %get-tuple-element.59), channel_id=1, source_target_pairs={{0,2},{1,3},{2,0},{3,1},{4,6},{5,7},{6,4},{7,5},{8,10},{9,11},{10,... | collective-permute-start | bytes 196616 | tf_op jit(solution)/shard_map/ppermute | solution.py:84
  42.9 4.3 %collective-permute-start.15 = (bf16[128,256]{1,0:T(8,128)(2,1)S(1)}, bf16[128,256]{1,0:T(8,128)(2,1)S(1)}, u32[]{:S(2)}, u32[]{:S(2)}) collective-permute-start(bf16[128,256]{1,0:T(8,128)(2,1)S(1)} %get-tuple-element.60), channel_id=1, source_target_pairs={{0,3},{1,2},{2,1},{3,0},{4,7},{5,6},{6,5},{7,4},{8,11},{9,10},{10,... | collective-permute-start | bytes 196616 | tf_op jit(solution)/shard_map/ppermute | solution.py:84
  44.3 3.0 %collective-permute-start.13 = (bf16[128,256]{1,0:T(8,128)(2,1)S(1)}, bf16[128,256]{1,0:T(8,128)(2,1)S(1)}, u32[]{:S(2)}, u32[]{:S(2)}) collective-permute-start(bf16[128,256]{1,0:T(8,128)(2,1)S(1)} %get-tuple-element.58), channel_id=1, source_target_pairs={{0,1},{1,0},{2,3},{3,2},{4,5},{5,4},{6,7},{7,6},{8,9},{9,8},{10,11... | collective-permute-start | bytes 196616 | tf_op jit(solution)/shard_map/ppermute | solution.py:84

commit v6 on v5

--- a/solution.py
+++ b/solution.py
@@ -97,7 +97,6 @@
 
 def gather_four(own, top):
     two = between(own, [(0, 2), (2, 0), (1, 3), (3, 1)])
-    own, _ = lax.optimization_barrier((own, top))
     one = between(own, [(0, 1), (1, 0), (2, 3), (3, 2)])
     middle = between(own, [(1, 2), (2, 1)])
     return [

time: 48.2 us -> 47.6 us (0.988)
  waiting for transfers between devices: 16.3 us -> 15.6 us
    ppermute x5, waiting for transfers between devices: 8.76 us -> 6.46 us  [between(): lax.ppermute(block, 'req', [(SUB * a + s, SUB * b + s) for a, b in routes...]
    ppermute x1, waiting for transfers between devices: 0.12 us -> 1.92 us  [trade(): lax.ppermute(far, 'req', [(i, i ^ 2) for i in range(count)])]
  transfers between devices with their start and end apart: 16 -> 16, of which waited for: 8 -> 7; matrix products, arithmetic and copies ran while one was open for 0% -> 0% of each run, Pallas kernels for 19% -> 19%
where the time goes in v6:
time: 47.6 us; the launch traced here: 47.4 us
  starting transfers between devices  18.4 us (39%)
  waiting for transfers between devices  15.6 us (33%)
  Pallas kernels  11.2 us (24%)
  local copies, waits for them, and re-layouts  1.94 us (4%)
    ppermute x5, starting transfers between devices, between(): lax.ppermute(block, 'req', [(SUB * a + s, SUB * b + s) for a, b in routes...  10.6 us
    ppermute x9, waiting for transfers between devices, exchange(): lax.ppermute(slab, 'req', [(i, i ^ distance) for i in range(count)])  7.25 us
    ppermute x5, waiting for transfers between devices, between(): lax.ppermute(block, 'req', [(SUB * a + s, SUB * b + s) for a, b in routes...  6.46 us
    pallas_call x3, Pallas kernels, carry_call(): pl.pallas_call(kernel, out_shape=[jax.ShapeDtypeStruct(a.shape, a.dtype)...  5.83 us
    ppermute x9, starting transfers between devices, exchange(): lax.ppermute(slab, 'req', [(i, i ^ distance) for i in range(count)])  5.29 us
    pallas_call x2, Pallas kernels, finish(): pl.pallas_call(functools.partial(last_kernel, [p[1] for p in pieces], oth...  2.65 us
    ppermute x1, starting transfers between devices, trade(): lax.ppermute(far, 'req', [(i, i ^ 2) for i in range(count)])  2.44 us
    unnamed x8, local copies, waits for them, and re-layouts  1.94 us
  transfers between devices with their start and end apart: 16, of which 7 were waited for; matrix products, arithmetic and copies ran while one was open for 0% of the time, Pallas kernels for 19%

profile of v6, /device:TPU:0, one launch (start us, length us, event | category | flops | bytes accessed | tf_op | source)
XLA Modules:
  0.0 47.4 jit_solution(6625630466705166114)
XLA Ops:
  0.0 4.9 %collective-permute-start.6 = (bf16[1,2,128,1024]{3,2,1,0:T(8,128)(2,1)}, bf16[1,2,128,1024]{3,2,1,0:T(8,128)(2,1)S(1)}, u32[]{:S(2)}, u32[]{:S(2)}) collective-permute-start(bf16[1,2,128,1024]{3,2,1,0:T(8,128)(2,1)} %refs_0_.3), channel_id=1, source_target_pairs={{0,4},{1,5},{2,6},{3,7},{4,8},{5,9},{6,10},{7,11},{8,12},{9,13},{1... | collective-permute-start | bytes 1572872 | tf_op jit(solution)/shard_map/ppermute | solution.py:89
  5.0 0.0 copy-start
  5.0 1.1 %copy-done = bf16[1,2,128,1024]{3,2,1,0:T(8,128)(2,1)S(1)} copy-done((bf16[1,2,128,1024]{3,2,1,0:T(8,128)(2,1)S(1)}, bf16[1,2,128,1024]{3,2,1,0:T(8,128)(2,1)}, u32[]{:S(2)}) %copy-start) | copy-done | bytes 524312
  6.0 0.0 copy-start.1
  6.0 0.0 copy-start.2
  6.0 0.1 deal.1
  6.1 0.1 collective-permute-start.4
  6.2 0.8 %copy-done.1 = bf16[1,2,64,1024]{3,2,1,0:T(8,128)(2,1)S(1)} copy-done((bf16[1,2,64,1024]{3,2,1,0:T(8,128)(2,1)S(1)}, bf16[1,2,64,1024]{3,2,1,0:T(8,128)(2,1)}, u32[]{:S(2)}) %copy-start.1) | copy-done | bytes 262168
  7.0 0.1 copy-done.2
  7.0 0.1 cut.2
  7.1 1.6 %collective-permute-start = (bf16[256,256]{1,0:T(8,128)(2,1)S(1)}, bf16[256,256]{1,0:T(8,128)(2,1)S(1)}, u32[]{:S(2)}, u32[]{:S(2)}) collective-permute-start(bf16[256,256]{1,0:T(8,128)(2,1)S(1)} %get-tuple-element.34), channel_id=1, source_target_pairs={{0,2},{1,3},{2,0},{3,1},{4,6},{5,7},{6,4},{7,5},{8,10},{9,11},{10,... | collective-permute-start | bytes 393224 | tf_op jit(solution)/shard_map/ppermute | solution.py:84
  8.7 0.0 collective-permute-start.2
  8.7 4.0 %collective-permute-done.refs_2_.s2 = bf16[256,256]{1,0:T(8,128)(2,1)S(1)} collective-permute-done((bf16[256,256]{1,0:T(8,128)(2,1)S(1)}, bf16[256,256]{1,0:T(8,128)(2,1)S(1)}, u32[]{:S(2)}, u32[]{:S(2)}) %collective-permute-start) | collective-permute-done | bytes 131104 | tf_op jit(solution)/shard_map/ppermute | solution.py:84
  12.7 0.0 collective-permute-start.1
  12.8 0.0 collective-permute-done.4.near.refs_1_
  12.8 2.4 %collective-permute-start.5 = (bf16[512,256]{1,0:T(8,128)(2,1)S(1)}, bf16[512,256]{1,0:T(8,128)(2,1)S(1)}, u32[]{:S(2)}, u32[]{:S(2)}) collective-permute-start(bf16[512,256]{1,0:T(8,128)(2,1)S(1)} %pair.1), channel_id=1, source_target_pairs={{0,2},{1,3},{2,0},{3,1},{4,6},{5,7},{6,4},{7,5},{8,10},{9,11},{10,... | collective-permute-start | bytes 786440 | tf_op jit(solution)/shard_map/ppermute | solution.py:176
  15.2 0.0 collective-permute-done.2.refs_3_.s3
  15.2 0.0 collective-permute-done.1.refs_1_.s1
  15.3 2.6 %collective-permute-start.3 = (bf16[2,256,256]{2,1,0:T(8,128)(2,1)S(1)}, bf16[2,256,256]{2,1,0:T(8,128)(2,1)S(1)}, u32[]{:S(2)}, u32[]{:S(2)}) collective-permute-start(bf16[2,256,256]{2,1,0:T(8,128)(2,1)S(1)} %lay.1.own), channel_id=1, source_target_pairs={{0,8},{1,9},{2,10},{3,11},{8,0},{9,1},{10,2},{11,3},{4,12},{5,13},... | collective-permute-start | bytes 786440 | tf_op jit(solution)/shard_map/ppermute | solution.py:89
  17.9 0.0 collective-permute-done.6.refs_0_
  17.9 0.1 cut.3
  17.9 0.0 copy-start.3
  18.0 1.3 %collective-permute-start.7 = (bf16[256,256]{1,0:T(8,128)(2,1)S(1)}, bf16[256,256]{1,0:T(8,128)(2,1)S(1)}, u32[]{:S(2)}, u32[]{:S(2)}) collective-permute-start(bf16[256,256]{1,0:T(8,128)(2,1)S(1)} %get-tuple-element.44), channel_id=1, source_target_pairs={{0,2},{1,3},{2,0},{3,1},{4,6},{5,7},{6,4},{7,5},{8,10},{9,11},{10,... | collective-permute-start | bytes 393224 | tf_op jit(solution)/shard_map/ppermute | solution.py:84
  19.3 0.1 collective-permute-start.8
  19.3 1.1 %collective-permute-start.10 = (bf16[2,256,256]{2,1,0:T(8,128)(2,1)S(1)}, bf16[2,256,256]{2,1,0:T(8,128)(2,1)S(1)}, u32[]{:S(2)}, u32[]{:S(2)}) collective-permute-start(bf16[2,256,256]{2,1,0:T(8,128)(2,1)S(1)} %lay.1.own), channel_id=1, source_target_pairs={{0,4},{1,5},{2,6},{3,7},{4,0},{5,1},{6,2},{7,3},{8,12},{9,13},{10,... | collective-permute-start | bytes 786440 | tf_op jit(solution)/shard_map/ppermute | solution.py:89
  20.5 1.9 %collective-permute-done.5.refs_2_ = bf16[512,256]{1,0:T(8,128)(2,1)S(1)} collective-permute-done((bf16[512,256]{1,0:T(8,128)(2,1)S(1)}, bf16[512,256]{1,0:T(8,128)(2,1)S(1)}, u32[]{:S(2)}, u32[]{:S(2)}) %collective-permute-start.5) | collective-permute-done | bytes 262176 | tf_op jit(solution)/shard_map/ppermute | solution.py:176
  22.4 0.7 %collective-permute-start.11 = (bf16[2,256,256]{2,1,0:T(8,128)(2,1)S(1)}, bf16[2,256,256]{2,1,0:T(8,128)(2,1)S(1)}, u32[]{:S(2)}, u32[]{:S(2)}) collective-permute-start(bf16[2,256,256]{2,1,0:T(8,128)(2,1)S(1)} %lay.1.own), channel_id=1, source_target_pairs={{4,8},{5,9},{6,10},{7,11},{8,4},{9,5},{10,6},{11,7},{20,24},{21,25... | collective-permute-start | bytes 786440 | tf_op jit(solution)/shard_map/ppermute | solution.py:89
  23.0 0.0 copy-done.3
  23.1 1.8 %begin.1 = (bf16[4,128,512]{2,1,0:T(8,128)(2,1)S(1)}, f32[8,512]{1,0:T(8,128)S(1)}, f32[4,80,512]{2,1,0:T(8,128)S(1)}) custom-call(s32[1,12]{1,0:T(1,128)S(1)} %copy-done.3, bf16[256,256]{1,0:T(8,128)(2,1)S(1)} %get-tuple-element.32.refs_0_.s0, bf16[256,256]{1,0:T(8,128)(2,1)S(1)} %collective-permute-done.1.refs_1_.s1, ...), custom_call_target="tpu_custom_call" | custom-call | flops 134217728 | bytes 4194304 | tf_op jit(solution)/shard_map/begin/pallas_call | solution.py:293
  24.8 2.4 %suffix.2 = (f32[8,512]{1,0:T(8,128)S(1)}, f32[4,80,512]{2,1,0:T(8,128)S(1)}) custom-call(s32[1,12]{1,0:T(1,128)S(1)} %copy-done.3, bf16[4,128,512]{2,1,0:T(8,128)(2,1)S(1)} %get-tuple-element.37.qm.qm_in, f32[8,512]{1,0:T(8,128)S(1)} %get-tuple-element.38.top_in, f32[4,80,512]{2,1,0:T(8,128)S(1)} %get-tuple-element.39.acc_in, ...), custom_call_target="tpu_custom_call" | custom-call | flops 268435456 | bytes 3145728 | tf_op jit(solution)/shard_map/suffix/pallas_call | solution.py:362
  27.2 3.8 %collective-permute-done.3.refs_2_ = bf16[2,256,256]{2,1,0:T(8,128)(2,1)S(1)} collective-permute-done((bf16[2,256,256]{2,1,0:T(8,128)(2,1)S(1)}, bf16[2,256,256]{2,1,0:T(8,128)(2,1)S(1)}, u32[]{:S(2)}, u32[]{:S(2)}) %collective-permute-start.3) | collective-permute-done | bytes 262176 | tf_op jit(solution)/shard_map/ppermute | solution.py:89
  31.0 0.0 collective-permute-done.7.refs_2_
  31.0 0.0 collective-permute-done.8.refs_3_
  31.0 1.3 %collective-permute-start.12 = (bf16[2,256,256]{2,1,0:T(8,128)(2,1)S(1)}, bf16[2,256,256]{2,1,0:T(8,128)(2,1)S(1)}, u32[]{:S(2)}, u32[]{:S(2)}) collective-permute-start(bf16[2,256,256]{2,1,0:T(8,128)(2,1)S(1)} %collective-permute-done.3.refs_2_), channel_id=1, source_target_pairs={{8,12},{9,13},{10,14},{11,15},{4,0},{5,1},{6,2},{7,3},{24,28},{25,... | collective-permute-start | bytes 786440 | tf_op jit(solution)/shard_map/ppermute | solution.py:89
  32.3 0.1 collective-permute-start.9
  32.4 1.3 %collective-permute-done.9.refs_1_ = bf16[256,256]{1,0:T(8,128)(2,1)S(1)} collective-permute-done((bf16[256,256]{1,0:T(8,128)(2,1)S(1)}, bf16[256,256]{1,0:T(8,128)(2,1)S(1)}, u32[]{:S(2)}, u32[]{:S(2)}) %collective-permute-start.9) | collective-permute-done | bytes 131104 | tf_op jit(solution)/shard_map/ppermute | solution.py:84
  33.7 0.7 %suffix.3 = (f32[8,512]{1,0:T(8,128)S(1)}, f32[4,80,512]{2,1,0:T(8,128)S(1)}) custom-call(s32[1,12]{1,0:T(1,128)S(1)} %copy-done.3, bf16[4,128,512]{2,1,0:T(8,128)(2,1)S(1)} %get-tuple-element.37.qm.qm_in, f32[8,512]{1,0:T(8,128)S(1)} %get-tuple-element.46.top_in, f32[4,80,512]{2,1,0:T(8,128)S(1)} %get-tuple-element.47.acc_in, ...), custom_call_target="tpu_custom_call" | custom-call | flops 268435456 | bytes 3145728 | tf_op jit(solution)/shard_map/suffix/pallas_call | solution.py:362
  34.4 0.0 collective-permute-done.10.refs_0_
  34.4 0.0 collective-permute-done.11.refs_1_
  34.5 2.7 %prefix.1 = (f32[8,512]{1,0:T(8,128)S(1)}, f32[4,80,512]{2,1,0:T(8,128)S(1)}) custom-call(s32[1,12]{1,0:T(1,128)S(1)} %copy-done.3, bf16[4,128,512]{2,1,0:T(8,128)(2,1)S(1)} %get-tuple-element.37.qm.qm_in, f32[8,512]{1,0:T(8,128)S(1)} %get-tuple-element.50.top_in, f32[4,80,512]{2,1,0:T(8,128)S(1)} %get-tuple-element.51.acc_in, ...), custom_call_target="tpu_custom_call" | custom-call | flops 402653184 | bytes 3145728 | tf_op jit(solution)/shard_map/prefix/pallas_call | solution.py:362
  37.2 2.6 %collective-permute-done.12.refs_0_ = bf16[2,256,256]{2,1,0:T(8,128)(2,1)S(1)} collective-permute-done((bf16[2,256,256]{2,1,0:T(8,128)(2,1)S(1)}, bf16[2,256,256]{2,1,0:T(8,128)(2,1)S(1)}, u32[]{:S(2)}, u32[]{:S(2)}) %collective-permute-start.12) | collective-permute-done | bytes 262176 | tf_op jit(solution)/shard_map/ppermute | solution.py:89
  39.8 1.3 %last.3 = (bf16[128,256]{1,0:T(8,128)(2,1)S(1)}, bf16[128,256]{1,0:T(8,128)(2,1)S(1)}) custom-call(s32[1,12]{1,0:T(1,128)S(1)} %copy-done.3, bf16[4,128,512]{2,1,0:T(8,128)(2,1)S(1)} %get-tuple-element.37.qm.qm_in, f32[8,512]{1,0:T(8,128)S(1)} %get-tuple-element.53.top_in, f32[4,80,512]{2,1,0:T(8,128)S(1)} %get-tuple-element.54.acc_in, ...), custom_call_target="tpu_custom_call" | custom-call | flops 67108864 | bytes 2097152 | tf_op jit(solution)/shard_map/last/pallas_call | solution.py:393
  41.2 1.1 %collective-permute-start.14 = (bf16[128,256]{1,0:T(8,128)(2,1)S(1)}, bf16[128,256]{1,0:T(8,128)(2,1)S(1)}, u32[]{:S(2)}, u32[]{:S(2)}) collective-permute-start(bf16[128,256]{1,0:T(8,128)(2,1)S(1)} %get-tuple-element.57), channel_id=1, source_target_pairs={{0,2},{1,3},{2,0},{3,1},{4,6},{5,7},{6,4},{7,5},{8,10},{9,11},{10,... | collective-permute-start | bytes 196616 | tf_op jit(solution)/shard_map/ppermute | solution.py:84
  42.3 0.0 collective-permute-start.15
  42.3 1.3 %last.2 = (bf16[128,256]{1,0:T(8,128)(2,1)S(1)}, bf16[128,256]{1,0:T(8,128)(2,1)S(1)}) custom-call(s32[1,12]{1,0:T(1,128)S(1)} %copy-done.3, bf16[4,128,512]{2,1,0:T(8,128)(2,1)S(1)} %get-tuple-element.37.qm.qm_in, f32[8,512]{1,0:T(8,128)S(1)} %get-tuple-element.53.top_in, f32[4,80,512]{2,1,0:T(8,128)S(1)} %get-tuple-element.54.acc_in, ...), custom_call_target="tpu_custom_call" | custom-call | flops 67108864 | bytes 2097152 | tf_op jit(solution)/shard_map/last/pallas_call | solution.py:393
  43.6 1.1 %collective-permute-start.13 = (bf16[128,256]{1,0:T(8,128)(2,1)S(1)}, bf16[128,256]{1,0:T(8,128)(2,1)S(1)}, u32[]{:S(2)}, u32[]{:S(2)}) collective-permute-start(bf16[128,256]{1,0:T(8,128)(2,1)S(1)} %get-tuple-element.56), channel_id=1, source_target_pairs={{0,1},{1,0},{2,3},{3,2},{4,5},{5,4},{6,7},{7,6},{8,9},{9,8},{10,11... | collective-permute-start | bytes 196616 | tf_op jit(solution)/shard_map/ppermute | solution.py:84
  44.8 1.0 %collective-permute-done.14.s2 = bf16[128,256]{1,0:T(8,128)(2,1)S(1)} collective-permute-done((bf16[128,256]{1,0:T(8,128)(2,1)S(1)}, bf16[128,256]{1,0:T(8,128)(2,1)S(1)}, u32[]{:S(2)}, u32[]{:S(2)}) %collective-permute-start.14) | collective-permute-done | bytes 65568 | tf_op jit(solution)/shard_map/ppermute | solution.py:84
  45.8 0.9 %collective-permute-done.15.s3 = bf16[128,256]{1,0:T(8,128)(2,1)S(1)} collective-permute-done((bf16[128,256]{1,0:T(8,128)(2,1)S(1)}, bf16[128,256]{1,0:T(8,128)(2,1)S(1)}, u32[]{:S(2)}, u32[]{:S(2)}) %collective-permute-start.15) | collective-permute-done | bytes 65568 | tf_op jit(solution)/shard_map/ppermute | solution.py:84
  46.6 0.0 collective-permute-done.13.s1
  46.6 0.7 %join.1 = bf16[1,128,1024]{2,1,0:T(8,128)(2,1)} custom-call(bf16[128,256]{1,0:T(8,128)(2,1)S(1)} %get-tuple-element.55.s0, bf16[128,256]{1,0:T(8,128)(2,1)S(1)} %collective-permute-done.13.s1, bf16[128,256]{1,0:T(8,128)(2,1)S(1)} %collective-permute-done.14.s2, bf16[128,256]{1,0:T(8,128)(2,1)S(1)} %collective-permute-done.15.s3), custom_call_target="tpu_custom_call" | custom-call | bytes 524288 | tf_op jit(solution)/shard_map/join/pallas_call | solution.py:418
  (2 shorter events, 0.0 us)
Async XLA Ops:
  0.0 17.9 %collective-permute-start.6 = (bf16[1,2,128,1024]{3,2,1,0:T(8,128)(2,1)}, bf16[1,2,128,1024]{3,2,1,0:T(8,128)(2,1)S(1)}, u32[]{:S(2)}, u32[]{:S(2)}) collective-permute-start(bf16[1,2,128,1024]{3,2,1,0:T(8,128)(2,1)} %refs_0_.3), channel_id=1, source_target_pairs={{0,4},{1,5},{2,6},{3,7},{4,8},{5,9},{6,10},{7,11},{8,12},{9,13},{1... | collective-permute-start | bytes 1572872 | tf_op jit(solution)/shard_map/ppermute | solution.py:89
  5.0 1.1 %copy-start = (bf16[1,2,128,1024]{3,2,1,0:T(8,128)(2,1)S(1)}, bf16[1,2,128,1024]{3,2,1,0:T(8,128)(2,1)}, u32[]{:S(2)}) copy-start(bf16[1,2,128,1024]{3,2,1,0:T(8,128)(2,1)} %refs_0_.3) | copy-start | bytes 1572868
  6.0 0.9 %copy-start.1 = (bf16[1,2,64,1024]{3,2,1,0:T(8,128)(2,1)S(1)}, bf16[1,2,64,1024]{3,2,1,0:T(8,128)(2,1)}, u32[]{:S(2)}) copy-start(bf16[1,2,64,1024]{3,2,1,0:T(8,128)(2,1)} %refs_0_.2) | copy-start | bytes 786436
  6.0 1.0 %copy-start.2 = (bf16[1,128,1024]{2,1,0:T(8,128)(2,1)S(1)}, bf16[1,128,1024]{2,1,0:T(8,128)(2,1)}, u32[]{:S(2)}) copy-start(bf16[1,128,1024]{2,1,0:T(8,128)(2,1)} %param.4) | copy-start | bytes 786436
  6.1 6.7 %collective-permute-start.4 = (bf16[512,256]{1,0:T(8,128)(2,1)S(1)}, bf16[512,256]{1,0:T(8,128)(2,1)S(1)}, u32[]{:S(2)}, u32[]{:S(2)}) collective-permute-start(bf16[512,256]{1,0:T(8,128)(2,1)S(1)} %get-tuple-element.41), channel_id=1, source_target_pairs={{0,1},{1,0},{2,3},{3,2},{4,5},{5,4},{6,7},{7,6},{8,9},{9,8},{10,11... | collective-permute-start | bytes 786440 | tf_op jit(solution)/shard_map/ppermute | solution.py:164
  7.1 5.6 %collective-permute-start = (bf16[256,256]{1,0:T(8,128)(2,1)S(1)}, bf16[256,256]{1,0:T(8,128)(2,1)S(1)}, u32[]{:S(2)}, u32[]{:S(2)}) collective-permute-start(bf16[256,256]{1,0:T(8,128)(2,1)S(1)} %get-tuple-element.34), channel_id=1, source_target_pairs={{0,2},{1,3},{2,0},{3,1},{4,6},{5,7},{6,4},{7,5},{8,10},{9,11},{10,... | collective-permute-start | bytes 393224 | tf_op jit(solution)/shard_map/ppermute | solution.py:84
  8.7 6.5 %collective-permute-start.2 = (bf16[256,256]{1,0:T(8,128)(2,1)S(1)}, bf16[256,256]{1,0:T(8,128)(2,1)S(1)}, u32[]{:S(2)}, u32[]{:S(2)}) collective-permute-start(bf16[256,256]{1,0:T(8,128)(2,1)S(1)} %get-tuple-element.36), channel_id=1, source_target_pairs={{0,3},{1,2},{2,1},{3,0},{4,7},{5,6},{6,5},{7,4},{8,11},{9,10},{10,... | collective-permute-start | bytes 393224 | tf_op jit(solution)/shard_map/ppermute | solution.py:84
  12.7 2.5 %collective-permute-start.1 = (bf16[256,256]{1,0:T(8,128)(2,1)S(1)}, bf16[256,256]{1,0:T(8,128)(2,1)S(1)}, u32[]{:S(2)}, u32[]{:S(2)}) collective-permute-start(bf16[256,256]{1,0:T(8,128)(2,1)S(1)} %get-tuple-element.35), channel_id=1, source_target_pairs={{0,1},{1,0},{2,3},{3,2},{4,5},{5,4},{6,7},{7,6},{8,9},{9,8},{10,11... | collective-permute-start | bytes 393224 | tf_op jit(solution)/shard_map/ppermute | solution.py:84
  12.8 9.6 %collective-permute-start.5 = (bf16[512,256]{1,0:T(8,128)(2,1)S(1)}, bf16[512,256]{1,0:T(8,128)(2,1)S(1)}, u32[]{:S(2)}, u32[]{:S(2)}) collective-permute-start(bf16[512,256]{1,0:T(8,128)(2,1)S(1)} %pair.1), channel_id=1, source_target_pairs={{0,2},{1,3},{2,0},{3,1},{4,6},{5,7},{6,4},{7,5},{8,10},{9,11},{10,... | collective-permute-start | bytes 786440 | tf_op jit(solution)/shard_map/ppermute | solution.py:176
  15.3 15.8 %collective-permute-start.3 = (bf16[2,256,256]{2,1,0:T(8,128)(2,1)S(1)}, bf16[2,256,256]{2,1,0:T(8,128)(2,1)S(1)}, u32[]{:S(2)}, u32[]{:S(2)}) collective-permute-start(bf16[2,256,256]{2,1,0:T(8,128)(2,1)S(1)} %lay.1.own), channel_id=1, source_target_pairs={{0,8},{1,9},{2,10},{3,11},{8,0},{9,1},{10,2},{11,3},{4,12},{5,13},... | collective-permute-start | bytes 786440 | tf_op jit(solution)/shard_map/ppermute | solution.py:89
  17.9 5.1 %copy-start.3 = (s32[1,12]{1,0:T(1,128)S(1)}, s32[1,12]{1,0:T(1,128)}, u32[]{:S(2)}) copy-start(s32[1,12]{1,0:T(1,128)} %lens.11) | copy-start | bytes 148
  18.0 13.1 %collective-permute-start.7 = (bf16[256,256]{1,0:T(8,128)(2,1)S(1)}, bf16[256,256]{1,0:T(8,128)(2,1)S(1)}, u32[]{:S(2)}, u32[]{:S(2)}) collective-permute-start(bf16[256,256]{1,0:T(8,128)(2,1)S(1)} %get-tuple-element.44), channel_id=1, source_target_pairs={{0,2},{1,3},{2,0},{3,1},{4,6},{5,7},{6,4},{7,5},{8,10},{9,11},{10,... | collective-permute-start | bytes 393224 | tf_op jit(solution)/shard_map/ppermute | solution.py:84
  19.3 11.8 %collective-permute-start.8 = (bf16[256,256]{1,0:T(8,128)(2,1)S(1)}, bf16[256,256]{1,0:T(8,128)(2,1)S(1)}, u32[]{:S(2)}, u32[]{:S(2)}) collective-permute-start(bf16[256,256]{1,0:T(8,128)(2,1)S(1)} %get-tuple-element.45), channel_id=1, source_target_pairs={{0,3},{1,2},{2,1},{3,0},{4,7},{5,6},{6,5},{7,4},{8,11},{9,10},{10,... | collective-permute-start | bytes 393224 | tf_op jit(solution)/shard_map/ppermute | solution.py:84
  19.3 15.1 %collective-permute-start.10 = (bf16[2,256,256]{2,1,0:T(8,128)(2,1)S(1)}, bf16[2,256,256]{2,1,0:T(8,128)(2,1)S(1)}, u32[]{:S(2)}, u32[]{:S(2)}) collective-permute-start(bf16[2,256,256]{2,1,0:T(8,128)(2,1)S(1)} %lay.1.own), channel_id=1, source_target_pairs={{0,4},{1,5},{2,6},{3,7},{4,0},{5,1},{6,2},{7,3},{8,12},{9,13},{10,... | collective-permute-start | bytes 786440 | tf_op jit(solution)/shard_map/ppermute | solution.py:89
  22.4 12.1 %collective-permute-start.11 = (bf16[2,256,256]{2,1,0:T(8,128)(2,1)S(1)}, bf16[2,256,256]{2,1,0:T(8,128)(2,1)S(1)}, u32[]{:S(2)}, u32[]{:S(2)}) collective-permute-start(bf16[2,256,256]{2,1,0:T(8,128)(2,1)S(1)} %lay.1.own), channel_id=1, source_target_pairs={{4,8},{5,9},{6,10},{7,11},{8,4},{9,5},{10,6},{11,7},{20,24},{21,25... | collective-permute-start | bytes 786440 | tf_op jit(solution)/shard_map/ppermute | solution.py:89
  31.0 8.8 %collective-permute-start.12 = (bf16[2,256,256]{2,1,0:T(8,128)(2,1)S(1)}, bf16[2,256,256]{2,1,0:T(8,128)(2,1)S(1)}, u32[]{:S(2)}, u32[]{:S(2)}) collective-permute-start(bf16[2,256,256]{2,1,0:T(8,128)(2,1)S(1)} %collective-permute-done.3.refs_2_), channel_id=1, source_target_pairs={{8,12},{9,13},{10,14},{11,15},{4,0},{5,1},{6,2},{7,3},{24,28},{25,... | collective-permute-start | bytes 786440 | tf_op jit(solution)/shard_map/ppermute | solution.py:89
  32.3 1.4 %collective-permute-start.9 = (bf16[256,256]{1,0:T(8,128)(2,1)S(1)}, bf16[256,256]{1,0:T(8,128)(2,1)S(1)}, u32[]{:S(2)}, u32[]{:S(2)}) collective-permute-start(bf16[256,256]{1,0:T(8,128)(2,1)S(1)} %get-tuple-element.49), channel_id=1, source_target_pairs={{0,1},{1,0},{2,3},{3,2},{4,5},{5,4},{6,7},{7,6},{8,9},{9,8},{10,11... | collective-permute-start | bytes 393224 | tf_op jit(solution)/shard_map/ppermute | solution.py:84
  41.2 4.6 %collective-permute-start.14 = (bf16[128,256]{1,0:T(8,128)(2,1)S(1)}, bf16[128,256]{1,0:T(8,128)(2,1)S(1)}, u32[]{:S(2)}, u32[]{:S(2)}) collective-permute-start(bf16[128,256]{1,0:T(8,128)(2,1)S(1)} %get-tuple-element.57), channel_id=1, source_target_pairs={{0,2},{1,3},{2,0},{3,1},{4,6},{5,7},{6,4},{7,5},{8,10},{9,11},{10,... | collective-permute-start | bytes 196616 | tf_op jit(solution)/shard_map/ppermute | solution.py:84
  42.3 4.3 %collective-permute-start.15 = (bf16[128,256]{1,0:T(8,128)(2,1)S(1)}, bf16[128,256]{1,0:T(8,128)(2,1)S(1)}, u32[]{:S(2)}, u32[]{:S(2)}) collective-permute-start(bf16[128,256]{1,0:T(8,128)(2,1)S(1)} %get-tuple-element.58), channel_id=1, source_target_pairs={{0,3},{1,2},{2,1},{3,0},{4,7},{5,6},{6,5},{7,4},{8,11},{9,10},{10,... | collective-permute-start | bytes 196616 | tf_op jit(solution)/shard_map/ppermute | solution.py:84
  43.6 3.0 %collective-permute-start.13 = (bf16[128,256]{1,0:T(8,128)(2,1)S(1)}, bf16[128,256]{1,0:T(8,128)(2,1)S(1)}, u32[]{:S(2)}, u32[]{:S(2)}) collective-permute-start(bf16[128,256]{1,0:T(8,128)(2,1)S(1)} %get-tuple-element.56), channel_id=1, source_target_pairs={{0,1},{1,0},{2,3},{3,2},{4,5},{5,4},{6,7},{7,6},{8,9},{9,8},{10,11... | collective-permute-start | bytes 196616 | tf_op jit(solution)/shard_map/ppermute | solution.py:84

commit v7 on v6

--- a/solution.py
+++ b/solution.py
@@ -341,12 +341,12 @@
 
 
 def last_kernel(sources, other, lens, qm_in, top_in, acc_in, *refs):
-    *refs, straight, cross, qm, top, acc, turned = refs
+    *refs, straight, cross, top, acc, turned = refs
     block, sub = place()
     half = top.shape[1]
     at = jnp.bitwise_xor(sub // 2, other) * half
     cols = pl.ds(pl.multiple_of(at, half), half)
-    qm[...] = qm_in[:, :, cols]
+    qm = qm_in.at[:, :, cols]
     top[...] = top_in[:, cols]
     acc[...] = acc_in[:, :, cols]
     pieces_step(sources, lens, qm, top, acc, refs, block * 2 * half + at)
@@ -396,7 +396,6 @@
         in_specs=[pl.BlockSpec(memory_space=pltpu.SMEM)] + vmem(3 + len(pieces)),
         out_specs=vmem(2),
         scratch_shapes=[
-            pltpu.VMEM((MINE, 2 * HEAD, half), BF16),
             pltpu.VMEM((8, half), F32),
             pltpu.VMEM((MINE, ROWS, half), F32),
             pltpu.VMEM((half, WIDE), BF16),

time: 47.6 us -> 47.6 us (level)
  no operation moved by 1% of the time
where the time goes in v7:
time: 47.6 us; the launch traced here: 47.3 us
  starting transfers between devices  18.4 us (39%)
  waiting for transfers between devices  15.6 us (33%)
  Pallas kernels  11.2 us (24%)
  local copies, waits for them, and re-layouts  1.94 us (4%)
    ppermute x5, starting transfers between devices, between(): lax.ppermute(block, 'req', [(SUB * a + s, SUB * b + s) for a, b in routes...  10.6 us
    ppermute x9, waiting for transfers between devices, exchange(): lax.ppermute(slab, 'req', [(i, i ^ distance) for i in range(count)])  7.27 us
    ppermute x5, waiting for transfers between devices, between(): lax.ppermute(block, 'req', [(SUB * a + s, SUB * b + s) for a, b in routes...  6.46 us
    pallas_call x3, Pallas kernels, carry_call(): pl.pallas_call(kernel, out_shape=[jax.ShapeDtypeStruct(a.shape, a.dtype)...  5.83 us
    ppermute x9, starting transfers between devices, exchange(): lax.ppermute(slab, 'req', [(i, i ^ distance) for i in range(count)])  5.29 us
    pallas_call x2, Pallas kernels, finish(): pl.pallas_call(functools.partial(last_kernel, [p[1] for p in pieces], oth...  2.62 us
    ppermute x1, starting transfers between devices, trade(): lax.ppermute(far, 'req', [(i, i ^ 2) for i in range(count)])  2.44 us
    unnamed x8, local copies, waits for them, and re-layouts  1.94 us
  transfers between devices with their start and end apart: 16, of which 7 were waited for; matrix products, arithmetic and copies ran while one was open for 0% of the time, Pallas kernels for 19%

profile of v7, /device:TPU:0, one launch (start us, length us, event | category | flops | bytes accessed | tf_op | source)
XLA Modules:
  0.0 47.3 jit_solution(2981064340274045634)
XLA Ops:
  0.0 4.9 %collective-permute-start.6 = (bf16[1,2,128,1024]{3,2,1,0:T(8,128)(2,1)}, bf16[1,2,128,1024]{3,2,1,0:T(8,128)(2,1)S(1)}, u32[]{:S(2)}, u32[]{:S(2)}) collective-permute-start(bf16[1,2,128,1024]{3,2,1,0:T(8,128)(2,1)} %refs_0_.3), channel_id=1, source_target_pairs={{0,4},{1,5},{2,6},{3,7},{4,8},{5,9},{6,10},{7,11},{8,12},{9,13},{1... | collective-permute-start | bytes 1572872 | tf_op jit(solution)/shard_map/ppermute | solution.py:89
  5.0 0.0 copy-start
  5.0 1.1 %copy-done = bf16[1,2,128,1024]{3,2,1,0:T(8,128)(2,1)S(1)} copy-done((bf16[1,2,128,1024]{3,2,1,0:T(8,128)(2,1)S(1)}, bf16[1,2,128,1024]{3,2,1,0:T(8,128)(2,1)}, u32[]{:S(2)}) %copy-start) | copy-done | bytes 524312
  6.0 0.0 copy-start.1
  6.0 0.0 copy-start.2
  6.0 0.1 deal.1
  6.1 0.1 collective-permute-start.4
  6.2 0.8 %copy-done.1 = bf16[1,2,64,1024]{3,2,1,0:T(8,128)(2,1)S(1)} copy-done((bf16[1,2,64,1024]{3,2,1,0:T(8,128)(2,1)S(1)}, bf16[1,2,64,1024]{3,2,1,0:T(8,128)(2,1)}, u32[]{:S(2)}) %copy-start.1) | copy-done | bytes 262168
  7.0 0.1 copy-done.2
  7.0 0.1 cut.2
  7.1 1.6 %collective-permute-start = (bf16[256,256]{1,0:T(8,128)(2,1)S(1)}, bf16[256,256]{1,0:T(8,128)(2,1)S(1)}, u32[]{:S(2)}, u32[]{:S(2)}) collective-permute-start(bf16[256,256]{1,0:T(8,128)(2,1)S(1)} %get-tuple-element.34), channel_id=1, source_target_pairs={{0,2},{1,3},{2,0},{3,1},{4,6},{5,7},{6,4},{7,5},{8,10},{9,11},{10,... | collective-permute-start | bytes 393224 | tf_op jit(solution)/shard_map/ppermute | solution.py:84
  8.7 0.0 collective-permute-start.2
  8.7 4.0 %collective-permute-done.refs_2_.s2 = bf16[256,256]{1,0:T(8,128)(2,1)S(1)} collective-permute-done((bf16[256,256]{1,0:T(8,128)(2,1)S(1)}, bf16[256,256]{1,0:T(8,128)(2,1)S(1)}, u32[]{:S(2)}, u32[]{:S(2)}) %collective-permute-start) | collective-permute-done | bytes 131104 | tf_op jit(solution)/shard_map/ppermute | solution.py:84
  12.7 0.0 collective-permute-start.1
  12.8 0.0 collective-permute-done.4.near.refs_1_
  12.8 2.4 %collective-permute-start.5 = (bf16[512,256]{1,0:T(8,128)(2,1)S(1)}, bf16[512,256]{1,0:T(8,128)(2,1)S(1)}, u32[]{:S(2)}, u32[]{:S(2)}) collective-permute-start(bf16[512,256]{1,0:T(8,128)(2,1)S(1)} %pair.1), channel_id=1, source_target_pairs={{0,2},{1,3},{2,0},{3,1},{4,6},{5,7},{6,4},{7,5},{8,10},{9,11},{10,... | collective-permute-start | bytes 786440 | tf_op jit(solution)/shard_map/ppermute | solution.py:176
  15.2 0.0 collective-permute-done.2.refs_3_.s3
  15.2 0.0 collective-permute-done.1.refs_1_.s1
  15.3 2.6 %collective-permute-start.3 = (bf16[2,256,256]{2,1,0:T(8,128)(2,1)S(1)}, bf16[2,256,256]{2,1,0:T(8,128)(2,1)S(1)}, u32[]{:S(2)}, u32[]{:S(2)}) collective-permute-start(bf16[2,256,256]{2,1,0:T(8,128)(2,1)S(1)} %lay.1.own), channel_id=1, source_target_pairs={{0,8},{1,9},{2,10},{3,11},{8,0},{9,1},{10,2},{11,3},{4,12},{5,13},... | collective-permute-start | bytes 786440 | tf_op jit(solution)/shard_map/ppermute | solution.py:89
  17.9 0.0 collective-permute-done.6.refs_0_
  17.9 0.1 cut.3
  17.9 0.0 copy-start.3
  18.0 1.3 %collective-permute-start.7 = (bf16[256,256]{1,0:T(8,128)(2,1)S(1)}, bf16[256,256]{1,0:T(8,128)(2,1)S(1)}, u32[]{:S(2)}, u32[]{:S(2)}) collective-permute-start(bf16[256,256]{1,0:T(8,128)(2,1)S(1)} %get-tuple-element.44), channel_id=1, source_target_pairs={{0,2},{1,3},{2,0},{3,1},{4,6},{5,7},{6,4},{7,5},{8,10},{9,11},{10,... | collective-permute-start | bytes 393224 | tf_op jit(solution)/shard_map/ppermute | solution.py:84
  19.3 0.1 collective-permute-start.8
  19.3 1.1 %collective-permute-start.10 = (bf16[2,256,256]{2,1,0:T(8,128)(2,1)S(1)}, bf16[2,256,256]{2,1,0:T(8,128)(2,1)S(1)}, u32[]{:S(2)}, u32[]{:S(2)}) collective-permute-start(bf16[2,256,256]{2,1,0:T(8,128)(2,1)S(1)} %lay.1.own), channel_id=1, source_target_pairs={{0,4},{1,5},{2,6},{3,7},{4,0},{5,1},{6,2},{7,3},{8,12},{9,13},{10,... | collective-permute-start | bytes 786440 | tf_op jit(solution)/shard_map/ppermute | solution.py:89
  20.5 1.9 %collective-permute-done.5.refs_2_ = bf16[512,256]{1,0:T(8,128)(2,1)S(1)} collective-permute-done((bf16[512,256]{1,0:T(8,128)(2,1)S(1)}, bf16[512,256]{1,0:T(8,128)(2,1)S(1)}, u32[]{:S(2)}, u32[]{:S(2)}) %collective-permute-start.5) | collective-permute-done | bytes 262176 | tf_op jit(solution)/shard_map/ppermute | solution.py:176
  22.4 0.7 %collective-permute-start.11 = (bf16[2,256,256]{2,1,0:T(8,128)(2,1)S(1)}, bf16[2,256,256]{2,1,0:T(8,128)(2,1)S(1)}, u32[]{:S(2)}, u32[]{:S(2)}) collective-permute-start(bf16[2,256,256]{2,1,0:T(8,128)(2,1)S(1)} %lay.1.own), channel_id=1, source_target_pairs={{4,8},{5,9},{6,10},{7,11},{8,4},{9,5},{10,6},{11,7},{20,24},{21,25... | collective-permute-start | bytes 786440 | tf_op jit(solution)/shard_map/ppermute | solution.py:89
  23.0 0.0 copy-done.3
  23.1 1.8 %begin.1 = (bf16[4,128,512]{2,1,0:T(8,128)(2,1)S(1)}, f32[8,512]{1,0:T(8,128)S(1)}, f32[4,80,512]{2,1,0:T(8,128)S(1)}) custom-call(s32[1,12]{1,0:T(1,128)S(1)} %copy-done.3, bf16[256,256]{1,0:T(8,128)(2,1)S(1)} %get-tuple-element.32.refs_0_.s0, bf16[256,256]{1,0:T(8,128)(2,1)S(1)} %collective-permute-done.1.refs_1_.s1, ...), custom_call_target="tpu_custom_call" | custom-call | flops 134217728 | bytes 4194304 | tf_op jit(solution)/shard_map/begin/pallas_call | solution.py:293
  24.8 2.4 %suffix.2 = (f32[8,512]{1,0:T(8,128)S(1)}, f32[4,80,512]{2,1,0:T(8,128)S(1)}) custom-call(s32[1,12]{1,0:T(1,128)S(1)} %copy-done.3, bf16[4,128,512]{2,1,0:T(8,128)(2,1)S(1)} %get-tuple-element.37.qm.qm_in, f32[8,512]{1,0:T(8,128)S(1)} %get-tuple-element.38.top_in, f32[4,80,512]{2,1,0:T(8,128)S(1)} %get-tuple-element.39.acc_in, ...), custom_call_target="tpu_custom_call" | custom-call | flops 268435456 | bytes 3145728 | tf_op jit(solution)/shard_map/suffix/pallas_call | solution.py:362
  27.2 3.8 %collective-permute-done.3.refs_2_ = bf16[2,256,256]{2,1,0:T(8,128)(2,1)S(1)} collective-permute-done((bf16[2,256,256]{2,1,0:T(8,128)(2,1)S(1)}, bf16[2,256,256]{2,1,0:T(8,128)(2,1)S(1)}, u32[]{:S(2)}, u32[]{:S(2)}) %collective-permute-start.3) | collective-permute-done | bytes 262176 | tf_op jit(solution)/shard_map/ppermute | solution.py:89
  31.0 0.0 collective-permute-done.7.refs_2_
  31.0 0.0 collective-permute-done.8.refs_3_
  31.0 1.3 %collective-permute-start.12 = (bf16[2,256,256]{2,1,0:T(8,128)(2,1)S(1)}, bf16[2,256,256]{2,1,0:T(8,128)(2,1)S(1)}, u32[]{:S(2)}, u32[]{:S(2)}) collective-permute-start(bf16[2,256,256]{2,1,0:T(8,128)(2,1)S(1)} %collective-permute-done.3.refs_2_), channel_id=1, source_target_pairs={{8,12},{9,13},{10,14},{11,15},{4,0},{5,1},{6,2},{7,3},{24,28},{25,... | collective-permute-start | bytes 786440 | tf_op jit(solution)/shard_map/ppermute | solution.py:89
  32.3 0.1 collective-permute-start.9
  32.4 1.3 %collective-permute-done.9.refs_1_ = bf16[256,256]{1,0:T(8,128)(2,1)S(1)} collective-permute-done((bf16[256,256]{1,0:T(8,128)(2,1)S(1)}, bf16[256,256]{1,0:T(8,128)(2,1)S(1)}, u32[]{:S(2)}, u32[]{:S(2)}) %collective-permute-start.9) | collective-permute-done | bytes 131104 | tf_op jit(solution)/shard_map/ppermute | solution.py:84
  33.7 0.7 %suffix.3 = (f32[8,512]{1,0:T(8,128)S(1)}, f32[4,80,512]{2,1,0:T(8,128)S(1)}) custom-call(s32[1,12]{1,0:T(1,128)S(1)} %copy-done.3, bf16[4,128,512]{2,1,0:T(8,128)(2,1)S(1)} %get-tuple-element.37.qm.qm_in, f32[8,512]{1,0:T(8,128)S(1)} %get-tuple-element.46.top_in, f32[4,80,512]{2,1,0:T(8,128)S(1)} %get-tuple-element.47.acc_in, ...), custom_call_target="tpu_custom_call" | custom-call | flops 268435456 | bytes 3145728 | tf_op jit(solution)/shard_map/suffix/pallas_call | solution.py:362
  34.4 0.0 collective-permute-done.10.refs_0_
  34.4 0.0 collective-permute-done.11.refs_1_
  34.5 2.7 %prefix.1 = (f32[8,512]{1,0:T(8,128)S(1)}, f32[4,80,512]{2,1,0:T(8,128)S(1)}) custom-call(s32[1,12]{1,0:T(1,128)S(1)} %copy-done.3, bf16[4,128,512]{2,1,0:T(8,128)(2,1)S(1)} %get-tuple-element.37.qm.qm_in, f32[8,512]{1,0:T(8,128)S(1)} %get-tuple-element.50.top_in, f32[4,80,512]{2,1,0:T(8,128)S(1)} %get-tuple-element.51.acc_in, ...), custom_call_target="tpu_custom_call" | custom-call | flops 402653184 | bytes 3145728 | tf_op jit(solution)/shard_map/prefix/pallas_call | solution.py:362
  37.2 2.6 %collective-permute-done.12.refs_0_ = bf16[2,256,256]{2,1,0:T(8,128)(2,1)S(1)} collective-permute-done((bf16[2,256,256]{2,1,0:T(8,128)(2,1)S(1)}, bf16[2,256,256]{2,1,0:T(8,128)(2,1)S(1)}, u32[]{:S(2)}, u32[]{:S(2)}) %collective-permute-start.12) | collective-permute-done | bytes 262176 | tf_op jit(solution)/shard_map/ppermute | solution.py:89
  39.8 1.3 %last.3 = (bf16[128,256]{1,0:T(8,128)(2,1)S(1)}, bf16[128,256]{1,0:T(8,128)(2,1)S(1)}) custom-call(s32[1,12]{1,0:T(1,128)S(1)} %copy-done.3, bf16[4,128,512]{2,1,0:T(8,128)(2,1)S(1)} %get-tuple-element.37.qm.qm_in, f32[8,512]{1,0:T(8,128)S(1)} %get-tuple-element.53.top_in, f32[4,80,512]{2,1,0:T(8,128)S(1)} %get-tuple-element.54.acc_in, ...), custom_call_target="tpu_custom_call" | custom-call | flops 67108864 | bytes 2097152 | tf_op jit(solution)/shard_map/last/pallas_call | solution.py:393
  41.1 1.1 %collective-permute-start.14 = (bf16[128,256]{1,0:T(8,128)(2,1)S(1)}, bf16[128,256]{1,0:T(8,128)(2,1)S(1)}, u32[]{:S(2)}, u32[]{:S(2)}) collective-permute-start(bf16[128,256]{1,0:T(8,128)(2,1)S(1)} %get-tuple-element.57), channel_id=1, source_target_pairs={{0,2},{1,3},{2,0},{3,1},{4,6},{5,7},{6,4},{7,5},{8,10},{9,11},{10,... | collective-permute-start | bytes 196616 | tf_op jit(solution)/shard_map/ppermute | solution.py:84
  42.3 0.0 collective-permute-start.15
  42.3 1.3 %last.2 = (bf16[128,256]{1,0:T(8,128)(2,1)S(1)}, bf16[128,256]{1,0:T(8,128)(2,1)S(1)}) custom-call(s32[1,12]{1,0:T(1,128)S(1)} %copy-done.3, bf16[4,128,512]{2,1,0:T(8,128)(2,1)S(1)} %get-tuple-element.37.qm.qm_in, f32[8,512]{1,0:T(8,128)S(1)} %get-tuple-element.53.top_in, f32[4,80,512]{2,1,0:T(8,128)S(1)} %get-tuple-element.54.acc_in, ...), custom_call_target="tpu_custom_call" | custom-call | flops 67108864 | bytes 2097152 | tf_op jit(solution)/shard_map/last/pallas_call | solution.py:393
  43.6 1.1 %collective-permute-start.13 = (bf16[128,256]{1,0:T(8,128)(2,1)S(1)}, bf16[128,256]{1,0:T(8,128)(2,1)S(1)}, u32[]{:S(2)}, u32[]{:S(2)}) collective-permute-start(bf16[128,256]{1,0:T(8,128)(2,1)S(1)} %get-tuple-element.56), channel_id=1, source_target_pairs={{0,1},{1,0},{2,3},{3,2},{4,5},{5,4},{6,7},{7,6},{8,9},{9,8},{10,11... | collective-permute-start | bytes 196616 | tf_op jit(solution)/shard_map/ppermute | solution.py:84
  44.7 1.0 %collective-permute-done.14.s2 = bf16[128,256]{1,0:T(8,128)(2,1)S(1)} collective-permute-done((bf16[128,256]{1,0:T(8,128)(2,1)S(1)}, bf16[128,256]{1,0:T(8,128)(2,1)S(1)}, u32[]{:S(2)}, u32[]{:S(2)}) %collective-permute-start.14) | collective-permute-done | bytes 65568 | tf_op jit(solution)/shard_map/ppermute | solution.py:84
  45.7 0.9 %collective-permute-done.15.s3 = bf16[128,256]{1,0:T(8,128)(2,1)S(1)} collective-permute-done((bf16[128,256]{1,0:T(8,128)(2,1)S(1)}, bf16[128,256]{1,0:T(8,128)(2,1)S(1)}, u32[]{:S(2)}, u32[]{:S(2)}) %collective-permute-start.15) | collective-permute-done | bytes 65568 | tf_op jit(solution)/shard_map/ppermute | solution.py:84
  46.6 0.0 collective-permute-done.13.s1
  46.6 0.7 %join.1 = bf16[1,128,1024]{2,1,0:T(8,128)(2,1)} custom-call(bf16[128,256]{1,0:T(8,128)(2,1)S(1)} %get-tuple-element.55.s0, bf16[128,256]{1,0:T(8,128)(2,1)S(1)} %collective-permute-done.13.s1, bf16[128,256]{1,0:T(8,128)(2,1)S(1)} %collective-permute-done.14.s2, bf16[128,256]{1,0:T(8,128)(2,1)S(1)} %collective-permute-done.15.s3), custom_call_target="tpu_custom_call" | custom-call | bytes 524288 | tf_op jit(solution)/shard_map/join/pallas_call | solution.py:417
  (2 shorter events, 0.0 us)
Async XLA Ops:
  0.0 17.9 %collective-permute-start.6 = (bf16[1,2,128,1024]{3,2,1,0:T(8,128)(2,1)}, bf16[1,2,128,1024]{3,2,1,0:T(8,128)(2,1)S(1)}, u32[]{:S(2)}, u32[]{:S(2)}) collective-permute-start(bf16[1,2,128,1024]{3,2,1,0:T(8,128)(2,1)} %refs_0_.3), channel_id=1, source_target_pairs={{0,4},{1,5},{2,6},{3,7},{4,8},{5,9},{6,10},{7,11},{8,12},{9,13},{1... | collective-permute-start | bytes 1572872 | tf_op jit(solution)/shard_map/ppermute | solution.py:89
  5.0 1.1 %copy-start = (bf16[1,2,128,1024]{3,2,1,0:T(8,128)(2,1)S(1)}, bf16[1,2,128,1024]{3,2,1,0:T(8,128)(2,1)}, u32[]{:S(2)}) copy-start(bf16[1,2,128,1024]{3,2,1,0:T(8,128)(2,1)} %refs_0_.3) | copy-start | bytes 1572868
  6.0 0.9 %copy-start.1 = (bf16[1,2,64,1024]{3,2,1,0:T(8,128)(2,1)S(1)}, bf16[1,2,64,1024]{3,2,1,0:T(8,128)(2,1)}, u32[]{:S(2)}) copy-start(bf16[1,2,64,1024]{3,2,1,0:T(8,128)(2,1)} %refs_0_.2) | copy-start | bytes 786436
  6.0 1.0 %copy-start.2 = (bf16[1,128,1024]{2,1,0:T(8,128)(2,1)S(1)}, bf16[1,128,1024]{2,1,0:T(8,128)(2,1)}, u32[]{:S(2)}) copy-start(bf16[1,128,1024]{2,1,0:T(8,128)(2,1)} %param.4) | copy-start | bytes 786436
  6.1 6.7 %collective-permute-start.4 = (bf16[512,256]{1,0:T(8,128)(2,1)S(1)}, bf16[512,256]{1,0:T(8,128)(2,1)S(1)}, u32[]{:S(2)}, u32[]{:S(2)}) collective-permute-start(bf16[512,256]{1,0:T(8,128)(2,1)S(1)} %get-tuple-element.41), channel_id=1, source_target_pairs={{0,1},{1,0},{2,3},{3,2},{4,5},{5,4},{6,7},{7,6},{8,9},{9,8},{10,11... | collective-permute-start | bytes 786440 | tf_op jit(solution)/shard_map/ppermute | solution.py:164
  7.1 5.6 %collective-permute-start = (bf16[256,256]{1,0:T(8,128)(2,1)S(1)}, bf16[256,256]{1,0:T(8,128)(2,1)S(1)}, u32[]{:S(2)}, u32[]{:S(2)}) collective-permute-start(bf16[256,256]{1,0:T(8,128)(2,1)S(1)} %get-tuple-element.34), channel_id=1, source_target_pairs={{0,2},{1,3},{2,0},{3,1},{4,6},{5,7},{6,4},{7,5},{8,10},{9,11},{10,... | collective-permute-start | bytes 393224 | tf_op jit(solution)/shard_map/ppermute | solution.py:84
  8.7 6.5 %collective-permute-start.2 = (bf16[256,256]{1,0:T(8,128)(2,1)S(1)}, bf16[256,256]{1,0:T(8,128)(2,1)S(1)}, u32[]{:S(2)}, u32[]{:S(2)}) collective-permute-start(bf16[256,256]{1,0:T(8,128)(2,1)S(1)} %get-tuple-element.36), channel_id=1, source_target_pairs={{0,3},{1,2},{2,1},{3,0},{4,7},{5,6},{6,5},{7,4},{8,11},{9,10},{10,... | collective-permute-start | bytes 393224 | tf_op jit(solution)/shard_map/ppermute | solution.py:84
  12.7 2.5 %collective-permute-start.1 = (bf16[256,256]{1,0:T(8,128)(2,1)S(1)}, bf16[256,256]{1,0:T(8,128)(2,1)S(1)}, u32[]{:S(2)}, u32[]{:S(2)}) collective-permute-start(bf16[256,256]{1,0:T(8,128)(2,1)S(1)} %get-tuple-element.35), channel_id=1, source_target_pairs={{0,1},{1,0},{2,3},{3,2},{4,5},{5,4},{6,7},{7,6},{8,9},{9,8},{10,11... | collective-permute-start | bytes 393224 | tf_op jit(solution)/shard_map/ppermute | solution.py:84
  12.8 9.6 %collective-permute-start.5 = (bf16[512,256]{1,0:T(8,128)(2,1)S(1)}, bf16[512,256]{1,0:T(8,128)(2,1)S(1)}, u32[]{:S(2)}, u32[]{:S(2)}) collective-permute-start(bf16[512,256]{1,0:T(8,128)(2,1)S(1)} %pair.1), channel_id=1, source_target_pairs={{0,2},{1,3},{2,0},{3,1},{4,6},{5,7},{6,4},{7,5},{8,10},{9,11},{10,... | collective-permute-start | bytes 786440 | tf_op jit(solution)/shard_map/ppermute | solution.py:176
  15.3 15.8 %collective-permute-start.3 = (bf16[2,256,256]{2,1,0:T(8,128)(2,1)S(1)}, bf16[2,256,256]{2,1,0:T(8,128)(2,1)S(1)}, u32[]{:S(2)}, u32[]{:S(2)}) collective-permute-start(bf16[2,256,256]{2,1,0:T(8,128)(2,1)S(1)} %lay.1.own), channel_id=1, source_target_pairs={{0,8},{1,9},{2,10},{3,11},{8,0},{9,1},{10,2},{11,3},{4,12},{5,13},... | collective-permute-start | bytes 786440 | tf_op jit(solution)/shard_map/ppermute | solution.py:89
  17.9 5.1 %copy-start.3 = (s32[1,12]{1,0:T(1,128)S(1)}, s32[1,12]{1,0:T(1,128)}, u32[]{:S(2)}) copy-start(s32[1,12]{1,0:T(1,128)} %lens.11) | copy-start | bytes 148
  18.0 13.1 %collective-permute-start.7 = (bf16[256,256]{1,0:T(8,128)(2,1)S(1)}, bf16[256,256]{1,0:T(8,128)(2,1)S(1)}, u32[]{:S(2)}, u32[]{:S(2)}) collective-permute-start(bf16[256,256]{1,0:T(8,128)(2,1)S(1)} %get-tuple-element.44), channel_id=1, source_target_pairs={{0,2},{1,3},{2,0},{3,1},{4,6},{5,7},{6,4},{7,5},{8,10},{9,11},{10,... | collective-permute-start | bytes 393224 | tf_op jit(solution)/shard_map/ppermute | solution.py:84
  19.3 11.8 %collective-permute-start.8 = (bf16[256,256]{1,0:T(8,128)(2,1)S(1)}, bf16[256,256]{1,0:T(8,128)(2,1)S(1)}, u32[]{:S(2)}, u32[]{:S(2)}) collective-permute-start(bf16[256,256]{1,0:T(8,128)(2,1)S(1)} %get-tuple-element.45), channel_id=1, source_target_pairs={{0,3},{1,2},{2,1},{3,0},{4,7},{5,6},{6,5},{7,4},{8,11},{9,10},{10,... | collective-permute-start | bytes 393224 | tf_op jit(solution)/shard_map/ppermute | solution.py:84
  19.3 15.1 %collective-permute-start.10 = (bf16[2,256,256]{2,1,0:T(8,128)(2,1)S(1)}, bf16[2,256,256]{2,1,0:T(8,128)(2,1)S(1)}, u32[]{:S(2)}, u32[]{:S(2)}) collective-permute-start(bf16[2,256,256]{2,1,0:T(8,128)(2,1)S(1)} %lay.1.own), channel_id=1, source_target_pairs={{0,4},{1,5},{2,6},{3,7},{4,0},{5,1},{6,2},{7,3},{8,12},{9,13},{10,... | collective-permute-start | bytes 786440 | tf_op jit(solution)/shard_map/ppermute | solution.py:89
  22.4 12.1 %collective-permute-start.11 = (bf16[2,256,256]{2,1,0:T(8,128)(2,1)S(1)}, bf16[2,256,256]{2,1,0:T(8,128)(2,1)S(1)}, u32[]{:S(2)}, u32[]{:S(2)}) collective-permute-start(bf16[2,256,256]{2,1,0:T(8,128)(2,1)S(1)} %lay.1.own), channel_id=1, source_target_pairs={{4,8},{5,9},{6,10},{7,11},{8,4},{9,5},{10,6},{11,7},{20,24},{21,25... | collective-permute-start | bytes 786440 | tf_op jit(solution)/shard_map/ppermute | solution.py:89
  31.0 8.8 %collective-permute-start.12 = (bf16[2,256,256]{2,1,0:T(8,128)(2,1)S(1)}, bf16[2,256,256]{2,1,0:T(8,128)(2,1)S(1)}, u32[]{:S(2)}, u32[]{:S(2)}) collective-permute-start(bf16[2,256,256]{2,1,0:T(8,128)(2,1)S(1)} %collective-permute-done.3.refs_2_), channel_id=1, source_target_pairs={{8,12},{9,13},{10,14},{11,15},{4,0},{5,1},{6,2},{7,3},{24,28},{25,... | collective-permute-start | bytes 786440 | tf_op jit(solution)/shard_map/ppermute | solution.py:89
  32.3 1.4 %collective-permute-start.9 = (bf16[256,256]{1,0:T(8,128)(2,1)S(1)}, bf16[256,256]{1,0:T(8,128)(2,1)S(1)}, u32[]{:S(2)}, u32[]{:S(2)}) collective-permute-start(bf16[256,256]{1,0:T(8,128)(2,1)S(1)} %get-tuple-element.49), channel_id=1, source_target_pairs={{0,1},{1,0},{2,3},{3,2},{4,5},{5,4},{6,7},{7,6},{8,9},{9,8},{10,11... | collective-permute-start | bytes 393224 | tf_op jit(solution)/shard_map/ppermute | solution.py:84
  41.1 4.6 %collective-permute-start.14 = (bf16[128,256]{1,0:T(8,128)(2,1)S(1)}, bf16[128,256]{1,0:T(8,128)(2,1)S(1)}, u32[]{:S(2)}, u32[]{:S(2)}) collective-permute-start(bf16[128,256]{1,0:T(8,128)(2,1)S(1)} %get-tuple-element.57), channel_id=1, source_target_pairs={{0,2},{1,3},{2,0},{3,1},{4,6},{5,7},{6,4},{7,5},{8,10},{9,11},{10,... | collective-permute-start | bytes 196616 | tf_op jit(solution)/shard_map/ppermute | solution.py:84
  42.3 4.3 %collective-permute-start.15 = (bf16[128,256]{1,0:T(8,128)(2,1)S(1)}, bf16[128,256]{1,0:T(8,128)(2,1)S(1)}, u32[]{:S(2)}, u32[]{:S(2)}) collective-permute-start(bf16[128,256]{1,0:T(8,128)(2,1)S(1)} %get-tuple-element.58), channel_id=1, source_target_pairs={{0,3},{1,2},{2,1},{3,0},{4,7},{5,6},{6,5},{7,4},{8,11},{9,10},{10,... | collective-permute-start | bytes 196616 | tf_op jit(solution)/shard_map/ppermute | solution.py:84
  43.6 3.0 %collective-permute-start.13 = (bf16[128,256]{1,0:T(8,128)(2,1)S(1)}, bf16[128,256]{1,0:T(8,128)(2,1)S(1)}, u32[]{:S(2)}, u32[]{:S(2)}) collective-permute-start(bf16[128,256]{1,0:T(8,128)(2,1)S(1)} %get-tuple-element.56), channel_id=1, source_target_pairs={{0,1},{1,0},{2,3},{3,2},{4,5},{5,4},{6,7},{7,6},{8,9},{9,8},{10,11... | collective-permute-start | bytes 196616 | tf_op jit(solution)/shard_map/ppermute | solution.py:84
